TPU v7x, 32 devices: a whole 2x2x4 slice. The times are simulated.
32 devices in a mesh: seq: 16 (over z, y, core), head: 2 (over x).
Axes of the slice: x: 2, y: 2, z: 4, core: 2. Of those that a mesh axis runs over, the one named last changes fastest.
Arguments:
- queries: bfloat16 [16384, 2048], P('seq', 'head'), may hold values from -8 to 8
- key_states: bfloat16 [16384, 2048], P('seq', 'head'), may hold values from -8 to 8
- value_states: bfloat16 [16384, 2048], P('seq', 'head'), may hold values from -6 to 6
- out_weight: bfloat16 [2048, 2048], P('head'), may hold values from -0.125 to 0.125
- cotangent: bfloat16 [16384, 2048], P('seq', 'head'), may hold values from -6 to 6
Outputs:
- attended: bfloat16 [16384, 2048], P('seq', 'head')
- grad_queries: bfloat16 [16384, 2048], P('seq', 'head')
- grad_keys: bfloat16 [16384, 2048], P('seq', 'head')
- grad_values: bfloat16 [16384, 2048], P('seq', 'head')
- grad_weight: bfloat16 [2048, 2048], P('head')
All inputs are finite; a program needn't handle non-finite values.
Results may differ from a plain program's by a relative error of at most 0.02.
Values may be sent and summed in bfloat16 or wider, within the bound.
No kernel may reach another device: no remote copies, remote signals or barrier semaphores. Data moves between devices by JAX's collectives and lax.ppermute only.
A program may use at most 256 MiB of HBM per device.

v0:
```python
import jax
import jax.numpy as jnp
from jax import lax
from jax.sharding import PartitionSpec as P

HEAD_DIM = 128
BLOCK = 256
POOLED = 128


def from_partner(block, axis, distance):
    count = lax.axis_size(axis)
    route = []
    for low in range(count):
        high = low | 1 << distance
        if high != low and high < count:
            route += [(low, high), (high, low)]
    return lax.ppermute(block, axis, route)


def pair_mean(rows):
    shape = rows.shape
    wide = rows.reshape(shape[:-2] + (shape[-2] // 2, 2, shape[-1])).astype(jnp.float32)
    return (0.5 * (wide[..., 0, :] + wide[..., 1, :])).astype(jnp.bfloat16)


def widen(rows):
    return jnp.repeat(rows, 2, axis=1) * 0.5


def body(queries, key_states, value_states, out_weight, cotangent):
    rows_here = queries.shape[0]
    features = queries.shape[1]
    heads = features // HEAD_DIM
    blocks = rows_here // BLOCK
    cross = lax.axis_size("seq").bit_length() - 1
    local = (rows_here // POOLED).bit_length() - 1
    position = lax.axis_index("seq")
    logit_scale = HEAD_DIM ** (-0.5)
    stacked = jnp.stack([key_states, value_states])
    coarse = stacked
    pooled_parts = []
    for level in range(1, local):
        coarse = pair_mean(coarse)
        halves = coarse.reshape(2, -1, 2, POOLED, features)[:, :, ::-1].reshape(
            2, -1, POOLED, features
        )
        pooled_parts.append(jnp.repeat(halves, 2 ** (level - 1), axis=1))
    summary = pair_mean(coarse)
    remote = []
    group = summary
    for bit in range(cross):
        partner = from_partner(group, "seq", bit)
        remote.append(partner)
        if bit + 1 < cross:
            upper = position >> bit & 1
            joined = jnp.where(
                upper == 0,
                jnp.concatenate([group, partner], axis=1),
                jnp.concatenate([partner, group], axis=1),
            )
            group = pair_mean(joined)
    far_parts = [
        jnp.broadcast_to(sibling[:, None], (2, blocks, POOLED, features)) for sibling in remote
    ]
    listed = jnp.concatenate(
        [stacked.reshape(2, blocks, BLOCK, features)] + pooled_parts + far_parts, axis=2
    )
    keys_count = listed.shape[2]
    gathered_key_rows = listed[0].reshape(blocks, keys_count, heads, HEAD_DIM)
    gathered_value_rows = listed[1].reshape(blocks, keys_count, heads, HEAD_DIM)
    blocked_queries = queries.reshape(blocks, BLOCK, heads, HEAD_DIM)
    attention_logits = logit_scale * jnp.einsum(
        "bqhe,bkhe->bhqk", blocked_queries, gathered_key_rows, preferred_element_type=jnp.float32
    )
    top = jnp.max(attention_logits, axis=-1, keepdims=True)
    expo = jnp.exp(attention_logits - top)
    probs = expo / jnp.sum(expo, axis=-1, keepdims=True)
    attention_probabilities = probs.astype(jnp.bfloat16)
    blended_output = (
        jnp.einsum(
            "bhqk,bkhe->bqhe",
            attention_probabilities,
            gathered_value_rows,
            preferred_element_type=jnp.float32,
        )
        .astype(jnp.bfloat16)
        .reshape(rows_here, features)
    )
    partial_out = jnp.dot(blended_output, out_weight, preferred_element_type=jnp.float32)
    attended = lax.psum_scatter(
        partial_out.astype(jnp.bfloat16), "head", scatter_dimension=1, tiled=True
    )
    piece = lax.all_gather(cotangent, "head", axis=1, tiled=True)
    grad_mix = lax.dot_general(
        piece, out_weight, (((1,), (1,)), ((), ())), preferred_element_type=jnp.float32
    )
    grad_cols = lax.dot_general(
        blended_output, piece, (((0,), (0,)), ((), ())), preferred_element_type=jnp.float32
    )
    grad_mix, weight_terms = (grad_mix, grad_cols)
    grad_weight = lax.psum(weight_terms, "seq").astype(jnp.bfloat16)
    block_gradient_rows = grad_mix.astype(jnp.bfloat16).reshape(blocks, BLOCK, heads, HEAD_DIM)
    probability_gradient = jnp.einsum(
        "bqhe,bkhe->bhqk",
        block_gradient_rows,
        gathered_value_rows,
        preferred_element_type=jnp.float32,
    )
    inner = jnp.sum(probs * probability_gradient, axis=-1, keepdims=True)
    logit_gradient = (probs * (probability_gradient - inner)).astype(jnp.bfloat16)
    grad_queries = (
        logit_scale
        * jnp.einsum(
            "bhqk,bkhe->bqhe", logit_gradient, gathered_key_rows, preferred_element_type=jnp.float32
        )
    ).astype(jnp.bfloat16)
    grad_queries = grad_queries.reshape(rows_here, features)
    gathered_key_gradient = logit_scale * jnp.einsum(
        "bhqk,bqhe->bkhe", logit_gradient, blocked_queries, preferred_element_type=jnp.float32
    )
    gathered_value_gradient = jnp.einsum(
        "bhqk,bqhe->bkhe",
        attention_probabilities,
        block_gradient_rows,
        preferred_element_type=jnp.float32,
    )
    grad_listed = jnp.stack([gathered_key_gradient, gathered_value_gradient]).reshape(
        2, blocks, keys_count, features
    )
    block_grad = grad_listed[:, :, :BLOCK].reshape(2, rows_here, features)
    offset = BLOCK
    local_grads = []
    for level in range(1, local):
        span = 2 ** (level - 1)
        piece_grad = grad_listed[:, :, offset : offset + POOLED]
        summed = jnp.sum(piece_grad.reshape(2, blocks // span, span, POOLED, features), axis=2)
        local_grads.append(
            summed.reshape(2, -1, 2, POOLED, features)[:, :, ::-1].reshape(2, -1, features)
        )
        offset += POOLED
    far_grads = []
    for bit in range(cross):
        far_grads.append(jnp.sum(grad_listed[:, :, offset : offset + POOLED], axis=1))
        offset += POOLED
    carried = None
    for bit in range(cross - 1, -1, -1):
        outgoing = far_grads[bit]
        kept = None
        if carried is not None:
            upper = position >> bit & 1
            lower_half = carried[:, : POOLED // 2]
            upper_half = carried[:, POOLED // 2 :]
            outgoing = outgoing + widen(jnp.where(upper == 0, upper_half, lower_half))
            kept = widen(jnp.where(upper == 0, lower_half, upper_half))
        incoming = from_partner(outgoing.astype(jnp.bfloat16), "seq", bit).astype(outgoing.dtype)
        carried = incoming if kept is None else incoming + kept
    accum = carried
    for level in range(local - 1, 0, -1):
        accum = widen(accum) + local_grads[level - 1]
    token_grad = block_grad + widen(accum)
    grad_keys = token_grad[0].astype(jnp.bfloat16)
    grad_values = token_grad[1].astype(jnp.bfloat16)
    return (attended, grad_queries, grad_keys, grad_values, grad_weight)


def solution(mesh):
    return jax.shard_map(
        body,
        mesh=mesh,
        in_specs=(
            P("seq", "head"),
            P("seq", "head"),
            P("seq", "head"),
            P("head", None),
            P("seq", "head"),
        ),
        out_specs=(
            P("seq", "head"),
            P("seq", "head"),
            P("seq", "head"),
            P("seq", "head"),
            P("head", None),
        ),
        check_vma=False,
    )
```

profile of v0, /device:TPU:0, one launch (start us, length us, event | category | flops | bytes accessed | tf_op | source)
XLA Modules:
  0.0 668.0 jit_solution(7932061163924948329)
XLA Ops:
  7.2 4.2 stack.28
  13.7 10.8 %maximum_convert_fusion = f32[2,512,2,1024]{3,2,1,0:T(2,128)} fusion(bf16[1,512,2,1024]{3,2,1,0:T(2,128)(2,1)} %stack.28, bf16[1,512,2,1024]{3,2,1,0:T(2,128)(2,1)} %stack.27), kind=kLoop, calls=%fused_computation.42 | loop fusion | flops 4194304 | bytes 12582912 | tf_op jit(solution)/shard_map/convert_element_type | solution.py:23
  24.5 22.4 %convert_reduce_fusion = (f32[2,512,1024]{2,1,0:T(8,128)}, bf16[2,512,1,1024]{3,2,1,0:T(2,128)(2,1)}) fusion(f32[2,512,2,1024]{3,2,1,0:T(2,128)} %maximum_convert_fusion), kind=kLoop, calls=%fused_computation.46 | loop fusion | flops 4194304 | bytes 14680064 | tf_op jit(solution)/shard_map/convert_element_type | solution.py:23
  46.9 6.0 reshape.202
  52.9 7.1 %fusion.55 = (f32[2,256,1,1024]{3,2,1,0:T(1,128)S(1)}, f32[2,256,1,1024]{3,2,1,0:T(1,128)S(1)}) fusion(f32[2,256,2,1024]{3,2,1,0:T(2,128)} %reshape.202), kind=kLoop, calls=%fused_computation.109 | loop fusion | bytes 8388608 | tf_op jit(solution)/shard_map/slice | solution.py:24
  69.9 2.9 collective-permute-start.1
  72.8 3.0 copy.193
  77.5 5.2 maximum_dynamic-update-slice_fusion
  85.3 3.8 broadcast_select_fusion.1
  93.7 3.5 copy.197
  97.2 3.0 copy.164
  105.6 3.7 broadcast_select_fusion
  111.2 2.6 collective-permute-start.3
  118.0 17.9 %collective-permute-done.3 = bf16[2,128,1024]{2,0,1:T(2,128)(2,1)S(1)} collective-permute-done((bf16[2,128,1024]{2,0,1:T(2,128)(2,1)S(1)}, bf16[2,128,1024]{2,0,1:T(2,128)(2,1)S(1)}, u32[]{:S(2)}, u32[]{:S(2)}) %collective-permute-start.3) | collective-permute-done | bytes 524320 | tf_op jit(solution)/shard_map/ppermute | solution.py:18
  137.6 11.7 %fusion.54 = (bf16[1,4,1024,1024]{3,2,1,0:T(8,128)(2,1)}, bf16[1,4,1024,1024]{3,2,1,0:T(8,128)(2,1)}) fusion(bf16[2,4,1024,1024]{3,2,1,0:T(8,128)(2,1)} %broadcast_dynamic-update-slice_fusion), kind=kLoop, calls=%fused_computation.108 | loop fusion | bytes 33554432 | tf_op jit(solution)/shard_map/slice | solution.py:70
  149.3 11.4 %copy.152 = bf16[1,4,1024,1024]{2,3,1,0:T(8,128)(2,1)} copy(bf16[1,4,1024,1024]{3,2,1,0:T(8,128)(2,1)} %get-tuple-element.13) | data formatting | bytes 16777216 | tf_op jit(solution)/shard_map/slice | solution.py:70
  160.7 17.4 %fusion.56 = (f32[4,8,256]{2,1,0:T(8,128)S(1)}, f32[4,8,256,1024]{2,3,1,0:T(8,128)}) fusion(bf16[4,1024,8,128]{1,3,2,0:T(8,128)(2,1)} %bitcast.109, bf16[4,256,8,128]{1,3,2,0:T(8,128)(2,1)S(1)} %copy.164), kind=kOutput, calls=%fused_computation.110 | convolution fusion | flops 2172650496 | bytes 44072960 | tf_op jit(solution)/shard_map/sub | solution.py:77
  178.1 11.4 %copy.151 = bf16[1,4,1024,1024]{2,3,1,0:T(8,128)(2,1)} copy(bf16[1,4,1024,1024]{3,2,1,0:T(8,128)(2,1)} %get-tuple-element.14) | data formatting | bytes 16777216 | tf_op jit(solution)/shard_map/slice | solution.py:71
  189.5 16.1 %convert_bitcast_fusion.1 = bf16[4,256,8,128]{1,3,2,0:T(8,128)(2,1)} fusion(bf16[4,1024,8,128]{1,3,2,0:T(8,128)(2,1)} %bitcast.116, f32[4,8,256,1024]{2,3,1,0:T(8,128)} %get-tuple-element.26, f32[4,8,256]{2,1,0:T(8,128)S(1)} %get-tuple-element.25), kind=kOutput, calls=%fused_computation.63 | convolution fusion | flops 2165309440 | bytes 44072960 | tf_op jit(solution)/shard_map/bhqk,bkhe->bqhe/dot_general | solution.py:81
  205.6 4.3 copy.156
  209.9 8.0 %convert_bitcast_fusion = bf16[128,8,8,128]{3,1,2,0:T(8,128)(2,1)S(1)} fusion(bf16[1024,2048]{1,0:T(8,128)(2,1)} %all-gather.2.cloned.1.call-done, bf16[1024,2048]{1,0:T(8,128)(2,1)} %param.8), kind=kOutput, calls=%fused_computation.62 | convolution fusion | flops 4296015872 | bytes 10485760 | tf_op jit(solution)/shard_map/dot_general | solution.py:95
  219.8 4.3 copy.165
  224.1 25.4 %multiply_reduce_fusion = (f32[4,8,256]{2,1,0:T(8,128)S(1)}, f32[4,8,256,1024]{2,3,1,0:T(8,128)}) fusion(f32[4,8,256,1024]{2,3,1,0:T(8,128)} %get-tuple-element.26, f32[4,8,256]{2,1,0:T(8,128)S(1)} %get-tuple-element.25, bf16[4,256,8,128]{1,3,2,0:T(8,128)(2,1)} %copy.165, bf16[4,1024,8,128]{1,3,2,0:T(8,128)(2,1)} %bitcast.117), kind=kOutput, calls=%fused_computation.18 | convolution fusion | flops 2172641280 | bytes 77660160 | tf_op jit(solution)/shard_map/bqhe,bkhe->bhqk/dot_general | solution.py:104
  249.5 17.6 %fusion.9 = f32[4,8,128,1024]{3,2,1,0:T(8,128)} fusion(bf16[4,256,8,128]{1,3,2,0:T(8,128)(2,1)} %copy.165, f32[4,8,256,1024]{2,3,1,0:T(8,128)} %get-tuple-element.26, f32[4,8,256]{2,1,0:T(8,128)S(1)} %get-tuple-element.25), kind=kOutput, calls=%fused_computation.26 | convolution fusion | flops 2164260864 | bytes 52461568 | tf_op jit(solution)/shard_map/bhqk,bqhe->bkhe/dot_general | solution.py:122
  267.0 27.5 %multiply_convert_fusion = bf16[4,8,256,1024]{2,3,1,0:T(8,128)(2,1)} fusion(f32[4,8,256,1024]{2,3,1,0:T(8,128)} %get-tuple-element.28, f32[4,8,256]{2,1,0:T(8,128)S(1)} %get-tuple-element.27, f32[4,8,256,1024]{2,3,1,0:T(8,128)} %get-tuple-element.26, f32[4,8,256]{2,1,0:T(8,128)S(1)} %get-tuple-element.25), kind=kLoop, calls=%fused_computation.17 | loop fusion | flops 33554432 | bytes 83951616 | tf_op jit(solution)/shard_map/convert_element_type | solution.py:111
  294.6 12.3 %convolution_multiply_fusion = f32[4,8,1024,128]{2,3,1,0:T(8,128)} fusion(bf16[4,8,256,1024]{2,3,1,0:T(8,128)(2,1)} %multiply_convert_fusion, bf16[4,256,8,128]{1,3,2,0:T(8,128)(2,1)S(1)} %copy.164), kind=kOutput, calls=%fused_computation.22 | convolution fusion | flops 2151677952 | bytes 35651584 | tf_op jit(solution)/shard_map/bhqk,bqhe->bkhe/dot_general | solution.py:119
  306.9 14.5 %fusion.15 = (f32[2,128,1024]{1,2,0:T(8,128)S(1)}, f32[2,128,1024]{1,2,0:T(8,128)S(1)}, f32[2,128,1024]{1,2,0:T(8,128)S(1)}, bf16[2,128,1024]{1,2,0:T(8,128)(2,1...) fusion(f32[1,4,1024,1024]{2,3,1,0:T(8,128)} %bitcast.105, f32[1,4,1024,1024]{2,3,1,0:T(8,128)} %bitcast.107), kind=kLoop, calls=%fused_computation.32 | loop fusion | flops 9437184 | bytes 45613056 | tf_op jit(solution)/shard_map/reduce_sum | solution.py:144
  323.5 9.3 %convolution_convert_fusion = bf16[1024,2048]{1,0:T(8,128)(2,1)} fusion(bf16[1024,2048]{1,0:T(8,128)(2,1)} %param.8, bf16[128,8,8,128]{3,2,1,0:T(8,128)(2,1)} %bitcast.135), kind=kOutput, calls=%fused_computation.49 | convolution fusion | flops 4297064448 | bytes 10485760 | tf_op jit(solution)/shard_map/dot_general | solution.py:90
  334.5 14.6 %collective-permute-done.4 = bf16[2,128,1024]{2,1,0:T(8,128)(2,1)} collective-permute-done((bf16[2,128,1024]{2,1,0:T(8,128)(2,1)}, bf16[2,128,1024]{2,1,0:T(8,128)(2,1)}, u32[]{:S(2)}, u32[]{:S(2)}) %collective-permute-start.4) | collective-permute-done | bytes 524320 | tf_op jit(solution)/shard_map/ppermute | solution.py:18
  351.8 6.8 %fusion.27 = f32[1024,2048]{1,0:T(8,128)} fusion(bf16[1024,2048]{1,0:T(8,128)(2,1)S(1)} %copy-done.8, bf16[128,8,8,128]{3,2,1,0:T(8,128)(2,1)S(1)} %bitcast.136), kind=kOutput, calls=%fused_computation.52 | convolution fusion | flops 4294967296 | bytes 14680064 | tf_op jit(solution)/shard_map/dot_general | solution.py:98
  359.0 5.4 collective-permute-done.5
  367.9 184.5 %all-reduce.1 = bf16[1024,2048]{1,0:T(8,128)(2,1)} all-reduce(f32[1024,2048]{1,0:T(8,128)} %fusion.27), channel_id=1, replica_groups=mesh['seq'=16,'head'=2] {'seq'}, use_global_device_ids=true, to_apply=%region_9.10 | all-reduce | flops 2097152 | bytes 12582912 | tf_op jit(solution)/shard_map/psum | solution.py:102
  556.6 2.5 collective-permute-start.7
  559.1 11.9 %fusion.37 = bf16[4,256,8,128]{1,3,2,0:T(8,128)(2,1)} fusion(bf16[4,1024,8,128]{1,3,2,0:T(8,128)(2,1)} %bitcast.110, bf16[4,8,256,1024]{2,3,1,0:T(8,128)(2,1)} %multiply_convert_fusion), kind=kOutput, calls=%fused_computation.69 | convolution fusion | flops 2149580800 | bytes 27262976 | tf_op jit(solution)/shard_map/bhqk,bkhe->bqhe/dot_general | solution.py:114
  571.0 3.1 copy.162
  576.1 2.7 reduce_sum.73
  582.2 5.4 copy.185
  587.7 4.7 rev.12
  592.4 5.9 fusion.7
  598.3 8.8 %copy.167 = f32[2,4,256,1024]{3,2,1,0:T(8,128)} copy(f32[2,4,256,1024]{2,3,1,0:T(8,128)} %fusion.7) | data formatting | bytes 16777216 | tf_op jit(solution)/shard_map/slice | solution.py:131
  616.0 3.9 mul.162
  621.7 3.4 broadcast_in_dim.69
  625.1 6.0 mul.164
  631.2 4.4 fusion.23
  635.6 4.5 broadcast_in_dim.70
  640.1 10.9 %mul.167 = f32[2,1024,1024]{2,1,0:T(8,128)} reshape(f32[2,512,2,1024]{3,2,1,0:T(2,128)} %broadcast_in_dim.70) | data formatting | bytes 16777216 | tf_op jit(solution)/shard_map/mul | solution.py:28
  651.0 7.3 %fusion.8 = bf16[2,1024,1024]{2,1,0:T(8,128)(2,1)S(1)} fusion(f32[2,1024,1024]{2,1,0:T(8,128)} %mul.167, f32[2,4,256,1024]{3,2,1,0:T(8,128)} %copy.167), kind=kLoop, calls=%fused_computation.25 | loop fusion | flops 4194304 | bytes 20971520 | tf_op jit(solution)/shard_map/convert.6
  658.3 2.4 slice_bitcast_fusion
  (92 shorter events, 66.5 us)
Async XLA Ops:
  7.2 4.3 copy-start.1
  7.2 202.7 %all-gather.2.cloned.1.call-start = ((), (), s32[]{:S(2)}) async-start(), calls=%async_computation.2 | async-start | bytes 6291456 | tf_op jit(solution)/shard_map/all_gather | solution.py:94
  62.8 2.1 collective-permute-start
  64.8 7.9 %copy-start.3 = (bf16[2,128,1024]{2,0,1:T(2,128)(2,1)}, bf16[2,128,1024]{2,0,1:T(2,128)(2,1)S(1)}, u32[]{:S(2)}) copy-start(bf16[2,128,1024]{2,0,1:T(2,128)(2,1)S(1)} %collective-permute-done) | copy-start | bytes 1572868
  69.9 15.4 %collective-permute-start.1 = (bf16[2,128,1024]{2,0,1:T(2,128)(2,1)}, bf16[2,128,1024]{2,0,1:T(2,128)(2,1)}, u32[]{:S(2)}, u32[]{:S(2)}) collective-permute-start(bf16[2,128,1024]{2,0,1:T(2,128)(2,1)} %fusion.49), channel_id=1, source_target_pairs={{0,4},{4,0},{2,6},{6,2},{8,12},{12,8},{10,14},{14,10},{16,20},{20,... | collective-permute-start | bytes 1572872 | tf_op jit(solution)/shard_map/ppermute | solution.py:18
  72.8 587.9 %reduce-scatter.2.cloned.1.call-start = ((), (), s32[]{:S(2)}) async-start(), calls=%async_computation.1 | async-start | bytes 6291456 | tf_op jit(solution)/shard_map/reduce_scatter | solution.py:91
  77.5 5.2 copy-start
  91.8 13.8 %collective-permute-start.2 = (bf16[2,128,1024]{2,0,1:T(2,128)(2,1)}, bf16[2,128,1024]{2,0,1:T(2,128)(2,1)}, u32[]{:S(2)}, u32[]{:S(2)}) collective-permute-start(bf16[2,128,1024]{2,0,1:T(2,128)(2,1)} %fusion.50), channel_id=1, source_target_pairs={{0,8},{8,0},{2,10},{10,2},{4,12},{12,4},{6,14},{14,6},{16,24},{24,... | collective-permute-start | bytes 1572872 | tf_op jit(solution)/shard_map/ppermute | solution.py:18
  100.2 1.7 copy-start.4
  111.2 24.8 %collective-permute-start.3 = (bf16[2,128,1024]{2,0,1:T(2,128)(2,1)S(1)}, bf16[2,128,1024]{2,0,1:T(2,128)(2,1)S(1)}, u32[]{:S(2)}, u32[]{:S(2)}) collective-permute-start(bf16[2,128,1024]{2,0,1:T(2,128)(2,1)S(1)} %fusion.51), channel_id=1, source_target_pairs={{0,16},{16,0},{2,18},{18,2},{4,20},{20,4},{6,22},{22,6},{8,24},{24... | collective-permute-start | bytes 1572872 | tf_op jit(solution)/shard_map/ppermute | solution.py:18
  323.5 25.6 %collective-permute-start.4 = (bf16[2,128,1024]{2,1,0:T(8,128)(2,1)}, bf16[2,128,1024]{2,1,0:T(8,128)(2,1)}, u32[]{:S(2)}, u32[]{:S(2)}) collective-permute-start(bf16[2,128,1024]{2,1,0:T(8,128)(2,1)} %copy.168), channel_id=1, source_target_pairs={{0,16},{16,0},{2,18},{18,2},{4,20},{20,4},{6,22},{22,6},{8,24},{24... | collective-permute-start | bytes 1572872 | tf_op jit(solution)/shard_map/ppermute | solution.py:18
  334.5 16.8 %copy-start.2 = (f32[2,128,1024]{2,1,0:T(8,128)S(1)}, f32[2,128,1024]{2,1,0:T(8,128)}, u32[]{:S(2)}) copy-start(f32[2,128,1024]{2,1,0:T(8,128)} %copy.170) | copy-start | bytes 3145732
  334.5 17.3 %copy-start.7 = (bf16[4,256,8,128]{3,2,1,0:T(8,128)(2,1)S(1)}, bf16[4,256,8,128]{3,2,1,0:T(8,128)(2,1)}, u32[]{:S(2)}) copy-start(bf16[4,256,8,128]{3,2,1,0:T(8,128)(2,1)} %copy.156) | copy-start | bytes 6291460
  334.5 17.3 %copy-start.8 = (bf16[1024,2048]{1,0:T(8,128)(2,1)S(1)}, bf16[1024,2048]{1,0:T(8,128)(2,1)}, u32[]{:S(2)}) copy-start(bf16[1024,2048]{1,0:T(8,128)(2,1)} %all-gather.2.cloned.1.call-done) | copy-start | bytes 12582916
  351.7 12.7 %collective-permute-start.5 = (bf16[2,128,1024]{2,1,0:T(8,128)(2,1)S(1)}, bf16[2,128,1024]{2,1,0:T(8,128)(2,1)S(1)}, u32[]{:S(2)}, u32[]{:S(2)}) collective-permute-start(bf16[2,128,1024]{2,1,0:T(8,128)(2,1)S(1)} %fusion.47), channel_id=1, source_target_pairs={{0,8},{8,0},{2,10},{10,2},{4,12},{12,4},{6,14},{14,6},{16,24},{24,... | collective-permute-start | bytes 1572872 | tf_op jit(solution)/shard_map/ppermute | solution.py:18
  367.9 184.5 %copy-start.6 = (f32[2,64,1024]{2,1,0:T(8,128)S(1)}, f32[2,64,1024]{2,1,0:T(8,128)}, u32[]{:S(2)}) copy-start(f32[2,64,1024]{2,1,0:T(8,128)} %get-tuple-element.22) | copy-start | bytes 1572868
  367.9 184.9 %collective-permute-start.6 = (bf16[2,128,1024]{2,1,0:T(8,128)(2,1)}, bf16[2,128,1024]{2,1,0:T(8,128)(2,1)S(1)}, u32[]{:S(2)}, u32[]{:S(2)}) collective-permute-start(bf16[2,128,1024]{2,1,0:T(8,128)(2,1)} %fusion.46), channel_id=1, source_target_pairs={{0,4},{4,0},{2,6},{6,2},{8,12},{12,8},{10,14},{14,10},{16,20},{20,... | collective-permute-start | bytes 1572872 | tf_op jit(solution)/shard_map/ppermute | solution.py:18
  556.6 53.6 %collective-permute-start.7 = (bf16[2,128,1024]{1,2,0:T(8,128)(2,1)}, bf16[2,128,1024]{1,2,0:T(8,128)(2,1)}, u32[]{:S(2)}, u32[]{:S(2)}) collective-permute-start(bf16[2,128,1024]{1,2,0:T(8,128)(2,1)} %add_convert_fusion), channel_id=1, source_target_pairs={{0,2},{2,0},{4,6},{6,4},{8,10},{10,8},{12,14},{14,12},{16,18},{18,... | collective-permute-start | bytes 1572872 | tf_op jit(solution)/shard_map/ppermute | solution.py:18
  598.3 8.8 %copy-start.5 = (f32[2,64,1024]{2,1,0:T(8,128)S(1)}, f32[2,64,1024]{2,1,0:T(8,128)}, u32[]{:S(2)}) copy-start(f32[2,64,1024]{2,1,0:T(8,128)} %get-tuple-element.20) | copy-start | bytes 1572868
Sparse Core Ops, SparseCore 0:
  72.9 57.0 all-gather.1
  332.9 55.5 reduce-scatter.1
where the time goes:
time: 678 us; the launch traced here: 668 us
  blocking collectives  184 us (27%)
  local copies, waits for them, and re-layouts  162 us (24%)
  other arithmetic  130 us (19%)
  matrix products  125 us (18%)
  waiting for transfers between devices  41.5 us (6%)
  between operations  14.9 us (2%)
  starting transfers between devices  10.4 us (2%)
    psum x1, blocking collectives, body(): grad_weight = lax.psum(weight_terms, 'seq').astype(jnp.bfloat16)  184 us
    ppermute x8, waiting for transfers between devices, from_partner(): return lax.ppermute(block, axis, route)  41.5 us
    convert_element_type x5, other arithmetic, pair_mean(): rows.reshape(shape[:-2] + (shape[-2] // 2, 2, shape[-1]))  36.9 us
    convert_element_type x1, other arithmetic, body(): (probs * (probability_gradient - inner)).astype(jnp.bfloat16)  27.5 us
    mul x12, local copies, waits for them, and re-layouts, widen(): return jnp.repeat(rows, 2, axis=1) * 0.5  26.7 us
    dot_general x1, matrix products, body(): jnp.einsum('bqhe,bkhe->bhqk', block_gradient_rows, gathered_value_rows, p...  25.4 us
    slice x2, local copies, waits for them, and re-layouts, body(): gathered_key_rows = listed[0].reshape(blocks, keys_count, heads, HEAD_DIM)  23.1 us
    unnamed x27, local copies, waits for them, and re-layouts  18.1 us
  transfers between devices with their start and end apart: 10, of which 6 were waited for; matrix products, arithmetic and copies ran while one was open for 36% of the time, Pallas kernels for 0%

commit v1 on v0

v1 whole, which is shorter than its diff:
```python
import functools

import jax
import jax.numpy as jnp
from jax import lax
from jax.experimental import pallas as pl
from jax.experimental.pallas import tpu as pltpu
from jax.sharding import PartitionSpec as P

HEAD_DIM = 128
BLOCK = 256
POOLED = 128
SCALE = HEAD_DIM ** -0.5
SCALE2 = SCALE * 1.4426950408889634
VMEM = 48 * 1024 * 1024
F32 = jnp.float32
BF16 = jnp.bfloat16


def params():
    return pltpu.CompilerParams(vmem_limit_bytes=VMEM)


def nn(a, b):
    return lax.dot_general(a, b, (((1,), (0,)), ((), ())), preferred_element_type=F32)


def nt(a, b):
    return lax.dot_general(a, b, (((1,), (1,)), ((), ())), preferred_element_type=F32)


def tn(a, b):
    return lax.dot_general(a, b, (((0,), (0,)), ((), ())), preferred_element_type=F32)


def pool_matrix(rows, columns):
    row = lax.broadcasted_iota(jnp.int32, (rows, columns), 0)
    column = lax.broadcasted_iota(jnp.int32, (rows, columns), 1)
    return jnp.where((column >> 1) == row, 0.5, 0.0).astype(BF16)


def widen_matrix(rows, columns, shift):
    row = lax.broadcasted_iota(jnp.int32, (rows, columns), 0)
    column = lax.broadcasted_iota(jnp.int32, (rows, columns), 1)
    return jnp.where((row >> shift) == column, 0.5 ** shift, 0.0).astype(BF16)


def from_partner(block, bit):
    count = lax.axis_size("seq")
    return lax.ppermute(block, "seq", [(low, low ^ 1 << bit) for low in range(count)])


def pool_kernel(local, cross, key_ref, value_ref, coarse_ref, summary_ref, pack_ref):
    big = pool_matrix(POOLED, BLOCK)
    small = pool_matrix(POOLED, POOLED)
    for index, ref in enumerate((key_ref, value_ref)):
        rows = ref[...]
        offset = 0
        for level in range(1, local + 1):
            parts = [
                nn(big, rows[start : start + BLOCK]) for start in range(0, rows.shape[0], BLOCK)
            ]
            rows = jnp.concatenate(parts, axis=0).astype(BF16)
            if level < local:
                coarse_ref[index, offset : offset + rows.shape[0], :] = rows
                offset += rows.shape[0]
        summary_ref[index] = rows
        pieces = []
        left = POOLED
        for bit in range(1, cross):
            wide = nn(small, rows)
            rows = wide.astype(BF16)
            pieces.append(wide[: POOLED >> bit])
            left -= POOLED >> bit
        pieces.append(jnp.zeros((left, rows.shape[1]), F32))
        pack_ref[index] = jnp.concatenate(pieces, axis=0).astype(BF16)


def pool(key_states, value_states, local, cross):
    rows, features = key_states.shape
    width = min(features, 256)
    total = sum(rows >> level for level in range(1, local))

    def spec(count):
        return pl.BlockSpec((2, count, width), lambda j: (0, 0, j))

    return pl.pallas_call(
        functools.partial(pool_kernel, local, cross),
        grid=(features // width,),
        in_specs=[pl.BlockSpec((rows, width), lambda j: (0, j))] * 2,
        out_specs=[spec(total), spec(POOLED), spec(POOLED)],
        out_shape=[
            jax.ShapeDtypeStruct((2, count, features), BF16) for count in (total, POOLED, POOLED)
        ],
        compiler_params=params(),
        name="pool",
    )(key_states, value_states)


def local_list(own, coarse, block, local, rows):
    parts = [own[block * BLOCK : (block + 1) * BLOCK]]
    offset = 0
    for level in range(1, local):
        sibling = block >> (level - 1) ^ 1
        start = offset + sibling * POOLED
        parts.append(coarse[start : start + POOLED])
        offset += rows >> level
    return jnp.concatenate(parts, axis=0)


def near_kernel(local, query_ref, key_ref, value_ref, coarse_ref, out_ref, stat_ref):
    rows = query_ref.shape[0]
    lane = lax.broadcasted_iota(jnp.int32, (BLOCK, HEAD_DIM), 1)
    for block in range(rows // BLOCK):
        here = slice(block * BLOCK, (block + 1) * BLOCK)
        keys = local_list(key_ref, coarse_ref.at[0], block, local, rows)
        values = local_list(value_ref, coarse_ref.at[1], block, local, rows)
        scores = nt(query_ref[here, :], keys)
        top = jnp.max(scores, axis=1, keepdims=True)
        weights = jnp.exp2((scores - top) * SCALE2)
        total = jnp.sum(weights, axis=1, keepdims=True)
        out_ref[here, :] = nn(weights.astype(BF16), values)
        stat_ref[here, :] = jnp.where(lane < 64, top, total)


def far_kernel(query_ref, first_ref, kept_ref, swapped_ref, near_ref, stat_ref, mixed_ref, lse_ref):
    rows = query_ref.shape[0]
    keys = jnp.concatenate([first_ref[0], kept_ref[0], swapped_ref[0]], axis=0)
    values = jnp.concatenate([first_ref[1], kept_ref[1], swapped_ref[1]], axis=0)
    for block in range(rows // BLOCK):
        here = slice(block * BLOCK, (block + 1) * BLOCK)
        scores = nt(query_ref[here, :], keys)
        near_top = stat_ref[here, 0:1]
        near_total = stat_ref[here, 64:65]
        top = jnp.maximum(near_top, jnp.max(scores, axis=1, keepdims=True))
        weights = jnp.exp2((scores - top) * SCALE2)
        shrink = jnp.exp2((near_top - top) * SCALE2)
        total = near_total * shrink + jnp.sum(weights, axis=1, keepdims=True)
        blend = near_ref[here, :] * shrink + nn(weights.astype(BF16), values)
        mixed_ref[here, :] = (blend / total).astype(BF16)
        lse = top * SCALE2 + jnp.log2(total)
        lse_ref[0, :, here] = jnp.broadcast_to(lse, (BLOCK, HEAD_DIM)).T[:8]


def column(rows):
    return pl.BlockSpec((rows, HEAD_DIM), lambda h: (0, h))


def pair(rows):
    return pl.BlockSpec((2, rows, HEAD_DIM), lambda h: (0, 0, h))


def row_stat(rows):
    return pl.BlockSpec((1, 8, rows), lambda h: (h, 0, 0))


def near_forward(queries, key_states, value_states, coarse, local):
    rows, features = queries.shape
    return pl.pallas_call(
        functools.partial(near_kernel, local),
        grid=(features // HEAD_DIM,),
        in_specs=[column(rows)] * 3 + [pair(coarse.shape[1])],
        out_specs=[column(rows)] * 2,
        out_shape=[jax.ShapeDtypeStruct((rows, features), F32)] * 2,
        compiler_params=params(),
        name="near_forward",
    )(queries, key_states, value_states, coarse)


def far_forward(queries, far, near, stat):
    rows, features = queries.shape
    heads = features // HEAD_DIM
    return pl.pallas_call(
        far_kernel,
        grid=(heads,),
        in_specs=[column(rows)] + [pair(part.shape[1]) for part in far] + [column(rows)] * 2,
        out_specs=[column(rows), row_stat(rows)],
        out_shape=[
            jax.ShapeDtypeStruct((rows, features), BF16),
            jax.ShapeDtypeStruct((heads, 8, rows), F32),
        ],
        compiler_params=params(),
        name="far_forward",
    )(queries, *far, near, stat)


def attend_back(queries, grad_mixed, keys, values, lse, inner):
    weights = jnp.exp2(nt(keys, queries) * SCALE2 - lse)
    grad_probs = nt(values, grad_mixed)
    grad_scores = (weights * (grad_probs - inner)).astype(BF16)
    grad_values = nn(weights.astype(BF16), grad_mixed)
    grad_keys = nn(grad_scores, queries)
    grad_queries = tn(grad_scores, keys)
    return grad_queries, grad_keys, grad_values


def far_back_kernel(
    query_ref, first_ref, kept_ref, swapped_ref, mixed_ref, grad_ref, lse_ref,
    grad_first_ref, grad_kept_ref, grad_swapped_ref, grad_query_ref, inner_ref,
):
    rows = query_ref.shape[0]
    keys = jnp.concatenate([first_ref[0], kept_ref[0], swapped_ref[0]], axis=0)
    values = jnp.concatenate([first_ref[1], kept_ref[1], swapped_ref[1]], axis=0)
    total_keys = None
    total_values = None
    for block in range(rows // BLOCK):
        here = slice(block * BLOCK, (block + 1) * BLOCK)
        grad = grad_ref[here, :]
        product = (grad.astype(F32) * mixed_ref[here, :].astype(F32)).T
        inner = jnp.sum(product, axis=0, keepdims=True)
        inner_ref[0, :, here] = jnp.broadcast_to(inner, (8, BLOCK))
        grad_queries, grad_keys, grad_values = attend_back(
            query_ref[here, :], grad, keys, values, lse_ref[0, 0:1, here], inner
        )
        grad_query_ref[here, :] = grad_queries
        total_keys = grad_keys if total_keys is None else total_keys + grad_keys
        total_values = grad_values if total_values is None else total_values + grad_values
    total_keys = (total_keys * SCALE).astype(BF16)
    total_values = total_values.astype(BF16)
    start = 0
    for ref in (grad_first_ref, grad_kept_ref, grad_swapped_ref):
        count = ref.shape[1]
        ref[0] = total_keys[start : start + count]
        ref[1] = total_values[start : start + count]
        start += count


def far_backward(queries, far, mixed, grad_mixed, lse):
    rows, features = queries.shape
    heads = features // HEAD_DIM
    return pl.pallas_call(
        far_back_kernel,
        grid=(heads,),
        in_specs=[column(rows)]
        + [pair(part.shape[1]) for part in far]
        + [column(rows)] * 2
        + [row_stat(rows)],
        out_specs=[pair(part.shape[1]) for part in far] + [column(rows), row_stat(rows)],
        out_shape=[jax.ShapeDtypeStruct(part.shape, BF16) for part in far]
        + [
            jax.ShapeDtypeStruct((rows, features), F32),
            jax.ShapeDtypeStruct((heads, 8, rows), F32),
        ],
        compiler_params=params(),
        name="far_backward",
    )(queries, *far, mixed, grad_mixed, lse)


def near_back_kernel(
    local, query_ref, key_ref, value_ref, coarse_ref, grad_ref, lse_ref, inner_ref, far_query_ref,
    grad_query_ref, grad_key_ref, grad_value_ref,
):
    rows = query_ref.shape[0]
    blocks = rows // BLOCK
    own = [[None] * blocks, [None] * blocks]
    pooled = [[None] * (2 * blocks) for _ in range(2 * local)]
    for block in range(blocks):
        here = slice(block * BLOCK, (block + 1) * BLOCK)
        keys = local_list(key_ref, coarse_ref.at[0], block, local, rows)
        values = local_list(value_ref, coarse_ref.at[1], block, local, rows)
        grad_queries, grad_keys, grad_values = attend_back(
            query_ref[here, :], grad_ref[here, :], keys, values,
            lse_ref[0, 0:1, here], inner_ref[0, 0:1, here],
        )
        grad_query_ref[here, :] = ((grad_queries + far_query_ref[here, :]) * SCALE).astype(BF16)
        for index, value in enumerate((grad_keys * SCALE, grad_values)):
            own[index][block] = value[:BLOCK]
            for level in range(1, local):
                sibling = block >> (level - 1) ^ 1
                start = BLOCK + (level - 1) * POOLED
                piece = value[start : start + POOLED]
                held = pooled[2 * level + index][sibling]
                pooled[2 * level + index][sibling] = piece if held is None else held + piece
    matrix = widen_matrix(BLOCK, POOLED, 1)
    for index, ref in enumerate((grad_key_ref, grad_value_ref)):
        for level in range(local - 1, 0, -1):
            for half in range(blocks >> (level - 1)):
                wide = nn(matrix, pooled[2 * level + index][half].astype(BF16))
                if level == 1:
                    own[index][half] = own[index][half] + wide
                else:
                    below = pooled[2 * (level - 1) + index]
                    below[2 * half] = below[2 * half] + wide[:POOLED]
                    below[2 * half + 1] = below[2 * half + 1] + wide[POOLED:]
        for block in range(blocks):
            ref[block * BLOCK : (block + 1) * BLOCK, :] = own[index][block].astype(BF16)


def near_backward(queries, key_states, value_states, coarse, grad_mixed, lse, inner, far_query, local):
    rows, features = queries.shape
    return pl.pallas_call(
        functools.partial(near_back_kernel, local),
        grid=(features // HEAD_DIM,),
        in_specs=[column(rows)] * 3
        + [pair(coarse.shape[1]), column(rows), row_stat(rows), row_stat(rows), column(rows)],
        out_specs=[column(rows)] * 3,
        out_shape=[jax.ShapeDtypeStruct((rows, features), BF16)] * 3,
        compiler_params=params(),
        name="near_backward",
    )(queries, key_states, value_states, coarse, grad_mixed, lse, inner, far_query)


def finish_kernel(local, key_ref, value_ref, *refs):
    parts, (grad_key_ref, grad_value_ref) = refs[:-2], refs[-2:]
    rows = key_ref.shape[0]
    spread = widen_matrix(rows, POOLED, local)
    for index, (near, out) in enumerate(((key_ref, grad_key_ref), (value_ref, grad_value_ref))):
        held = None
        for part in parts[::-1]:
            value = part[index].astype(F32)
            if held is not None:
                value = value + nn(widen_matrix(value.shape[0], held.shape[0], 1), held.astype(BF16))
            held = value
        out[...] = (near[...].astype(F32) + nn(spread, held.astype(BF16))).astype(BF16)


def finish(grad_key, grad_value, parts, local):
    rows, features = grad_key.shape
    width = min(features, 256)
    near = pl.BlockSpec((rows, width), lambda j: (0, j))
    return pl.pallas_call(
        functools.partial(finish_kernel, local),
        grid=(features // width,),
        in_specs=[near] * 2
        + [pl.BlockSpec((2, part.shape[1], width), lambda j: (0, 0, j)) for part in parts],
        out_specs=[near] * 2,
        out_shape=[jax.ShapeDtypeStruct((rows, features), BF16)] * 2,
        compiler_params=params(),
        name="finish",
    )(grad_key, grad_value, *parts)


def gather_far(summary, pack, cross):
    first = from_partner(summary, 0)
    chunks = []
    start = 0
    for bit in range(1, cross):
        count = POOLED >> bit
        chunks.append(from_partner(pack[:, start : start + count], bit))
        start += count
    for bit in range(1, cross - 1):
        sizes = [chunk.shape[1] for chunk in chunks[bit:]]
        sent = jnp.concatenate(chunks[bit:], axis=1)
        arrived = from_partner(sent, bit)
        start = 0
        for index, size in enumerate(sizes):
            chunks[bit + index] = jnp.concatenate(
                [chunks[bit + index], arrived[:, start : start + size]], axis=1
            )
            start += size
    kept = jnp.concatenate(chunks, axis=1)
    return first, kept, from_partner(kept, 0)


def added(first, second):
    return (first.astype(F32) + second.astype(F32)).astype(BF16)


def scatter_far(grad_first, grad_kept, grad_swapped, cross):
    parts = [from_partner(grad_first, 0)]
    kept = added(grad_kept, from_partner(grad_swapped, 0))
    half = POOLED // 2
    chunks = [kept[:, index * half : (index + 1) * half] for index in range(cross - 1)]
    for bit in range(cross - 2, 0, -1):
        sizes = [chunk.shape[1] // 2 for chunk in chunks[bit:]]
        sent = jnp.concatenate([chunk[:, chunk.shape[1] // 2 :] for chunk in chunks[bit:]], axis=1)
        arrived = from_partner(sent, bit)
        start = 0
        for index, size in enumerate(sizes):
            chunks[bit + index] = added(
                chunks[bit + index][:, :size], arrived[:, start : start + size]
            )
            start += size
    for bit in range(1, cross):
        parts.append(from_partner(chunks[bit - 1], bit))
    return parts


def solution_body(queries, key_states, value_states, out_weight, cotangent):
    rows, features = queries.shape
    cross = lax.axis_size("seq").bit_length() - 1
    local = (rows // POOLED).bit_length() - 1
    groups = lax.axis_size("head")
    piece = lax.all_gather(cotangent, "head", axis=1, tiled=True)
    coarse, summary, pack = pool(key_states, value_states, local, cross)
    far = gather_far(summary, pack, cross)
    near, stat = near_forward(queries, key_states, value_states, coarse, local)
    mixed, lse = far_forward(queries, far, near, stat)
    partial_out = jnp.dot(mixed, out_weight, preferred_element_type=F32).astype(BF16)
    attended = lax.psum_scatter(partial_out, "head", scatter_dimension=1, tiled=True)
    grad_mixed = nt(piece, out_weight).astype(BF16)
    grad_weight = lax.psum(tn(mixed, piece).astype(BF16), "seq")
    *grad_far, far_query, inner = far_backward(queries, far, mixed, grad_mixed, lse)
    parts = scatter_far(*grad_far, cross)
    grad_queries, grad_key, grad_value = near_backward(
        queries, key_states, value_states, coarse, grad_mixed, lse, inner, far_query, local
    )
    grad_keys, grad_values = finish(grad_key, grad_value, parts, local)
    return attended, grad_queries, grad_keys, grad_values, grad_weight


def solution(mesh):
    split = P("seq", "head")
    return jax.shard_map(
        solution_body,
        mesh=mesh,
        in_specs=(split, split, split, P("head", None), split),
        out_specs=(split, split, split, split, P("head", None)),
        check_vma=False,
    )
```

time: 678 us -> 269 us (0.40); the launches traced: 668 us -> 269 us
  blocking collectives: 184 us -> 0 us
  local copies, waits for them, and re-layouts: 162 us -> 9.84 us
  other arithmetic: 130 us -> 0.44 us
  matrix products: 125 us -> 26.8 us
  Pallas kernels: 0 us -> 89.6 us
  waiting for transfers between devices: 41.5 us -> 110 us
  starting transfers between devices: 10.4 us -> 18.4 us
    psum x1 -> x0, blocking collectives: 184 us -> none  [body(): grad_weight = lax.psum(weight_terms, 'seq').astype(jnp.bfloat16)]
    pallas_call x0 -> x6, Pallas kernels: none -> 89.6 us  [the longest x1 23.9 us: far_forward(): pl.pallas_call(far_kernel, grid=(heads,), in_specs=[column(rows)] + [pair...]
    dot_general x8 -> x3, matrix products: 107 us -> 26.8 us  [the longest x1 9.52 us: nt(): lax.dot_general(a, b, (((1,), (1,)), ((), ())), preferred_element_type=F32)]
    convert_element_type x15 -> x4, other arithmetic: 73.5 us -> 0.4 us  [added(): return (first.astype(F32) + second.astype(F32)).astype(BF16)]
    reduce_scatter x1, waiting for transfers between devices: 0.01 us -> 56.2 us  [solution_body(): lax.psum_scatter(partial_out, 'head', scatter_dimension=1, tiled=True)]
    slice x6 -> x7, local copies, waits for them, and re-layouts: 55.7 us -> 0.09 us  [the longest x3 0.03 us: gather_far(): chunks.append(from_partner(pack[:, start:start + count], bit))]
    psum x0 -> x1, waiting for transfers between devices: none -> 28.2 us  [solution_body(): grad_weight = lax.psum(tn(mixed, piece).astype(BF16), 'seq')]
    mul x12 -> x0, local copies, waits for them, and re-layouts: 26.7 us -> none  [widen(): return jnp.repeat(rows, 2, axis=1) * 0.5]
  transfers between devices with their start and end apart: 10 -> 17, of which waited for: 6 -> 8; matrix products, arithmetic and copies ran while one was open for 36% -> 7% of each run, Pallas kernels for 0% -> 33%
where the time goes in v1:
time: 269 us
  waiting for transfers between devices  110 us (41%)
  Pallas kernels  89.6 us (33%)
  matrix products  26.8 us (10%)
  starting transfers between devices  18.4 us (7%)
  between operations  14 us (5%)
  local copies, waits for them, and re-layouts  9.84 us (4%)
    reduce_scatter x1, waiting for transfers between devices, solution_body(): lax.psum_scatter(partial_out, 'head', scatter_dimension=1, tiled=True)  56.2 us
    psum x1, waiting for transfers between devices, solution_body(): grad_weight = lax.psum(tn(mixed, piece).astype(BF16), 'seq')  28.2 us
    ppermute x14, waiting for transfers between devices, from_partner(): lax.ppermute(block, 'seq', [(low, low ^ 1 << bit) for low in range(count)])  24.9 us
    pallas_call x1, Pallas kernels, far_forward(): pl.pallas_call(far_kernel, grid=(heads,), in_specs=[column(rows)] + [pair...  23.9 us
    pallas_call x1, Pallas kernels, near_backward(): pl.pallas_call(functools.partial(near_back_kernel, local), grid=(features...  19.9 us
    ppermute x14, starting transfers between devices, from_partner(): lax.ppermute(block, 'seq', [(low, low ^ 1 << bit) for low in range(count)])  18.2 us
    pallas_call x1, Pallas kernels, far_backward(): pl.pallas_call(far_back_kernel, grid=(heads,), in_specs=[column(rows)] +...  17.6 us
    pallas_call x1, Pallas kernels, near_forward(): pl.pallas_call(functools.partial(near_kernel, local), grid=(features // H...  14.1 us
  transfers between devices with their start and end apart: 17, of which 8 were waited for; matrix products, arithmetic and copies ran while one was open for 7% of the time, Pallas kernels for 33%

profile of v1, /device:TPU:0, one launch (start us, length us, event | category | flops | bytes accessed | tf_op | source)
XLA Modules:
  0.0 269.2 jit_solution(7940863796164413503)
XLA Ops:
  7.2 0.0 all-gather.2.cloned.1.call-start
  7.2 0.7 all-gather.2.cloned.1.call-update
  7.9 0.0 copy-start
  7.9 0.0 all-reduce.2.cloned.1.call-start
  8.0 0.0 copy-start.1
  8.0 1.7 copy-done.1
  9.7 1.6 copy-done.2
  11.3 8.3 %pool.1 = (bf16[2,768,1024]{2,1,0:T(8,128)(2,1)}, bf16[2,128,1024]{2,1,0:T(8,128)(2,1)S(1)}, bf16[2,128,1024]{2,1,0:T(8,128)(2,1)S(1)}) custom-call(bf16[1024,1024]{1,0:T(8,128)(2,1)S(1)} %copy-done.1, bf16[1024,1024]{1,0:T(8,128)(2,1)S(1)} %copy-done.2), custom_call_target="tpu_custom_call" | custom-call | tf_op jit(solution)/shard_map/pool/pallas_call | solution.py:87
  19.6 3.0 %collective-permute-start.1 = (bf16[2,64,1024]{2,1,0:T(8,128)(2,1)S(1)}, bf16[2,64,1024]{2,1,0:T(8,128)(2,1)S(1)}, u32[]{:S(2)}, u32[]{:S(2)}) collective-permute-start(bf16[2,64,1024]{2,1,0:T(8,128)(2,1)S(1)} %slice.48), channel_id=1, source_target_pairs={{0,4},{2,6},{4,0},{6,2},{8,12},{10,14},{12,8},{14,10},{16,20},{18,... | collective-permute-start | bytes 786440 | tf_op jit(solution)/shard_map/ppermute | solution.py:50
  22.6 1.6 collective-permute-start.2
  24.3 2.6 collective-permute-start.3
  26.8 3.0 %collective-permute-done.3 = bf16[2,16,1024]{2,1,0:T(8,128)(2,1)S(1)} collective-permute-done((bf16[2,16,1024]{2,1,0:T(8,128)(2,1)S(1)}, bf16[2,16,1024]{2,1,0:T(8,128)(2,1)S(1)}, u32[]{:S(2)}, u32[]{:S(2)}) %collective-permute-start.3) | collective-permute-done | bytes 65568 | tf_op jit(solution)/shard_map/ppermute | solution.py:50
  29.9 0.0 collective-permute-done.2
  29.9 0.6 collective-permute-start.4
  30.5 5.1 %collective-permute-done.4 = bf16[2,48,1024]{2,1,0:T(8,128)(2,1)S(1)} collective-permute-done((bf16[2,48,1024]{2,1,0:T(8,128)(2,1)S(1)}, bf16[2,48,1024]{2,1,0:T(8,128)(2,1)S(1)}, u32[]{:S(2)}, u32[]{:S(2)}) %collective-permute-start.4) | collective-permute-done | bytes 196640 | tf_op jit(solution)/shard_map/ppermute | solution.py:50
  35.7 1.8 collective-permute-start.5
  37.5 3.2 %collective-permute-done.5 = bf16[2,32,1024]{2,1,0:T(8,128)(2,1)S(1)} collective-permute-done((bf16[2,32,1024]{2,1,0:T(8,128)(2,1)S(1)}, bf16[2,32,1024]{2,1,0:T(8,128)(2,1)S(1)}, u32[]{:S(2)}, u32[]{:S(2)}) %collective-permute-start.5) | collective-permute-done | bytes 131104 | tf_op jit(solution)/shard_map/ppermute | solution.py:50
  40.7 0.1 collective-permute-start.6
  40.8 0.5 collective-permute-start
  41.3 14.1 %near_forward.1 = (f32[1024,1024]{1,0:T(8,128)}, f32[1024,1024]{1,0:T(8,128)}) custom-call(bf16[1024,1024]{1,0:T(8,128)(2,1)S(1)} %copy-done, bf16[1024,1024]{1,0:T(8,128)(2,1)S(1)} %copy-done.1, bf16[1024,1024]{1,0:T(8,128)(2,1)} %value_ref.5, bf16[2,768,1024]{2,1,0:T(8,128)(2,1)} %get-tuple-element.24.coarse_ref), custom_call_target="tpu_custom_call" | custom-call | tf_op jit(solution)/shard_map/near_forward/pallas_call | solution.py:159
  55.4 23.9 %far_forward.1 = (bf16[1024,1024]{1,0:T(8,128)(2,1)S(1)}, f32[8,8,1024]{2,1,0:T(8,128)S(1)}) custom-call(bf16[1024,1024]{1,0:T(8,128)(2,1)} %query_ref.7, bf16[2,128,1024]{2,1,0:T(8,128)(2,1)S(1)} %collective-permute-done.first_ref, bf16[2,192,1024]{2,1,0:T(8,128)(2,1)S(1)} %constant_dynamic-update-slice_fusion.kept_ref, ...), custom_call_target="tpu_custom_call" | custom-call | tf_op jit(solution)/shard_map/far_forward/pallas_call | solution.py:173
  79.3 0.0 copy-start.3
  79.3 0.9 copy-done.3
  80.1 0.7 copy-done.6
  80.8 9.1 %convolution_convert_fusion = bf16[1024,2048]{1,0:T(8,128)(2,1)} fusion(bf16[1024,1024]{1,0:T(8,128)(2,1)S(1)} %get-tuple-element.27.mixed_ref, bf16[1024,2048]{1,0:T(8,128)(2,1)} %all-gather.2.cloned.1.call-done), kind=kOutput, calls=%fused_computation | convolution fusion | flops 4297064448 | bytes 10485760 | tf_op jit(solution)/shard_map/dot_general | solution.py:33
  89.9 0.0 all-reduce.2.cloned.1.call-update
  90.0 0.2 reduce-scatter.2.cloned.1.call-start
  90.2 8.2 %convolution_convert_fusion.1 = bf16[1024,2048]{1,0:T(8,128)(2,1)} fusion(bf16[1024,1024]{1,0:T(8,128)(2,1)S(1)} %get-tuple-element.27.mixed_ref, bf16[1024,2048]{1,0:T(8,128)(2,1)} %param.8), kind=kOutput, calls=%fused_computation.1 | convolution fusion | flops 4297064448 | bytes 10485760 | tf_op jit(solution)/shard_map/dot_general | solution.py:389
  98.4 0.0 reduce-scatter.2.cloned.1.call-update
  98.4 0.0 copy-start.4
  98.5 9.5 %convolution_convert_fusion.2.grad_ref = bf16[1024,1024]{1,0:T(8,128)(2,1)} fusion(bf16[1024,2048]{1,0:T(8,128)(2,1)} %all-gather.2.cloned.1.call-done, bf16[1024,2048]{1,0:T(8,128)(2,1)} %param.8), kind=kOutput, calls=%fused_computation.2 | convolution fusion | flops 4296015872 | bytes 10485760 | tf_op jit(solution)/shard_map/dot_general | solution.py:29
  108.0 17.6 %far_backward.1 = (bf16[2,128,1024]{2,1,0:T(8,128)(2,1)S(1)}, bf16[2,192,1024]{2,1,0:T(8,128)(2,1)S(1)}, bf16[2,192,1024]{2,1,0:T(8,128)(2,1)S(1)}, f32[1024,1024]{1,0:T(8,128)}, f32[8,8,1024]{2,1,0:T(8,128)S(1)}) custom-call(bf16[1024,1024]{1,0:T(8,128)(2,1)} %query_ref.7, bf16[2,128,1024]{2,1,0:T(8,128)(2,1)S(1)} %collective-permute-done.first_ref, ...), custom_call_target="tpu_custom_call" | custom-call | tf_op jit(solution)/shard_map/far_backward/pallas_call | solution.py:231
  125.6 0.1 collective-permute-start.8
  125.7 2.2 collective-permute-done.8
  127.9 0.3 add_convert_fusion
  128.2 1.9 collective-permute-start.10
  130.1 5.7 %collective-permute-done.10 = bf16[2,32,1024]{2,1,0:T(8,128)(2,1)S(1)} collective-permute-done((bf16[2,32,1024]{2,1,0:T(8,128)(2,1)S(1)}, bf16[2,32,1024]{2,1,0:T(8,128)(2,1)S(1)}, u32[]{:S(2)}, u32[]{:S(2)}) %collective-permute-start.10) | collective-permute-done | bytes 131104 | tf_op jit(solution)/shard_map/ppermute | solution.py:50
  135.9 0.1 collective-permute-start.11
  135.9 0.1 collective-permute-start.7
  136.1 2.0 collective-permute-start.9
  138.0 5.7 %collective-permute-done.11 = bf16[2,48,1024]{2,1,0:T(8,128)(2,1)S(1)} collective-permute-done((bf16[2,48,1024]{2,1,0:T(8,128)(2,1)S(1)}, bf16[2,48,1024]{2,1,0:T(8,128)(2,1)S(1)}, u32[]{:S(2)}, u32[]{:S(2)}) %collective-permute-start.11) | collective-permute-done | bytes 196640 | tf_op jit(solution)/shard_map/ppermute | solution.py:50
  143.7 1.8 collective-permute-start.12
  145.6 2.0 collective-permute-start.13
  147.6 19.9 %near_backward.1 = (bf16[1024,1024]{1,0:T(8,128)(2,1)}, bf16[1024,1024]{1,0:T(8,128)(2,1)S(1)}, bf16[1024,1024]{1,0:T(8,128)(2,1)S(1)}) custom-call(bf16[1024,1024]{1,0:T(8,128)(2,1)} %query_ref.7, bf16[1024,1024]{1,0:T(8,128)(2,1)} %key_ref.5, bf16[1024,1024]{1,0:T(8,128)(2,1)} %value_ref.5, bf16[2,768,1024]{2,1,0:T(8,128)(2,1)} %get-tuple-element.24.coarse_ref, ...), custom_call_target="tpu_custom_call" | custom-call | tf_op jit(solution)/shard_map/near_backward/pallas_call | solution.py:291
  167.5 5.9 %finish.1 = (bf16[1024,1024]{1,0:T(8,128)(2,1)}, bf16[1024,1024]{1,0:T(8,128)(2,1)}) custom-call(bf16[1024,1024]{1,0:T(8,128)(2,1)S(1)} %get-tuple-element.32.key_ref, bf16[1024,1024]{1,0:T(8,128)(2,1)S(1)} %get-tuple-element.33.value_ref, bf16[2,128,1024]{2,1,0:T(8,128)(2,1)S(1)} %collective-permute-done.7.refs_0_, ...), custom_call_target="tpu_custom_call" | custom-call | tf_op jit(solution)/shard_map/finish/pallas_call | solution.py:321
  173.4 28.2 %all-reduce.2.cloned.1.call-done = bf16[1024,2048]{1,0:T(8,128)(2,1)} async-done(((bf16[1024,2048]{1,0:T(8,128)(2,1)}), bf16[1024,2048]{1,0:T(8,128)(2,1)}) %all-reduce.2.cloned.1.call-update) | async-done | bytes 4194320 | tf_op jit(solution)/shard_map/psum | solution.py:392
  201.6 56.2 %reduce-scatter.2.cloned.1.call-done = bf16[1024,1024]{1,0:T(8,128)(2,1)} async-done(((bf16[1024,2048]{1,0:T(8,128)(2,1)}), bf16[1024,1024]{1,0:T(8,128)(2,1)}) %reduce-scatter.2.cloned.1.call-update) | async-done | bytes 2097168 | tf_op jit(solution)/shard_map/reduce_scatter | solution.py:390
  257.8 4.8 %copy.16 = bf16[1024,2048]{1,0:T(8,128)(2,1)} copy(bf16[1024,2048]{1,0:T(8,128)(2,1)} %all-reduce.2.cloned.1.call-done) | data formatting | bytes 8388608
  (34 shorter events, 0.3 us)
Async XLA Ops:
  7.2 73.7 %all-gather.2.cloned.1.call-start = ((), (), s32[]{:S(2)}) async-start(), calls=%async_computation.2 | async-start | bytes 6291456 | tf_op jit(solution)/shard_map/all_gather | solution.py:384
  7.9 33.4 %copy-start = (bf16[1024,1024]{1,0:T(8,128)(2,1)S(1)}, bf16[1024,1024]{1,0:T(8,128)(2,1)}, u32[]{:S(2)}) copy-start(bf16[1024,1024]{1,0:T(8,128)(2,1)} %query_ref.7) | copy-start | bytes 6291460
  7.9 193.7 %all-reduce.2.cloned.1.call-start = ((), (), s32[]{:S(2)}) async-start(), calls=%async_computation.3 | async-start | bytes 8388608 | tf_op jit(solution)/shard_map/psum | solution.py:392
  8.0 1.7 copy-start.1
  9.7 1.6 copy-start.2
  19.6 10.9 %collective-permute-start.1 = (bf16[2,64,1024]{2,1,0:T(8,128)(2,1)S(1)}, bf16[2,64,1024]{2,1,0:T(8,128)(2,1)S(1)}, u32[]{:S(2)}, u32[]{:S(2)}) collective-permute-start(bf16[2,64,1024]{2,1,0:T(8,128)(2,1)S(1)} %slice.48), channel_id=1, source_target_pairs={{0,4},{2,6},{4,0},{6,2},{8,12},{10,14},{12,8},{14,10},{16,20},{18,... | collective-permute-start | bytes 786440 | tf_op jit(solution)/shard_map/ppermute | solution.py:50
  22.6 7.2 %collective-permute-start.2 = (bf16[2,32,1024]{2,1,0:T(8,128)(2,1)S(1)}, bf16[2,32,1024]{2,1,0:T(8,128)(2,1)S(1)}, u32[]{:S(2)}, u32[]{:S(2)}) collective-permute-start(bf16[2,32,1024]{2,1,0:T(8,128)(2,1)S(1)} %slice.49), channel_id=1, source_target_pairs={{0,8},{2,10},{4,12},{6,14},{8,0},{10,2},{12,4},{14,6},{16,24},{18,... | collective-permute-start | bytes 393224 | tf_op jit(solution)/shard_map/ppermute | solution.py:50
  24.3 5.6 %collective-permute-start.3 = (bf16[2,16,1024]{2,1,0:T(8,128)(2,1)S(1)}, bf16[2,16,1024]{2,1,0:T(8,128)(2,1)S(1)}, u32[]{:S(2)}, u32[]{:S(2)}) collective-permute-start(bf16[2,16,1024]{2,1,0:T(8,128)(2,1)S(1)} %slice.50), channel_id=1, source_target_pairs={{0,16},{2,18},{4,20},{6,22},{8,24},{10,26},{12,28},{14,30},{16,0},... | collective-permute-start | bytes 196616 | tf_op jit(solution)/shard_map/ppermute | solution.py:50
  29.9 5.7 %collective-permute-start.4 = (bf16[2,48,1024]{2,1,0:T(8,128)(2,1)S(1)}, bf16[2,48,1024]{2,1,0:T(8,128)(2,1)S(1)}, u32[]{:S(2)}, u32[]{:S(2)}) collective-permute-start(bf16[2,48,1024]{2,1,0:T(8,128)(2,1)S(1)} %pad_maximum_fusion), channel_id=1, source_target_pairs={{0,4},{2,6},{4,0},{6,2},{8,12},{10,14},{12,8},{14,10},{16,20},{18,... | collective-permute-start | bytes 589832 | tf_op jit(solution)/shard_map/ppermute | solution.py:50
  35.7 5.0 %collective-permute-start.5 = (bf16[2,32,1024]{2,1,0:T(8,128)(2,1)S(1)}, bf16[2,32,1024]{2,1,0:T(8,128)(2,1)S(1)}, u32[]{:S(2)}, u32[]{:S(2)}) collective-permute-start(bf16[2,32,1024]{2,1,0:T(8,128)(2,1)S(1)} %pad_maximum_fusion.2), channel_id=1, source_target_pairs={{0,8},{2,10},{4,12},{6,14},{8,0},{10,2},{12,4},{14,6},{16,24},{18,... | collective-permute-start | bytes 393224 | tf_op jit(solution)/shard_map/ppermute | solution.py:50
  40.7 14.6 %collective-permute-start.6 = (bf16[2,192,1024]{2,1,0:T(8,128)(2,1)S(1)}, bf16[2,192,1024]{2,1,0:T(8,128)(2,1)S(1)}, u32[]{:S(2)}, u32[]{:S(2)}) collective-permute-start(bf16[2,192,1024]{2,1,0:T(8,128)(2,1)S(1)} %constant_dynamic-update-slice_fusion.kept_ref), channel_id=1, source_target_pairs={{0,2},{2,0},{4,6},{6,4},{8,10},{10,8},{12,14},{14,12},{16,18},{18,... | collective-permute-start | bytes 2359304 | tf_op jit(solution)/shard_map/ppermute | solution.py:50
  40.8 14.6 %collective-permute-start = (bf16[2,128,1024]{2,1,0:T(8,128)(2,1)S(1)}, bf16[2,128,1024]{2,1,0:T(8,128)(2,1)S(1)}, u32[]{:S(2)}, u32[]{:S(2)}) collective-permute-start(bf16[2,128,1024]{2,1,0:T(8,128)(2,1)S(1)} %get-tuple-element.22), channel_id=1, source_target_pairs={{0,2},{2,0},{4,6},{6,4},{8,10},{10,8},{12,14},{14,12},{16,18},{18,... | collective-permute-start | bytes 1572872 | tf_op jit(solution)/shard_map/ppermute | solution.py:50
  79.3 0.9 copy-start.3
  80.1 0.7 copy-start.6
  80.8 9.4 %copy-start.5 = (bf16[1024,1024]{1,0:T(8,128)(2,1)}, bf16[1024,1024]{1,0:T(8,128)(2,1)S(1)}, u32[]{:S(2)}) copy-start(bf16[1024,1024]{1,0:T(8,128)(2,1)S(1)} %get-tuple-element.27.mixed_ref) | copy-start | bytes 6291460
  90.0 167.9 %reduce-scatter.2.cloned.1.call-start = ((), (), s32[]{:S(2)}) async-start(), calls=%async_computation.1 | async-start | bytes 6291456 | tf_op jit(solution)/shard_map/reduce_scatter | solution.py:390
  98.4 9.5 %copy-start.4 = (bf16[2,192,1024]{2,1,0:T(8,128)(2,1)S(1)}, bf16[2,192,1024]{2,1,0:T(8,128)(2,1)}, u32[]{:S(2)}) copy-start(bf16[2,192,1024]{2,1,0:T(8,128)(2,1)} %copy-done.3) | copy-start | bytes 2359300
  98.5 9.5 %copy-start.7 = (f32[8,8,1024]{2,1,0:T(8,128)S(1)}, f32[8,8,1024]{2,1,0:T(8,128)}, u32[]{:S(2)}) copy-start(f32[8,8,1024]{2,1,0:T(8,128)} %copy-done.6) | copy-start | bytes 786436
  125.6 2.3 collective-permute-start.8
  128.2 7.6 %collective-permute-start.10 = (bf16[2,32,1024]{2,1,0:T(8,128)(2,1)S(1)}, bf16[2,32,1024]{2,1,0:T(8,128)(2,1)S(1)}, u32[]{:S(2)}, u32[]{:S(2)}) collective-permute-start(bf16[2,32,1024]{2,1,0:T(8,128)(2,1)S(1)} %get-tuple-element.40), channel_id=1, source_target_pairs={{0,8},{2,10},{4,12},{6,14},{8,0},{10,2},{12,4},{14,6},{16,24},{18,... | collective-permute-start | bytes 393224 | tf_op jit(solution)/shard_map/ppermute | solution.py:50
  135.9 7.8 %collective-permute-start.11 = (bf16[2,48,1024]{2,1,0:T(8,128)(2,1)S(1)}, bf16[2,48,1024]{2,1,0:T(8,128)(2,1)S(1)}, u32[]{:S(2)}, u32[]{:S(2)}) collective-permute-start(bf16[2,48,1024]{2,1,0:T(8,128)(2,1)S(1)} %pad_maximum_fusion.1), channel_id=1, source_target_pairs={{0,4},{2,6},{4,0},{6,2},{8,12},{10,14},{12,8},{14,10},{16,20},{18,... | collective-permute-start | bytes 589832 | tf_op jit(solution)/shard_map/ppermute | solution.py:50
  135.9 31.5 %collective-permute-start.7 = (bf16[2,128,1024]{2,1,0:T(8,128)(2,1)S(1)}, bf16[2,128,1024]{2,1,0:T(8,128)(2,1)S(1)}, u32[]{:S(2)}, u32[]{:S(2)}) collective-permute-start(bf16[2,128,1024]{2,1,0:T(8,128)(2,1)S(1)} %get-tuple-element.34), channel_id=1, source_target_pairs={{0,2},{2,0},{4,6},{6,4},{8,10},{10,8},{12,14},{14,12},{16,18},{18,... | collective-permute-start | bytes 1572872 | tf_op jit(solution)/shard_map/ppermute | solution.py:50
  136.1 31.4 %collective-permute-start.9 = (bf16[2,64,1024]{2,1,0:T(8,128)(2,1)S(1)}, bf16[2,64,1024]{2,1,0:T(8,128)(2,1)S(1)}, u32[]{:S(2)}, u32[]{:S(2)}) collective-permute-start(bf16[2,64,1024]{2,1,0:T(8,128)(2,1)S(1)} %slice.64), channel_id=1, source_target_pairs={{0,4},{2,6},{4,0},{6,2},{8,12},{10,14},{12,8},{14,10},{16,20},{18,... | collective-permute-start | bytes 786440 | tf_op jit(solution)/shard_map/ppermute | solution.py:50
  143.7 23.7 %collective-permute-start.12 = (bf16[2,32,1024]{2,1,0:T(8,128)(2,1)S(1)}, bf16[2,32,1024]{2,1,0:T(8,128)(2,1)S(1)}, u32[]{:S(2)}, u32[]{:S(2)}) collective-permute-start(bf16[2,32,1024]{2,1,0:T(8,128)(2,1)S(1)} %add_convert_fusion.1), channel_id=1, source_target_pairs={{0,8},{2,10},{4,12},{6,14},{8,0},{10,2},{12,4},{14,6},{16,24},{18,... | collective-permute-start | bytes 393224 | tf_op jit(solution)/shard_map/ppermute | solution.py:50
  145.6 21.9 %collective-permute-start.13 = (bf16[2,16,1024]{2,1,0:T(8,128)(2,1)S(1)}, bf16[2,16,1024]{2,1,0:T(8,128)(2,1)S(1)}, u32[]{:S(2)}, u32[]{:S(2)}) collective-permute-start(bf16[2,16,1024]{2,1,0:T(8,128)(2,1)S(1)} %add_convert_fusion.3), channel_id=1, source_target_pairs={{0,16},{2,18},{4,20},{6,22},{8,24},{10,26},{12,28},{14,30},{16,0},... | collective-permute-start | bytes 196616 | tf_op jit(solution)/shard_map/ppermute | solution.py:50
Sparse Core Ops, SparseCore 0:
  9.5 59.4 all-gather.1
  90.1 111.4 all-reduce.1
  204.6 53.2 reduce-scatter.1

commit v2 on v1

v2 whole, which is shorter than its diff:
```python
import functools

import jax
import jax.numpy as jnp
from jax import lax
from jax.experimental import pallas as pl
from jax.experimental.pallas import tpu as pltpu
from jax.sharding import PartitionSpec as P

HEAD_DIM = 128
BLOCK = 256
POOLED = 128
SCALE = HEAD_DIM ** -0.5
SCALE2 = SCALE * 1.4426950408889634
VMEM = 48 * 1024 * 1024
WIDE_VMEM = 60 * 1024 * 1024
F32 = jnp.float32
BF16 = jnp.bfloat16


def params(limit=VMEM):
    return pltpu.CompilerParams(vmem_limit_bytes=limit)


def cost(micros, like):
    scale = 0.05 * micros * like.shape[0] * like.shape[1] / (1 << 20)
    return pl.CostEstimate(
        flops=int(scale * 1.15e9), bytes_accessed=int(scale * 3.6e6), transcendentals=0
    )


def nn(a, b):
    return lax.dot_general(a, b, (((1,), (0,)), ((), ())), preferred_element_type=F32)


def nt(a, b):
    return lax.dot_general(a, b, (((1,), (1,)), ((), ())), preferred_element_type=F32)


def tn(a, b):
    return lax.dot_general(a, b, (((0,), (0,)), ((), ())), preferred_element_type=F32)


def widen_matrix(rows, columns, shift):
    row = lax.broadcasted_iota(jnp.int32, (rows, columns), 0)
    column = lax.broadcasted_iota(jnp.int32, (rows, columns), 1)
    return jnp.where((row >> shift) == column, 0.5 ** shift, 0.0).astype(BF16)


def added(first, second):
    return (first.astype(F32) + second.astype(F32)).astype(BF16)


def tie(value, *others):
    return lax.optimization_barrier((value, *others))[0] if others else value


def from_partner(block, bit):
    count = lax.axis_size("seq")
    return lax.ppermute(block, "seq", [(low, low ^ 1 << bit) for low in range(count)])


def column(rows, width):
    return pl.BlockSpec((rows, width), lambda h: (0, h))


def row(rows, width):
    return pl.BlockSpec((width, rows), lambda h: (h, 0))


def pair(rows, width):
    return pl.BlockSpec((2, rows, width), lambda h: (0, 0, h))


def stat(rows, heads):
    return pl.BlockSpec((heads, 8, rows), lambda h: (h, 0, 0))


def lanes_of(ref):
    return [slice(start, start + HEAD_DIM) for start in range(0, ref.shape[-1], HEAD_DIM)]


def blocks_of(ref):
    return [slice(start, start + BLOCK) for start in range(0, ref.shape[0], BLOCK)]


def step_heads(features):
    return min(features // HEAD_DIM, 2)


def pool_kernel(local, cross, key_ref, value_ref, coarse_ref, *refs):
    pooled, held_ref = refs[:-1], refs[-1]
    for index, ref in enumerate((key_ref, value_ref)):
        for head, lanes in enumerate(lanes_of(ref)):
            held = held_ref.at[index, head]
            count = ref.shape[0]
            coarse_start = 0
            held[...] = ref[:, lanes].astype(F32)
            for level in range(1, local + cross):
                count //= 2
                even = held[pl.ds(0, count, stride=2), :]
                odd = held[pl.ds(1, count, stride=2), :]
                rows = (0.5 * (even + odd)).astype(BF16)
                if level < local:
                    coarse_ref[index, coarse_start : coarse_start + count, lanes] = rows
                    coarse_start += count
                else:
                    pooled[level - local][index, :, lanes] = rows
                held[0:count, :] = rows.astype(F32)


def pool(key_states, value_states, local, cross):
    rows, features = key_states.shape
    heads = step_heads(features)
    width = heads * HEAD_DIM
    counts = [sum(rows >> level for level in range(1, local))]
    counts += [POOLED >> bit for bit in range(cross)]
    return pl.pallas_call(
        functools.partial(pool_kernel, local, cross),
        grid=(features // width,),
        in_specs=[column(rows, width)] * 2,
        out_specs=[pair(count, width) for count in counts],
        out_shape=[jax.ShapeDtypeStruct((2, count, features), BF16) for count in counts],
        scratch_shapes=[pltpu.VMEM((2, heads, rows, HEAD_DIM), F32)],
        compiler_params=params(WIDE_VMEM),
        cost_estimate=cost(5, key_states),
        name="pool",
    )(key_states, value_states)


def local_starts(block, local, rows):
    starts = []
    offset = 0
    for level in range(1, local):
        starts.append(offset + (block >> (level - 1) ^ 1) * POOLED)
        offset += rows >> level
    return starts


def local_list(own, coarse, block, local):
    parts = [own[block * BLOCK : (block + 1) * BLOCK]]
    parts += [coarse[at : at + POOLED] for at in local_starts(block, local, own.shape[0])]
    return jnp.concatenate(parts, axis=0)


def lane_max(scores):
    count = scores.shape[1]
    while count > HEAD_DIM:
        half = (count // HEAD_DIM + 1) // 2 * HEAD_DIM
        top = jnp.maximum(scores[:, : count - half], scores[:, half:])
        if 2 * half > count:
            top = jnp.concatenate([top, scores[:, count - half : half]], axis=1)
        scores, count = top, half
    return jnp.max(scores, axis=1, keepdims=True)


def attend(queries, keys, values):
    scores = nt(queries, keys)
    top = lane_max(scores)
    weights = jnp.exp2((scores - top) * SCALE2).astype(BF16)
    ones = jnp.ones((values.shape[0], HEAD_DIM), BF16)
    mixed = nn(weights, jnp.concatenate([values, ones], axis=1))
    total = mixed[:, HEAD_DIM:]
    return mixed[:, :HEAD_DIM] / total, top * SCALE2 + jnp.log2(total)


def near_kernel(local, query_ref, key_ref, value_ref, coarse_ref, out_ref, lse_ref):
    for head, lanes in enumerate(lanes_of(query_ref)):
        keys, values = key_ref[:, lanes], value_ref[:, lanes]
        coarse_keys, coarse_values = coarse_ref[0, :, lanes], coarse_ref[1, :, lanes]
        for block, here in enumerate(blocks_of(query_ref)):
            mixed, lse = attend(
                query_ref[here, lanes],
                local_list(keys, coarse_keys, block, local),
                local_list(values, coarse_values, block, local),
            )
            out_ref[here, lanes] = mixed.astype(BF16)
            lse_ref[head, :, here] = lse.T[:8]


def far_kernel(parts, query_ref, *refs):
    far, (near_ref, near_lse_ref, mixed_ref, lse_ref) = refs[:parts], refs[parts:]
    for head, lanes in enumerate(lanes_of(query_ref)):
        keys = jnp.concatenate([part[0, :, lanes] for part in far], axis=0)
        values = jnp.concatenate([part[1, :, lanes] for part in far], axis=0)
        for here in blocks_of(query_ref):
            mixed, lse = attend(query_ref[here, lanes], keys, values)
            near_lse = jnp.broadcast_to(near_lse_ref[head, 0:1, here], (HEAD_DIM, BLOCK)).T
            top = jnp.maximum(near_lse, lse)
            near_share = jnp.exp2(near_lse - top)
            far_share = jnp.exp2(lse - top)
            total = near_share + far_share
            both = near_ref[here, lanes].astype(F32) * near_share + mixed * far_share
            mixed_ref[here, lanes] = (both / total).astype(BF16)
            lse_ref[head, :, here] = (top + jnp.log2(total)).T[:8]


def near_forward(queries, key_states, value_states, coarse, local):
    rows, features = queries.shape
    heads = step_heads(features)
    width = heads * HEAD_DIM
    return pl.pallas_call(
        functools.partial(near_kernel, local),
        grid=(features // width,),
        in_specs=[column(rows, width)] * 3 + [pair(coarse.shape[1], width)],
        out_specs=[column(rows, width), stat(rows, heads)],
        out_shape=[
            jax.ShapeDtypeStruct((rows, features), BF16),
            jax.ShapeDtypeStruct((features // HEAD_DIM, 8, rows), F32),
        ],
        compiler_params=params(),
        cost_estimate=cost(9, queries),
        name="near_forward",
    )(queries, key_states, value_states, coarse)


def far_forward(queries, far, near, near_lse):
    rows, features = queries.shape
    heads = step_heads(features)
    width = heads * HEAD_DIM
    return pl.pallas_call(
        functools.partial(far_kernel, len(far)),
        grid=(features // width,),
        in_specs=[column(rows, width)]
        + [pair(part.shape[1], width) for part in far]
        + [column(rows, width), stat(rows, heads)],
        out_specs=[column(rows, width), stat(rows, heads)],
        out_shape=[
            jax.ShapeDtypeStruct((rows, features), BF16),
            jax.ShapeDtypeStruct((features // HEAD_DIM, 8, rows), F32),
        ],
        compiler_params=params(WIDE_VMEM),
        cost_estimate=cost(10, queries),
        name="far_forward",
    )(queries, *far, near, near_lse)


def attend_back(queries, grad_mixed, keys, values, keys_across, lse, inner):
    weights = jnp.exp2(nt(keys, queries) * SCALE2 - lse)
    grad_probs = nt(values, grad_mixed)
    grad_scores = (weights * (grad_probs - inner)).astype(BF16)
    both = jnp.concatenate([grad_mixed, queries], axis=1)
    grad_values = nn(weights.astype(BF16), both)[:, :HEAD_DIM]
    grad_keys = nn(grad_scores, both)[:, HEAD_DIM:]
    return nn(keys_across, grad_scores), grad_keys, grad_values


def far_back_kernel(parts, query_ref, mixed_ref, grad_ref, lse_ref, *refs):
    far, grad_far = refs[:parts], refs[parts : 2 * parts]
    grad_query_ref, inner_ref = refs[2 * parts :]
    for head, lanes in enumerate(lanes_of(query_ref)):
        keys = jnp.concatenate([part[0, :, lanes] for part in far], axis=0)
        values = jnp.concatenate([part[1, :, lanes] for part in far], axis=0)
        keys_across = keys.T
        total_keys = total_values = None
        for here in blocks_of(query_ref):
            grad = grad_ref[here, lanes]
            product = (grad.astype(F32) * mixed_ref[here, lanes].astype(F32)).T
            inner = jnp.sum(product, axis=0, keepdims=True)
            inner_ref[head, :, here] = jnp.broadcast_to(inner, (8, BLOCK))
            grad_queries, grad_keys, grad_values = attend_back(
                query_ref[here, lanes], grad, keys, values, keys_across,
                lse_ref[head, 0:1, here], inner,
            )
            grad_query_ref[lanes, here] = grad_queries.astype(BF16)
            total_keys = grad_keys if total_keys is None else total_keys + grad_keys
            total_values = grad_values if total_values is None else total_values + grad_values
        total_keys = (total_keys * SCALE).astype(BF16)
        total_values = total_values.astype(BF16)
        start = 0
        for ref in grad_far:
            count = ref.shape[1]
            ref[0, :, lanes] = total_keys[start : start + count]
            ref[1, :, lanes] = total_values[start : start + count]
            start += count


def far_backward(queries, far, mixed, grad_mixed, lse):
    rows, features = queries.shape
    heads = step_heads(features)
    width = heads * HEAD_DIM
    far_specs = [pair(part.shape[1], width) for part in far]
    return pl.pallas_call(
        functools.partial(far_back_kernel, len(far)),
        grid=(features // width,),
        in_specs=[column(rows, width)] * 3 + [stat(rows, heads)] + far_specs,
        out_specs=far_specs + [row(rows, width), stat(rows, heads)],
        out_shape=[jax.ShapeDtypeStruct(part.shape, BF16) for part in far]
        + [
            jax.ShapeDtypeStruct((features, rows), BF16),
            jax.ShapeDtypeStruct((features // HEAD_DIM, 8, rows), F32),
        ],
        compiler_params=params(WIDE_VMEM),
        cost_estimate=cost(14, queries),
        name="far_backward",
    )(queries, mixed, grad_mixed, lse, *far)


def near_back_kernel(
    local, parts, query_ref, key_ref, value_ref, coarse_ref, grad_ref, lse_ref, inner_ref,
    far_query_ref, *refs,
):
    far, (grad_query_ref, grad_key_ref, grad_value_ref) = refs[:parts], refs[-3:]
    rows = query_ref.shape[0]
    blocks = rows // BLOCK
    matrix = widen_matrix(BLOCK, POOLED, 1)
    for head, lanes in enumerate(lanes_of(query_ref)):
        keys, values = key_ref[:, lanes], value_ref[:, lanes]
        coarse_keys, coarse_values = coarse_ref[0, :, lanes], coarse_ref[1, :, lanes]
        keys_across, coarse_across = keys.T, coarse_keys.T
        own = [[None] * blocks, [None] * blocks]
        pooled = [[[None] * (blocks >> (level - 1)) for level in range(1, local)] for _ in range(2)]
        for index in range(2):
            held = None
            for part in far[::-1]:
                value = part[index, :, lanes].astype(F32)
                if held is not None:
                    wider = widen_matrix(value.shape[0], held.shape[0], 1)
                    value = value + nn(wider, held.astype(BF16))
                held = value
            pooled[index].append([held])
        for block, here in enumerate(blocks_of(query_ref)):
            starts = local_starts(block, local, rows)
            across = [keys_across[:, here]] + [coarse_across[:, at : at + POOLED] for at in starts]
            grad_queries, grad_keys, grad_values = attend_back(
                query_ref[here, lanes], grad_ref[here, lanes],
                local_list(keys, coarse_keys, block, local),
                local_list(values, coarse_values, block, local),
                jnp.concatenate(across, axis=1),
                lse_ref[head, 0:1, here], inner_ref[head, 0:1, here],
            )
            grad_queries = (grad_queries + far_query_ref[lanes, here].astype(F32)) * SCALE
            grad_query_ref[here, lanes] = grad_queries.T.astype(BF16)
            for index, value in enumerate((grad_keys * SCALE, grad_values)):
                own[index][block] = value[:BLOCK]
                for level in range(1, local):
                    sibling = block >> (level - 1) ^ 1
                    start = BLOCK + (level - 1) * POOLED
                    piece = value[start : start + POOLED]
                    held = pooled[index][level - 1]
                    held[sibling] = piece if held[sibling] is None else held[sibling] + piece
        for index, ref in enumerate((grad_key_ref, grad_value_ref)):
            for level in range(local, 0, -1):
                for half in range(len(pooled[index][level - 1])):
                    wide = nn(matrix, pooled[index][level - 1][half].astype(BF16))
                    if level == 1:
                        own[index][half] = own[index][half] + wide
                    else:
                        below = pooled[index][level - 2]
                        below[2 * half] = below[2 * half] + wide[:POOLED]
                        below[2 * half + 1] = below[2 * half + 1] + wide[POOLED:]
            for block, here in enumerate(blocks_of(query_ref)):
                ref[here, lanes] = own[index][block].astype(BF16)


def near_backward(operands, grads, local, part, parts):
    queries, coarse, pooled = operands[0], operands[3], operands[8:]
    rows, features = queries.shape
    heads = step_heads(features)
    width = heads * HEAD_DIM
    steps = features // width // parts
    first = part * steps

    def wide(count):
        return pl.BlockSpec((count, width), lambda h: (0, first + h))

    def pair_at(count):
        return pl.BlockSpec((2, count, width), lambda h: (0, 0, first + h))

    stats = pl.BlockSpec((heads, 8, rows), lambda h: (first + h, 0, 0))
    across = pl.BlockSpec((width, rows), lambda h: (first + h, 0))
    count = len(operands)
    return pl.pallas_call(
        functools.partial(near_back_kernel, local, len(pooled)),
        grid=(steps,),
        in_specs=[wide(rows)] * 3
        + [pair_at(coarse.shape[1]), wide(rows), stats, stats, across]
        + [pair_at(rows_of.shape[1]) for rows_of in pooled]
        + [pl.BlockSpec(memory_space=pl.ANY)] * len(grads),
        out_specs=[wide(rows)] * 3,
        out_shape=[jax.ShapeDtypeStruct((rows, features), BF16)] * 3,
        input_output_aliases={count + index: index for index in range(len(grads))},
        compiler_params=params(),
        cost_estimate=cost(18 / parts, queries),
        name="near_backward",
    )(*operands, *grads)


def index_call(
    kernel, name, micros, scalars, grid, in_specs, out_spec, out_shape, args, limit=VMEM, aliases={}
):
    return pl.pallas_call(
        kernel,
        grid_spec=pltpu.PrefetchScalarGridSpec(
            num_scalar_prefetch=1, grid=grid, in_specs=in_specs, out_specs=out_spec
        ),
        out_shape=out_shape,
        compiler_params=params(limit),
        input_output_aliases=aliases,
        cost_estimate=cost(micros, args[0]),
        name=name,
    )(scalars, *args)


def project_kernel(which_ref, mixed_ref, weight_ref, *refs):
    share = nn(mixed_ref[...], weight_ref[...]).astype(BF16)
    if len(refs) == 2:
        share = (share.astype(F32) + refs[0][...].astype(F32)).astype(BF16)
    refs[-1][...] = share


def project(mixed, out_weight, which, arrived=None):
    rows, features = mixed.shape
    width = min(512, features)
    steps = features // width
    out = pl.BlockSpec((rows, width), lambda j, which: (0, j))
    return index_call(
        project_kernel, "project", 5, which, (steps,),
        [
            pl.BlockSpec((rows, features), lambda j, which: (0, 0)),
            pl.BlockSpec((features, width), lambda j, which: (0, which[0] * steps + j)),
        ]
        + ([] if arrived is None else [out]),
        out, jax.ShapeDtypeStruct((rows, features), BF16),
        (mixed, out_weight) if arrived is None else (mixed, out_weight, arrived),
    )


def mix_back_kernel(which_ref, own_ref, other_ref, own_weight_ref, other_weight_ref, out_ref):
    total = nt(own_ref[...], own_weight_ref[...]) + nt(other_ref[...], other_weight_ref[...])
    out_ref[...] = total.astype(BF16)


def mix_back(own, other, out_weight, which):
    rows, features = own.shape
    width = min(512, features)
    whole = pl.BlockSpec((rows, features), lambda j, which: (0, 0))
    return index_call(
        mix_back_kernel, "mix_back", 8, which, (features // width,),
        [
            whole,
            whole,
            pl.BlockSpec((width, features), lambda j, which: (j, which[0])),
            pl.BlockSpec((width, features), lambda j, which: (j, 1 - which[0])),
        ],
        pl.BlockSpec((rows, width), lambda j, which: (0, j)),
        jax.ShapeDtypeStruct((rows, features), BF16),
        (own, other, out_weight, out_weight),
    )


def weight_kernel(which_ref, mixed_ref, grad_ref, mine_ref, sent_ref):
    share = tn(mixed_ref[...], grad_ref[...]).astype(BF16)

    @pl.when(pl.program_id(0) == 0)
    def first():
        sent_ref[...] = share

    @pl.when(pl.program_id(0) == 1)
    def second():
        mine_ref[...] = share


def weight_halves(mixed, grad, which):
    rows, features = mixed.shape
    half = features // 2
    columns = grad.shape[1]
    steps = max(columns // 512, 1)
    width = columns // steps

    def mine_index(i, j, which):
        return 0, jnp.where(i == 1, j, 0)

    def sent_index(i, j, which):
        return 0, jnp.where(i == 0, j, steps - 1)

    return index_call(
        weight_kernel, "weight_halves", 4, which[None], (2, steps),
        [
            pl.BlockSpec((rows, half), lambda i, j, which: (0, 1 - i ^ which[0])),
            pl.BlockSpec((rows, width), lambda i, j, which: (0, j)),
        ],
        [pl.BlockSpec((half, width), mine_index), pl.BlockSpec((half, width), sent_index)],
        [jax.ShapeDtypeStruct((half, columns), BF16)] * 2, (mixed, grad),
    )


def add_kernel(which_ref, first_ref, second_ref, mine_ref, sent_ref):
    total = added(first_ref[...], second_ref[...])

    @pl.when(pl.program_id(0) == 0)
    def first():
        sent_ref[...] = total

    @pl.when(pl.program_id(0) == 1)
    def second():
        mine_ref[...] = total


def add_halves(first, second, which, micros):
    rows, columns = first.shape
    half = rows // 2
    spec = pl.BlockSpec((half, columns), lambda j, which: (1 - j ^ which[0], 0))
    out = pl.BlockSpec((half, columns), lambda j, which: (0, 0))
    return index_call(
        add_kernel, "add_halves", micros, which[None], (2,), [spec, spec], [out, out],
        [jax.ShapeDtypeStruct((half, columns), BF16)] * 2, (first, second), limit=WIDE_VMEM,
    )


def place_kernel(chunks, where_ref, first_ref, second_ref, *refs):
    out_ref = refs[-1]
    for index, ref in enumerate((first_ref, second_ref)):

        @pl.when(pl.program_id(0) == index)
        def copy(index=index, ref=ref):
            size = ref.shape[0] // chunks
            for chunk in range(chunks):
                start = pl.multiple_of((chunk ^ where_ref[index]) * size, size)
                out_ref[pl.ds(start, size), :] = ref[chunk * size : (chunk + 1) * size, :]


def place(first, second, chunks, where, held=None):
    half, columns = first.shape
    spec = pl.BlockSpec((half, columns), lambda step, where: (0, 0))
    return index_call(
        functools.partial(place_kernel, chunks), "place", 2, where, (2,),
        [spec, spec] + ([] if held is None else [pl.BlockSpec(memory_space=pl.ANY)]),
        pl.BlockSpec((half, columns), lambda step, where: (where[2], step ^ where[3])),
        jax.ShapeDtypeStruct((2 * half, 2 * columns), BF16),
        (first, second) if held is None else (first, second, held),
        aliases={} if held is None else {3: 0},
    )


def gather_far(pooled, meanwhile):
    cross = len(pooled)
    first, *chunks = [from_partner(rows, bit) for bit, rows in enumerate(pooled)]
    for bit in range(1, cross - 1):
        sizes = [chunk.shape[1] for chunk in chunks[bit:]]
        sent = jnp.concatenate(chunks[bit:], axis=1)
        if bit == 1:
            sent = tie(sent, meanwhile)
        arrived = from_partner(sent, bit)
        start = 0
        for index, size in enumerate(sizes):
            chunks[bit + index] = jnp.concatenate(
                [chunks[bit + index], arrived[:, start : start + size]], axis=1
            )
            start += size
    kept = jnp.concatenate(chunks, axis=1)
    return first, kept, from_partner(kept, 0)


def scatter_far(grad_first, grad_kept, grad_swapped, cross):
    parts = [from_partner(grad_first, 0)]
    arrived, after = yield move(grad_swapped, 0)
    kept = added(tie(grad_kept, *after), arrived)
    half = POOLED // 2
    chunks = [kept[:, index * half : (index + 1) * half] for index in range(cross - 1)]
    for bit in range(cross - 2, 0, -1):
        sizes = [chunk.shape[1] // 2 for chunk in chunks[bit:]]
        sent = jnp.concatenate([chunk[:, chunk.shape[1] // 2 :] for chunk in chunks[bit:]], axis=1)
        arrived, after = yield move(sent, bit, chunks[-1])
        chunks = list(tie(tuple(chunks), *after))
        start = 0
        for index, size in enumerate(sizes):
            chunks[bit + index] = added(
                chunks[bit + index][:, :size], arrived[:, start : start + size]
            )
            start += size
    parts += [from_partner(chunk, bit + 1) for bit, chunk in enumerate(chunks)]
    yield chunks[-1], tuple(parts)


def move(rows, bit, kept=None):
    return rows if kept is None else kept, from_partner(rows, bit)


def seq_bit(bit):
    return lax.axis_index("seq") >> bit & 1


def sum_rows(mine, sent, bits, micros):
    arrived, after = yield move(sent, 0, mine)
    for bit in bits[:-1]:
        mine, sent = add_halves(tie(mine, *after), arrived, seq_bit(bit), micros if after else 1)
        arrived, after = yield move(sent, bit, mine)
    rows = added(tie(mine, *after), arrived)
    arrived, after = yield move(rows, bits[-1])
    rows = added(tie(rows, *after), arrived)
    for bit in bits[-2::-1]:
        arrived, after = yield move(rows, bit)
        rows = jnp.concatenate([tie(rows, *after), arrived], axis=0)
    yield rows, move(rows, 0)


class Chain:
    def __init__(self, steps, count):
        self.steps, self.left = steps, count
        self.kept, self.moving = next(steps)

    def advance(self, *after):
        self.left -= 1
        self.kept, self.moving = self.steps.send((self.moving, after))


def chunk_index(bits):
    index = 0
    for bit in bits[:-1]:
        index = index * 2 + seq_bit(bit)
    return index


def solution_body(queries, key_states, value_states, out_weight, cotangent):
    rows, features = queries.shape
    cross = lax.axis_size("seq").bit_length() - 1
    local = (rows // POOLED).bit_length() - 1
    groups = lax.axis_size("head")
    group = lax.axis_index("head")
    swap = [(0, 1), (1, 0)]
    if groups == 2:
        other = lax.ppermute(cotangent, "head", swap)
    else:
        piece = lax.all_gather(cotangent, "head", axis=1, tiled=True)
    coarse, *pooled = pool(key_states, value_states, local, cross)
    near, near_lse = near_forward(queries, key_states, value_states, coarse, local)
    far = gather_far(pooled, near)
    mixed, lse = far_forward(queries, far, near, near_lse)
    if groups == 2:
        share = project(mixed, out_weight, (1 - group)[None])
        shared = lax.ppermute(share, "head", swap)
        first, second, flip = tie(cotangent, share), other, group
    else:
        partial_out = jnp.dot(mixed, out_weight, preferred_element_type=F32).astype(BF16)
        attended = lax.psum_scatter(partial_out, "head", scatter_dimension=1, tiled=True)
        grad_mixed = nt(piece, out_weight).astype(BF16)
        middle = piece.shape[1] // 2
        first, second, flip = piece[:, :middle], piece[:, middle:], 0
    first_bits = list(range(1, cross))
    second_bits = first_bits[1:] + first_bits[:1]
    first_halves = weight_halves(mixed, first, seq_bit(0))
    first_sum = Chain(sum_rows(*first_halves, first_bits, 1), 2 * cross - 2)
    second_halves = weight_halves(mixed, tie(second, *first_halves), seq_bit(0))
    second_sum = Chain(sum_rows(*second_halves, second_bits, 400), 2 * cross - 2)
    first_sum.advance()
    second_sum.advance()
    if groups == 2:
        ready = tie(cotangent, first_sum.kept, second_sum.kept)
        grad_mixed = mix_back(ready, other, out_weight, group[None])
    *grad_far, far_query, inner = far_backward(queries, far, mixed, grad_mixed, lse)
    far_sum = Chain(scatter_far(*grad_far, cross), cross - 1)
    arrivals = (inner, shared) if groups == 2 else (inner,)
    first_sum.advance(*arrivals)
    second_sum.advance(*arrivals)
    far_sum.advance(first_sum.kept, second_sum.kept)
    if groups == 2:
        attended = project(tie(mixed, far_sum.kept), out_weight, group[None], shared)
    far_sum.advance(*([attended] if groups == 2 else []))
    first_sum.advance(far_sum.kept)
    while far_sum.left:
        far_sum.advance(first_sum.kept)
    second_sum.advance(far_sum.kept)
    first_sum.advance(second_sum.kept, *far_sum.moving)
    second_sum.advance(*far_sum.moving)
    inner = tie(inner, first_sum.kept, second_sum.kept)
    operands = (
        queries, key_states, value_states, coarse, grad_mixed, lse, inner, far_query,
        *far_sum.moving,
    )
    parts = 2 if features % (4 * HEAD_DIM) == 0 else 1
    grads = ()
    for part in range(parts):
        grads = near_backward(operands, grads, local, part, parts)
        if first_sum.left:
            first_sum.advance(grads[0])
            second_sum.advance(grads[0])
    grad_queries, grad_keys, grad_values = grads
    for chain in (first_sum, second_sum):
        while chain.left:
            chain.advance()
    spots = [chunk_index(first_bits), chunk_index(second_bits)]
    flip = jnp.asarray(flip, jnp.int32)
    chunks = 1 << (cross - 2)
    (first_mine, first_other), (second_mine, second_other) = first_sum.moving, second_sum.moving
    grad_weight = place(
        first_mine, second_mine, chunks, jnp.stack([*spots, seq_bit(0), flip])
    )
    grad_weight = place(
        first_other, second_other, chunks, jnp.stack([*spots, 1 - seq_bit(0), flip]), grad_weight
    )
    return attended, grad_queries, grad_keys, grad_values, grad_weight


def solution(mesh):
    split = P("seq", "head")
    return jax.shard_map(
        solution_body,
        mesh=mesh,
        in_specs=(split, split, split, P("head", None), split),
        out_specs=(split, split, split, split, P("head", None)),
        check_vma=False,
    )
```

time: 269 us -> 178 us (0.66)
  waiting for transfers between devices: 110 us -> 31.5 us
  matrix products: 26.8 us -> 0 us
  Pallas kernels: 89.6 us -> 106 us
  between operations: 14 us -> 1.07 us
  starting transfers between devices: 18.4 us -> 28 us
    reduce_scatter x1 -> x0, waiting for transfers between devices: 56.2 us -> none  [solution_body(): lax.psum_scatter(partial_out, 'head', scatter_dimension=1, tiled=True)]
    psum x1 -> x0, waiting for transfers between devices: 28.2 us -> none  [solution_body(): grad_weight = lax.psum(tn(mixed, piece).astype(BF16), 'seq')]
    dot_general x3 -> x0, matrix products: 26.8 us -> none  [the longest x1 9.52 us: nt(): lax.dot_general(a, b, (((1,), (1,)), ((), ())), preferred_element_type=F32)]
    pallas_call x5 -> x16, Pallas kernels: 81.3 us -> 99.9 us  [the longest x11 43.6 us: index_call(): pl.pallas_call(kernel, grid_spec=pltpu.PrefetchScalarGridSpec(num_scalar_...]
    ppermute x14 -> x28, starting transfers between devices: 18.2 us -> 26 us  [from_partner(): lax.ppermute(block, 'seq', [(low, low ^ 1 << bit) for low in range(count)])]
    ppermute x0 -> x2, waiting for transfers between devices: none -> 4.69 us  [the longest x1 4.68 us: solution_body(): shared = lax.ppermute(share, 'head', swap)]
    ppermute x14 -> x28, waiting for transfers between devices: 24.9 us -> 26.8 us  [from_partner(): lax.ppermute(block, 'seq', [(low, low ^ 1 << bit) for low in range(count)])]
    unnamed x21 -> x54, local copies, waits for them, and re-layouts: 9.74 us -> 9.77 us
  transfers between devices with their start and end apart: 17 -> 30, of which waited for: 8 -> 11; matrix products, arithmetic and copies ran while one was open for 7% -> 1% of each run, Pallas kernels for 33% -> 55%
where the time goes in v2:
time: 178 us; the launch traced here: 177 us
  Pallas kernels  106 us (60%)
  waiting for transfers between devices  31.5 us (18%)
  starting transfers between devices  28 us (16%)
  local copies, waits for them, and re-layouts  10 us (6%)
    pallas_call x11, Pallas kernels, index_call(): pl.pallas_call(kernel, grid_spec=pltpu.PrefetchScalarGridSpec(num_scalar_...  43.6 us
    ppermute x28, waiting for transfers between devices, from_partner(): lax.ppermute(block, 'seq', [(low, low ^ 1 << bit) for low in range(count)])  26.8 us
    ppermute x28, starting transfers between devices, from_partner(): lax.ppermute(block, 'seq', [(low, low ^ 1 << bit) for low in range(count)])  26 us
    pallas_call x2, Pallas kernels, near_backward(): pl.pallas_call(functools.partial(near_back_kernel, local, len(pooled)), g...  24.2 us
    pallas_call x1, Pallas kernels, far_backward(): pl.pallas_call(functools.partial(far_back_kernel, len(far)), grid=(featur...  13.3 us
    pallas_call x1, Pallas kernels, far_forward(): pl.pallas_call(functools.partial(far_kernel, len(far)), grid=(features //...  10.6 us
    unnamed x54, local copies, waits for them, and re-layouts  9.77 us
    pallas_call x1, Pallas kernels, near_forward(): pl.pallas_call(functools.partial(near_kernel, local), grid=(features // w...  8.27 us
  transfers between devices with their start and end apart: 30, of which 11 were waited for; matrix products, arithmetic and copies ran while one was open for 1% of the time, Pallas kernels for 55%

profile of v2, /device:TPU:0, one launch (start us, length us, event | category | flops | bytes accessed | tf_op | source)
XLA Modules:
  0.0 177.3 jit_solution(11128142740958468295)
XLA Ops:
  0.6 6.0 %pool.1 = (bf16[2,768,1024]{2,1,0:T(8,128)(2,1)}, bf16[2,128,1024]{2,1,0:T(8,128)(2,1)}, bf16[2,64,1024]{2,1,0:T(8,128)(2,1)}, bf16[2,32,1024]{2,1,0:T(8,128)(2,1)}, bf16[2,16,1024]{2,1,0:T(8,128)(2,1)}) custom-call(bf16[1024,1024]{1,0:T(8,128)(2,1)} %key_ref.7, bf16[1024,1024]{1,0:T(8,128)(2,1)} %value_ref.7), custom_call_target="tpu_custom_call" | custom-call | flops 287500000 | bytes 900000 | tf_op jit(solution)/shard_map/pool/pallas_call | solution.py:118
  6.6 3.0 %collective-permute-start.1 = (bf16[2,64,1024]{2,1,0:T(8,128)(2,1)}, bf16[2,64,1024]{2,1,0:T(8,128)(2,1)S(1)}, u32[]{:S(2)}, u32[]{:S(2)}) collective-permute-start(bf16[2,64,1024]{2,1,0:T(8,128)(2,1)} %get-tuple-element.61), channel_id=1, source_target_pairs={{0,4},{2,6},{4,0},{6,2},{8,12},{10,14},{12,8},{14,10},{16,20},{18,... | collective-permute-start | bytes 786440 | tf_op jit(solution)/shard_map/ppermute | solution.py:60
  9.6 1.6 collective-permute-start.2
  11.2 2.6 %collective-permute-start.3 = (bf16[2,16,1024]{2,1,0:T(8,128)(2,1)}, bf16[2,16,1024]{2,1,0:T(8,128)(2,1)S(1)}, u32[]{:S(2)}, u32[]{:S(2)}) collective-permute-start(bf16[2,16,1024]{2,1,0:T(8,128)(2,1)} %get-tuple-element.63), channel_id=1, source_target_pairs={{0,16},{2,18},{4,20},{6,22},{8,24},{10,26},{12,28},{14,30},{16,0},... | collective-permute-start | bytes 196616 | tf_op jit(solution)/shard_map/ppermute | solution.py:60
  13.8 1.5 collective-permute-start.8
  15.3 8.3 %near_forward.1 = (bf16[1024,1024]{1,0:T(8,128)(2,1)S(1)}, f32[8,8,1024]{2,1,0:T(8,128)S(1)}) custom-call(bf16[1024,1024]{1,0:T(8,128)(2,1)S(1)} %copy-done.3, bf16[1024,1024]{1,0:T(8,128)(2,1)} %key_ref.7, bf16[1024,1024]{1,0:T(8,128)(2,1)} %value_ref.7, bf16[2,768,1024]{2,1,0:T(8,128)(2,1)} %get-tuple-element.64.coarse_ref), custom_call_target="tpu_custom_call" | custom-call | flops 517500000 | bytes 1620000 | tf_op jit(solution)/shard_map/near_forward/pallas_call | solution.py:202
  23.6 1.3 copy-done.9
  24.9 0.7 copy-done.13
  26.3 5.1 %collective-permute-done.4 = bf16[2,48,1024]{2,1,0:T(8,128)(2,1)S(1)} collective-permute-done((bf16[2,48,1024]{2,1,0:T(8,128)(2,1)S(1)}, bf16[2,48,1024]{2,1,0:T(8,128)(2,1)S(1)}, u32[]{:S(2)}, u32[]{:S(2)}) %collective-permute-start.4) | collective-permute-done | bytes 196640 | tf_op jit(solution)/shard_map/ppermute | solution.py:60
  32.0 4.5 %collective-permute-done.5 = bf16[2,32,1024]{2,1,0:T(8,128)(2,1)S(1)} collective-permute-done((bf16[2,32,1024]{2,1,0:T(8,128)(2,1)S(1)}, bf16[2,32,1024]{2,1,0:T(8,128)(2,1)S(1)}, u32[]{:S(2)}, u32[]{:S(2)}) %collective-permute-start.5) | collective-permute-done | bytes 131104 | tf_op jit(solution)/shard_map/ppermute | solution.py:60
  37.1 2.5 %collective-permute-done.refs_0_ = bf16[2,128,1024]{2,1,0:T(8,128)(2,1)S(1)} collective-permute-done((bf16[2,128,1024]{2,1,0:T(8,128)(2,1)S(1)}, bf16[2,128,1024]{2,1,0:T(8,128)(2,1)S(1)}, u32[]{:S(2)}, u32[]{:S(2)}) %collective-permute-start) | collective-permute-done | bytes 524320 | tf_op jit(solution)/shard_map/ppermute | solution.py:60
  39.6 0.8 copy-done.16
  40.7 10.6 %far_forward.1 = (bf16[1024,1024]{1,0:T(8,128)(2,1)}, f32[8,8,1024]{2,1,0:T(8,128)}) custom-call(bf16[1024,1024]{1,0:T(8,128)(2,1)} %query_ref.9, bf16[2,128,1024]{2,1,0:T(8,128)(2,1)} %copy-done.16, bf16[2,192,1024]{2,1,0:T(8,128)(2,1)} %copy-done.14, bf16[2,192,1024]{2,1,0:T(8,128)(2,1)} %copy-done.15, bf16[1024,1024]{1,0:T(8,128)(2,1)} %copy-done.9, ...), custom_call_target="tpu_custom_call" | custom-call | flops 575000000 | bytes 1800000 | tf_op jit(solution)/shard_map/far_forward/pallas_call | solution.py:221
  51.2 1.6 copy-done
  52.8 4.9 %project.2 = bf16[1024,1024]{1,0:T(8,128)(2,1)} custom-call(s32[1]{0:T(128)} %bitcast.3.which_ref, bf16[1024,1024]{1,0:T(8,128)(2,1)S(1)} %copy-done, bf16[1024,2048]{1,0:T(8,128)(2,1)} %weight_ref.3), custom_call_target="tpu_custom_call" | custom-call | flops 287500000 | bytes 900000 | tf_op jit(solution)/shard_map/project/pallas_call | solution.py:392
  58.2 6.0 %weight_halves.2 = (bf16[512,1024]{1,0:T(8,128)(2,1)S(1)}, bf16[512,1024]{1,0:T(8,128)(2,1)}) custom-call(s32[1]{0:T(128)} %bitcast.2.which_ref, bf16[1024,1024]{1,0:T(8,128)(2,1)S(1)} %copy-done.1, bf16[1024,1024]{1,0:T(8,128)(2,1)} %own_ref), custom_call_target="tpu_custom_call" | custom-call | flops 230000000 | bytes 720000 | tf_op jit(solution)/shard_map/weight_halves/pallas_call | solution.py:392
  64.2 1.0 copy-done.11
  65.2 5.2 %weight_halves.3 = (bf16[512,1024]{1,0:T(8,128)(2,1)S(1)}, bf16[512,1024]{1,0:T(8,128)(2,1)S(1)}) custom-call(s32[1]{0:T(128)} %bitcast.2.which_ref, bf16[1024,1024]{1,0:T(8,128)(2,1)S(1)} %copy-done.1, bf16[1024,1024]{1,0:T(8,128)(2,1)} %collective-permute-done.8.grad_ref.other_ref), custom_call_target="tpu_custom_call" | custom-call | flops 230000000 | bytes 720000 | tf_op jit(solution)/shard_map/weight_halves/pallas_call | solution.py:392
  70.4 1.0 copy-done.10
  71.9 2.9 %add_halves.4 = (bf16[256,1024]{1,0:T(8,128)(2,1)}, bf16[256,1024]{1,0:T(8,128)(2,1)}) custom-call(s32[1]{0:T(128)} %bitcast.1.which_ref, bf16[512,1024]{1,0:T(8,128)(2,1)} %copy-done.11, bf16[512,1024]{1,0:T(8,128)(2,1)} %collective-permute-done.7.second_ref), custom_call_target="tpu_custom_call" | custom-call | flops 28750000 | bytes 90000 | tf_op jit(solution)/shard_map/add_halves/pallas_call | solution.py:392
  75.4 2.8 %add_halves.5 = (bf16[256,1024]{1,0:T(8,128)(2,1)}, bf16[256,1024]{1,0:T(8,128)(2,1)}) custom-call(s32[1]{0:T(128)} %bitcast.4.which_ref, bf16[512,1024]{1,0:T(8,128)(2,1)} %copy-done.10, bf16[512,1024]{1,0:T(8,128)(2,1)} %collective-permute-done.9.second_ref), custom_call_target="tpu_custom_call" | custom-call | flops 28750000 | bytes 90000 | tf_op jit(solution)/shard_map/add_halves/pallas_call | solution.py:392
  78.6 7.2 %mix_back.1.grad_ref = bf16[1024,1024]{1,0:T(8,128)(2,1)S(1)} custom-call(s32[1]{0:T(128)} %bitcast.which_ref, bf16[1024,1024]{1,0:T(8,128)(2,1)S(1)} %copy-done.7, bf16[1024,1024]{1,0:T(8,128)(2,1)} %collective-permute-done.8.grad_ref.other_ref, bf16[1024,2048]{1,0:T(8,128)(2,1)} %weight_ref.3, bf16[1024,2048]{1,0:T(8,128)(2,1)} %weight_ref.3), custom_call_target="tpu_custom_call" | custom-call | flops 460000000 | bytes 1440000 | tf_op jit(solution)/shard_map/mix_back/pallas_call | solution.py:392
  85.8 1.3 copy-done.6
  87.1 13.3 %far_backward.1 = (bf16[2,128,1024]{2,1,0:T(8,128)(2,1)}, bf16[2,192,1024]{2,1,0:T(8,128)(2,1)}, bf16[2,192,1024]{2,1,0:T(8,128)(2,1)}, bf16[1024,1024]{1,0:T(8,128)(2,1)}, f32[8,8,1024]{2,1,0:T(8,128)}) custom-call(bf16[1024,1024]{1,0:T(8,128)(2,1)} %query_ref.9, bf16[1024,1024]{1,0:T(8,128)(2,1)} %get-tuple-element.89.mixed_ref, ...), custom_call_target="tpu_custom_call" | custom-call | flops 805000000 | bytes 2520000 | tf_op jit(solution)/shard_map/far_backward/pallas_call | solution.py:283
  101.0 4.7 %collective-permute-done.10.refs_0_ = bf16[1024,1024]{1,0:T(8,128)(2,1)} collective-permute-done((bf16[1024,1024]{1,0:T(8,128)(2,1)}, bf16[1024,1024]{1,0:T(8,128)(2,1)}, u32[]{:S(2)}, u32[]{:S(2)}) %collective-permute-start.10) | collective-permute-done | bytes 2097184 | tf_op jit(solution)/shard_map/ppermute | solution.py:632
  105.7 0.8 copy-done.18
  106.5 2.1 %add_halves.6 = (bf16[128,1024]{1,0:T(8,128)(2,1)}, bf16[128,1024]{1,0:T(8,128)(2,1)}) custom-call(s32[1]{0:T(128)} %bitcast.4.which_ref, bf16[256,1024]{1,0:T(8,128)(2,1)} %get-tuple-element.81.first_ref, bf16[256,1024]{1,0:T(8,128)(2,1)} %copy-done.18), custom_call_target="tpu_custom_call" | custom-call | flops 14375000 | bytes 45000 | tf_op jit(solution)/shard_map/add_halves/pallas_call | solution.py:392
  109.0 0.8 copy-done.22
  109.8 2.2 %add_halves.7 = (bf16[128,1024]{1,0:T(8,128)(2,1)}, bf16[128,1024]{1,0:T(8,128)(2,1)}) custom-call(s32[1]{0:T(128)} %bitcast.5.which_ref, bf16[256,1024]{1,0:T(8,128)(2,1)} %get-tuple-element.84.first_ref, bf16[256,1024]{1,0:T(8,128)(2,1)} %copy-done.22), custom_call_target="tpu_custom_call" | custom-call | flops 5750000128 | bytes 18000000 | tf_op jit(solution)/shard_map/add_halves/pallas_call | solution.py:392
  112.7 1.6 collective-permute-start.14
  114.5 5.1 %project.3 = bf16[1024,1024]{1,0:T(8,128)(2,1)} custom-call(s32[1]{0:T(128)} %bitcast.which_ref, bf16[1024,1024]{1,0:T(8,128)(2,1)S(1)} %copy-done.2, bf16[1024,2048]{1,0:T(8,128)(2,1)} %weight_ref.3, bf16[1024,1024]{1,0:T(8,128)(2,1)} %collective-permute-done.10.refs_0_), custom_call_target="tpu_custom_call" | custom-call | flops 287500000 | bytes 900000 | tf_op jit(solution)/shard_map/project/pallas_call | solution.py:392
  119.6 3.1 %collective-permute-done.14 = bf16[2,32,1024]{2,1,0:T(8,128)(2,1)S(1)} collective-permute-done((bf16[2,32,1024]{2,1,0:T(8,128)(2,1)S(1)}, bf16[2,32,1024]{2,1,0:T(8,128)(2,1)S(1)}, u32[]{:S(2)}, u32[]{:S(2)}) %collective-permute-start.14) | collective-permute-done | bytes 131104 | tf_op jit(solution)/shard_map/ppermute | solution.py:60
  122.8 0.6 collective-permute-start.16
  123.5 2.4 %collective-permute-start.22 = (bf16[128,1024]{1,0:T(8,128)(2,1)S(1)}, bf16[128,1024]{1,0:T(8,128)(2,1)S(1)}, u32[]{:S(2)}, u32[]{:S(2)}) collective-permute-start(bf16[128,1024]{1,0:T(8,128)(2,1)S(1)} %add_convert_fusion.4), channel_id=1, source_target_pairs={{0,16},{2,18},{4,20},{6,22},{8,24},{10,26},{12,28},{14,30},{16,0},... | collective-permute-start | bytes 786440 | tf_op jit(solution)/shard_map/ppermute | solution.py:60
  125.9 1.5 collective-permute-start.19
  127.4 3.2 %collective-permute-done.16 = bf16[2,48,1024]{2,1,0:T(8,128)(2,1)S(1)} collective-permute-done((bf16[2,48,1024]{2,1,0:T(8,128)(2,1)S(1)}, bf16[2,48,1024]{2,1,0:T(8,128)(2,1)S(1)}, u32[]{:S(2)}, u32[]{:S(2)}) %collective-permute-start.16) | collective-permute-done | bytes 196640 | tf_op jit(solution)/shard_map/ppermute | solution.py:60
  130.7 2.5 %collective-permute-start.21 = (bf16[2,16,1024]{2,1,0:T(8,128)(2,1)S(1)}, bf16[2,16,1024]{2,1,0:T(8,128)(2,1)S(1)}, u32[]{:S(2)}, u32[]{:S(2)}) collective-permute-start(bf16[2,16,1024]{2,1,0:T(8,128)(2,1)S(1)} %add_convert_fusion.7), channel_id=1, source_target_pairs={{0,16},{2,18},{4,20},{6,22},{8,24},{10,26},{12,28},{14,30},{16,0},... | collective-permute-start | bytes 196616 | tf_op jit(solution)/shard_map/ppermute | solution.py:60
  133.5 0.6 collective-permute-start.23
  134.1 2.2 %collective-permute-done.19.refs_1_ = bf16[2,64,1024]{2,1,0:T(8,128)(2,1)S(1)} collective-permute-done((bf16[2,64,1024]{2,1,0:T(8,128)(2,1)S(1)}, bf16[2,64,1024]{2,1,0:T(8,128)(2,1)S(1)}, u32[]{:S(2)}, u32[]{:S(2)}) %collective-permute-start.19) | collective-permute-done | bytes 262176 | tf_op jit(solution)/shard_map/ppermute | solution.py:60
  136.3 3.9 %collective-permute-done.21.refs_3_ = bf16[2,16,1024]{2,1,0:T(8,128)(2,1)S(1)} collective-permute-done((bf16[2,16,1024]{2,1,0:T(8,128)(2,1)S(1)}, bf16[2,16,1024]{2,1,0:T(8,128)(2,1)S(1)}, u32[]{:S(2)}, u32[]{:S(2)}) %collective-permute-start.21) | collective-permute-done | bytes 65568 | tf_op jit(solution)/shard_map/ppermute | solution.py:60
  140.2 0.6 collective-permute-done.20.refs_2_
  141.0 2.6 %collective-permute-start.27 = (bf16[128,1024]{1,0:T(8,128)(2,1)S(1)}, bf16[128,1024]{1,0:T(8,128)(2,1)S(1)}, u32[]{:S(2)}, u32[]{:S(2)}) collective-permute-start(bf16[128,1024]{1,0:T(8,128)(2,1)S(1)} %add_convert_fusion.1), channel_id=1, source_target_pairs={{0,16},{2,18},{4,20},{6,22},{8,24},{10,26},{12,28},{14,30},{16,0},... | collective-permute-start | bytes 786440 | tf_op jit(solution)/shard_map/ppermute | solution.py:60
  143.6 12.0 %near_backward.2 = (bf16[1024,1024]{1,0:T(8,128)(2,1)}, bf16[1024,1024]{1,0:T(8,128)(2,1)}, bf16[1024,1024]{1,0:T(8,128)(2,1)}) custom-call(bf16[1024,1024]{1,0:T(8,128)(2,1)S(1)} %copy-done.4, bf16[1024,1024]{1,0:T(8,128)(2,1)S(1)} %copy-done.5, bf16[1024,1024]{1,0:T(8,128)(2,1)} %value_ref.7, bf16[2,768,1024]{2,1,0:T(8,128)(2,1)} %get-tuple-element.64.coarse_ref, ...), custom_call_target="tpu_custom_call" | custom-call | flops 517500000 | bytes 1620000 | tf_op jit(solution)/shard_map/near_backward/pallas_call | solution.py:373
  155.7 1.6 collective-permute-start.25
  157.4 12.2 %near_backward.3 = (bf16[1024,1024]{1,0:T(8,128)(2,1)}, bf16[1024,1024]{1,0:T(8,128)(2,1)}, bf16[1024,1024]{1,0:T(8,128)(2,1)}) custom-call(bf16[1024,1024]{1,0:T(8,128)(2,1)S(1)} %copy-done.4, bf16[1024,1024]{1,0:T(8,128)(2,1)S(1)} %copy-done.5, bf16[1024,1024]{1,0:T(8,128)(2,1)} %value_ref.7, ...), custom_call_target="tpu_custom_call", output_to_operand_aliasing={{0}: (12, {}), {1}: (13, {}), {2}: (14, {})} | custom-call | flops 517500000 | bytes 1620000 | tf_op jit(solution)/shard_map/near_backward/pallas_call | solution.py:373
  170.6 2.0 %place.2.refs_0_ = bf16[1024,2048]{1,0:T(8,128)(2,1)} custom-call(s32[4]{0:T(128)S(1)} %add_add_fusion.1.where_ref, bf16[512,1024]{1,0:T(8,128)(2,1)S(1)} %constant_dynamic-update-slice_fusion.7.first_ref, bf16[512,1024]{1,0:T(8,128)(2,1)S(1)} %constant_dynamic-update-slice_fusion.11.second_ref), custom_call_target="tpu_custom_call" | custom-call | flops 57500000 | bytes 180000 | tf_op jit(solution)/shard_map/place/pallas_call | solution.py:392
  172.6 1.5 collective-permute-done.29.second_ref
  174.1 3.2 %place.3 = bf16[1024,2048]{1,0:T(8,128)(2,1)} custom-call(s32[4]{0:T(128)S(1)} %add_add_fusion.where_ref, bf16[512,1024]{1,0:T(8,128)(2,1)S(1)} %collective-permute-done.26.first_ref, bf16[512,1024]{1,0:T(8,128)(2,1)} %collective-permute-done.29.second_ref, bf16[1024,2048]{1,0:T(8,128)(2,1)} %place.2.refs_0_), custom_call_target="tpu_custom_call", output_to_operand_aliasing={{}: (3, {})} | custom-call | flops 57500000 | bytes 180000 | tf_op jit(solution)/shard_map/place/pallas_call | solution.py:392
  (106 shorter events, 7.7 us)
Async XLA Ops:
  0.6 14.7 %copy-start.3 = (bf16[1024,1024]{1,0:T(8,128)(2,1)S(1)}, bf16[1024,1024]{1,0:T(8,128)(2,1)}, u32[]{:S(2)}) copy-start(bf16[1024,1024]{1,0:T(8,128)(2,1)} %query_ref.9) | copy-start | bytes 6291460
  6.6 19.6 %collective-permute-start.1 = (bf16[2,64,1024]{2,1,0:T(8,128)(2,1)}, bf16[2,64,1024]{2,1,0:T(8,128)(2,1)S(1)}, u32[]{:S(2)}, u32[]{:S(2)}) collective-permute-start(bf16[2,64,1024]{2,1,0:T(8,128)(2,1)} %get-tuple-element.61), channel_id=1, source_target_pairs={{0,4},{2,6},{4,0},{6,2},{8,12},{10,14},{12,8},{14,10},{16,20},{18,... | collective-permute-start | bytes 786440 | tf_op jit(solution)/shard_map/ppermute | solution.py:60
  9.6 16.0 %collective-permute-start.2 = (bf16[2,32,1024]{2,1,0:T(8,128)(2,1)}, bf16[2,32,1024]{2,1,0:T(8,128)(2,1)S(1)}, u32[]{:S(2)}, u32[]{:S(2)}) collective-permute-start(bf16[2,32,1024]{2,1,0:T(8,128)(2,1)} %get-tuple-element.62), channel_id=1, source_target_pairs={{0,8},{2,10},{4,12},{6,14},{8,0},{10,2},{12,4},{14,6},{16,24},{18,... | collective-permute-start | bytes 393224 | tf_op jit(solution)/shard_map/ppermute | solution.py:60
  11.2 14.4 %collective-permute-start.3 = (bf16[2,16,1024]{2,1,0:T(8,128)(2,1)}, bf16[2,16,1024]{2,1,0:T(8,128)(2,1)S(1)}, u32[]{:S(2)}, u32[]{:S(2)}) collective-permute-start(bf16[2,16,1024]{2,1,0:T(8,128)(2,1)} %get-tuple-element.63), channel_id=1, source_target_pairs={{0,16},{2,18},{4,20},{6,22},{8,24},{10,26},{12,28},{14,30},{16,0},... | collective-permute-start | bytes 196616 | tf_op jit(solution)/shard_map/ppermute | solution.py:60
  13.8 51.4 %collective-permute-start.8 = (bf16[1024,1024]{1,0:T(8,128)(2,1)}, bf16[1024,1024]{1,0:T(8,128)(2,1)}, u32[]{:S(2)}, u32[]{:S(2)}) collective-permute-start(bf16[1024,1024]{1,0:T(8,128)(2,1)} %own_ref), channel_id=1, source_target_pairs={{0,1},{1,0},{2,3},{3,2},{4,5},{5,4},{6,7},{7,6},{8,9},{9,8},{10,11... | collective-permute-start | bytes 6291464 | tf_op jit(solution)/shard_map/ppermute | solution.py:623
  23.6 1.3 copy-start.9
  25.6 11.0 %copy-start.21 = (bf16[2,128,1024]{2,1,0:T(8,128)(2,1)S(1)}, bf16[2,128,1024]{2,1,0:T(8,128)(2,1)}, u32[]{:S(2)}) copy-start(bf16[2,128,1024]{2,1,0:T(8,128)(2,1)} %get-tuple-element.60) | copy-start | bytes 1572868
  25.6 5.7 %collective-permute-start.4 = (bf16[2,48,1024]{2,1,0:T(8,128)(2,1)S(1)}, bf16[2,48,1024]{2,1,0:T(8,128)(2,1)S(1)}, u32[]{:S(2)}, u32[]{:S(2)}) collective-permute-start(bf16[2,48,1024]{2,1,0:T(8,128)(2,1)S(1)} %pad_maximum_fusion), channel_id=1, source_target_pairs={{0,4},{2,6},{4,0},{6,2},{8,12},{10,14},{12,8},{14,10},{16,20},{18,... | collective-permute-start | bytes 589832 | tf_op jit(solution)/shard_map/ppermute | solution.py:60
  31.4 5.0 %collective-permute-start.5 = (bf16[2,32,1024]{2,1,0:T(8,128)(2,1)S(1)}, bf16[2,32,1024]{2,1,0:T(8,128)(2,1)S(1)}, u32[]{:S(2)}, u32[]{:S(2)}) collective-permute-start(bf16[2,32,1024]{2,1,0:T(8,128)(2,1)S(1)} %pad_maximum_fusion.2), channel_id=1, source_target_pairs={{0,8},{2,10},{4,12},{6,14},{8,0},{10,2},{12,4},{14,6},{16,24},{18,... | collective-permute-start | bytes 393224 | tf_op jit(solution)/shard_map/ppermute | solution.py:60
  36.5 3.1 %copy-start.14 = (bf16[2,192,1024]{2,1,0:T(8,128)(2,1)}, bf16[2,192,1024]{2,1,0:T(8,128)(2,1)S(1)}, u32[]{:S(2)}) copy-start(bf16[2,192,1024]{2,1,0:T(8,128)(2,1)S(1)} %constant_dynamic-update-slice_fusion.refs_1_) | copy-start | bytes 2359300
  36.5 3.1 %collective-permute-start.6 = (bf16[2,192,1024]{2,1,0:T(8,128)(2,1)S(1)}, bf16[2,192,1024]{2,1,0:T(8,128)(2,1)S(1)}, u32[]{:S(2)}, u32[]{:S(2)}) collective-permute-start(bf16[2,192,1024]{2,1,0:T(8,128)(2,1)S(1)} %constant_dynamic-update-slice_fusion.refs_1_), channel_id=1, source_target_pairs={{0,2},{2,0},{4,6},{6,4},{8,10},{10,8},{12,14},{14,12},{16,18},{18,... | collective-permute-start | bytes 2359304 | tf_op jit(solution)/shard_map/ppermute | solution.py:60
  36.6 3.0 %collective-permute-start = (bf16[2,128,1024]{2,1,0:T(8,128)(2,1)S(1)}, bf16[2,128,1024]{2,1,0:T(8,128)(2,1)S(1)}, u32[]{:S(2)}, u32[]{:S(2)}) collective-permute-start(bf16[2,128,1024]{2,1,0:T(8,128)(2,1)S(1)} %copy-done.21), channel_id=1, source_target_pairs={{0,2},{2,0},{4,6},{6,4},{8,10},{10,8},{12,14},{14,12},{16,18},{18,... | collective-permute-start | bytes 1572872 | tf_op jit(solution)/shard_map/ppermute | solution.py:60
  39.6 1.1 copy-start.15
  51.2 1.6 copy-start
  52.8 5.4 %copy-start.1 = (bf16[1024,1024]{1,0:T(8,128)(2,1)S(1)}, bf16[1024,1024]{1,0:T(8,128)(2,1)}, u32[]{:S(2)}) copy-start(bf16[1024,1024]{1,0:T(8,128)(2,1)} %get-tuple-element.89.mixed_ref) | copy-start | bytes 6291460
  57.7 48.0 %collective-permute-start.10 = (bf16[1024,1024]{1,0:T(8,128)(2,1)}, bf16[1024,1024]{1,0:T(8,128)(2,1)}, u32[]{:S(2)}, u32[]{:S(2)}) collective-permute-start(bf16[1024,1024]{1,0:T(8,128)(2,1)} %project.2), channel_id=1, source_target_pairs={{0,1},{1,0},{2,3},{3,2},{4,5},{5,4},{6,7},{7,6},{8,9},{9,8},{10,11... | collective-permute-start | bytes 6291464 | tf_op jit(solution)/shard_map/ppermute | solution.py:632
  65.2 6.8 %collective-permute-start.7 = (bf16[512,1024]{1,0:T(8,128)(2,1)}, bf16[512,1024]{1,0:T(8,128)(2,1)}, u32[]{:S(2)}, u32[]{:S(2)}) collective-permute-start(bf16[512,1024]{1,0:T(8,128)(2,1)} %get-tuple-element.71), channel_id=1, source_target_pairs={{0,2},{2,0},{4,6},{6,4},{8,10},{10,8},{12,14},{14,12},{16,18},{18,... | collective-permute-start | bytes 3145736 | tf_op jit(solution)/shard_map/ppermute | solution.py:60
  70.4 1.0 copy-start.10
  71.4 3.9 %collective-permute-start.9 = (bf16[512,1024]{1,0:T(8,128)(2,1)S(1)}, bf16[512,1024]{1,0:T(8,128)(2,1)}, u32[]{:S(2)}, u32[]{:S(2)}) collective-permute-start(bf16[512,1024]{1,0:T(8,128)(2,1)S(1)} %get-tuple-element.75), channel_id=1, source_target_pairs={{0,2},{2,0},{4,6},{6,4},{8,10},{10,8},{12,14},{14,12},{16,18},{18,... | collective-permute-start | bytes 3145736 | tf_op jit(solution)/shard_map/ppermute | solution.py:60
  71.9 6.7 %copy-start.7 = (bf16[1024,1024]{1,0:T(8,128)(2,1)S(1)}, bf16[1024,1024]{1,0:T(8,128)(2,1)}, u32[]{:S(2)}) copy-start(bf16[1024,1024]{1,0:T(8,128)(2,1)} %own_ref) | copy-start | bytes 6291460
  74.9 30.8 %collective-permute-start.11 = (bf16[256,1024]{1,0:T(8,128)(2,1)}, bf16[256,1024]{1,0:T(8,128)(2,1)S(1)}, u32[]{:S(2)}, u32[]{:S(2)}) collective-permute-start(bf16[256,1024]{1,0:T(8,128)(2,1)} %get-tuple-element.82), channel_id=1, source_target_pairs={{0,4},{2,6},{4,0},{6,2},{8,12},{10,14},{12,8},{14,10},{16,20},{18,... | collective-permute-start | bytes 1572872 | tf_op jit(solution)/shard_map/ppermute | solution.py:60
  78.1 30.9 %collective-permute-start.12 = (bf16[256,1024]{1,0:T(8,128)(2,1)}, bf16[256,1024]{1,0:T(8,128)(2,1)S(1)}, u32[]{:S(2)}, u32[]{:S(2)}) collective-permute-start(bf16[256,1024]{1,0:T(8,128)(2,1)} %get-tuple-element.85), channel_id=1, source_target_pairs={{0,8},{2,10},{4,12},{6,14},{8,0},{10,2},{12,4},{14,6},{16,24},{18,... | collective-permute-start | bytes 1572872 | tf_op jit(solution)/shard_map/ppermute | solution.py:60
  85.8 1.4 copy-start.6
  100.4 12.0 %collective-permute-start.13 = (bf16[2,192,1024]{2,1,0:T(8,128)(2,1)}, bf16[2,192,1024]{2,1,0:T(8,128)(2,1)S(1)}, u32[]{:S(2)}, u32[]{:S(2)}) collective-permute-start(bf16[2,192,1024]{2,1,0:T(8,128)(2,1)} %get-tuple-element.88), channel_id=1, source_target_pairs={{0,2},{2,0},{4,6},{6,4},{8,10},{10,8},{12,14},{14,12},{16,18},{18,... | collective-permute-start | bytes 2359304 | tf_op jit(solution)/shard_map/ppermute | solution.py:60
  100.5 33.0 %collective-permute-start.18 = (bf16[2,128,1024]{2,1,0:T(8,128)(2,1)}, bf16[2,128,1024]{2,1,0:T(8,128)(2,1)S(1)}, u32[]{:S(2)}, u32[]{:S(2)}) collective-permute-start(bf16[2,128,1024]{2,1,0:T(8,128)(2,1)} %get-tuple-element.98), channel_id=1, source_target_pairs={{0,2},{2,0},{4,6},{6,4},{8,10},{10,8},{12,14},{14,12},{16,18},{18,... | collective-permute-start | bytes 1572872 | tf_op jit(solution)/shard_map/ppermute | solution.py:60
  108.6 14.8 %collective-permute-start.15 = (bf16[128,1024]{1,0:T(8,128)(2,1)}, bf16[128,1024]{1,0:T(8,128)(2,1)S(1)}, u32[]{:S(2)}, u32[]{:S(2)}) collective-permute-start(bf16[128,1024]{1,0:T(8,128)(2,1)} %get-tuple-element.92), channel_id=1, source_target_pairs={{0,8},{2,10},{4,12},{6,14},{8,0},{10,2},{12,4},{14,6},{16,24},{18,... | collective-permute-start | bytes 786440 | tf_op jit(solution)/shard_map/ppermute | solution.py:60
  109.8 2.6 %copy-start.17 = (bf16[2,192,1024]{2,1,0:T(8,128)(2,1)S(1)}, bf16[2,192,1024]{2,1,0:T(8,128)(2,1)}, u32[]{:S(2)}) copy-start(bf16[2,192,1024]{2,1,0:T(8,128)(2,1)} %get-tuple-element.87) | copy-start | bytes 2359300
  112.0 2.4 %copy-start.2 = (bf16[1024,1024]{1,0:T(8,128)(2,1)S(1)}, bf16[1024,1024]{1,0:T(8,128)(2,1)}, u32[]{:S(2)}) copy-start(bf16[1024,1024]{1,0:T(8,128)(2,1)} %get-tuple-element.89.mixed_ref) | copy-start | bytes 6291460
  112.0 21.2 %collective-permute-start.17 = (bf16[128,1024]{1,0:T(8,128)(2,1)}, bf16[128,1024]{1,0:T(8,128)(2,1)S(1)}, u32[]{:S(2)}, u32[]{:S(2)}) collective-permute-start(bf16[128,1024]{1,0:T(8,128)(2,1)} %get-tuple-element.97), channel_id=1, source_target_pairs={{0,16},{2,18},{4,20},{6,22},{8,24},{10,26},{12,28},{14,30},{16,0},... | collective-permute-start | bytes 786440 | tf_op jit(solution)/shard_map/ppermute | solution.py:60
  112.7 10.0 %collective-permute-start.14 = (bf16[2,32,1024]{2,1,0:T(8,128)(2,1)S(1)}, bf16[2,32,1024]{2,1,0:T(8,128)(2,1)S(1)}, u32[]{:S(2)}, u32[]{:S(2)}) collective-permute-start(bf16[2,32,1024]{2,1,0:T(8,128)(2,1)S(1)} %slice.58), channel_id=1, source_target_pairs={{0,8},{2,10},{4,12},{6,14},{8,0},{10,2},{12,4},{14,6},{16,24},{18,... | collective-permute-start | bytes 393224 | tf_op jit(solution)/shard_map/ppermute | solution.py:60
  114.4 9.0 %copy-start.20 = (bf16[128,1024]{1,0:T(8,128)(2,1)S(1)}, bf16[128,1024]{1,0:T(8,128)(2,1)}, u32[]{:S(2)}) copy-start(bf16[128,1024]{1,0:T(8,128)(2,1)} %get-tuple-element.91) | copy-start | bytes 786436
  114.4 19.0 %copy-start.19 = (bf16[128,1024]{1,0:T(8,128)(2,1)S(1)}, bf16[128,1024]{1,0:T(8,128)(2,1)}, u32[]{:S(2)}) copy-start(bf16[128,1024]{1,0:T(8,128)(2,1)} %get-tuple-element.96) | copy-start | bytes 786436
  119.6 24.0 %copy-start.12 = (f32[8,8,1024]{2,1,0:T(8,128)S(1)}, f32[8,8,1024]{2,1,0:T(8,128)}, u32[]{:S(2)}) copy-start(f32[8,8,1024]{2,1,0:T(8,128)} %get-tuple-element.103.inner_ref) | copy-start | bytes 786436
  122.7 20.9 %copy-start.8 = (f32[8,8,1024]{2,1,0:T(8,128)S(1)}, f32[8,8,1024]{2,1,0:T(8,128)}, u32[]{:S(2)}) copy-start(f32[8,8,1024]{2,1,0:T(8,128)} %get-tuple-element.78.lse_ref) | copy-start | bytes 786436
  122.8 20.9 %copy-start.5 = (bf16[1024,1024]{1,0:T(8,128)(2,1)S(1)}, bf16[1024,1024]{1,0:T(8,128)(2,1)}, u32[]{:S(2)}) copy-start(bf16[1024,1024]{1,0:T(8,128)(2,1)} %key_ref.7) | copy-start | bytes 6291460
  122.8 20.9 %copy-start.4 = (bf16[1024,1024]{1,0:T(8,128)(2,1)S(1)}, bf16[1024,1024]{1,0:T(8,128)(2,1)}, u32[]{:S(2)}) copy-start(bf16[1024,1024]{1,0:T(8,128)(2,1)} %query_ref.9) | copy-start | bytes 6291460
  122.8 7.8 %collective-permute-start.16 = (bf16[2,48,1024]{2,1,0:T(8,128)(2,1)S(1)}, bf16[2,48,1024]{2,1,0:T(8,128)(2,1)S(1)}, u32[]{:S(2)}, u32[]{:S(2)}) collective-permute-start(bf16[2,48,1024]{2,1,0:T(8,128)(2,1)S(1)} %pad_maximum_fusion.1), channel_id=1, source_target_pairs={{0,4},{2,6},{4,0},{6,2},{8,12},{10,14},{12,8},{14,10},{16,20},{18,... | collective-permute-start | bytes 589832 | tf_op jit(solution)/shard_map/ppermute | solution.py:60
  123.5 17.3 %collective-permute-start.22 = (bf16[128,1024]{1,0:T(8,128)(2,1)S(1)}, bf16[128,1024]{1,0:T(8,128)(2,1)S(1)}, u32[]{:S(2)}, u32[]{:S(2)}) collective-permute-start(bf16[128,1024]{1,0:T(8,128)(2,1)S(1)} %add_convert_fusion.4), channel_id=1, source_target_pairs={{0,16},{2,18},{4,20},{6,22},{8,24},{10,26},{12,28},{14,30},{16,0},... | collective-permute-start | bytes 786440 | tf_op jit(solution)/shard_map/ppermute | solution.py:60
  125.9 10.4 %collective-permute-start.19 = (bf16[2,64,1024]{2,1,0:T(8,128)(2,1)S(1)}, bf16[2,64,1024]{2,1,0:T(8,128)(2,1)S(1)}, u32[]{:S(2)}, u32[]{:S(2)}) collective-permute-start(bf16[2,64,1024]{2,1,0:T(8,128)(2,1)S(1)} %get-tuple-element.99), channel_id=1, source_target_pairs={{0,4},{2,6},{4,0},{6,2},{8,12},{10,14},{12,8},{14,10},{16,20},{18,... | collective-permute-start | bytes 786440 | tf_op jit(solution)/shard_map/ppermute | solution.py:60
  130.7 9.5 %collective-permute-start.21 = (bf16[2,16,1024]{2,1,0:T(8,128)(2,1)S(1)}, bf16[2,16,1024]{2,1,0:T(8,128)(2,1)S(1)}, u32[]{:S(2)}, u32[]{:S(2)}) collective-permute-start(bf16[2,16,1024]{2,1,0:T(8,128)(2,1)S(1)} %add_convert_fusion.7), channel_id=1, source_target_pairs={{0,16},{2,18},{4,20},{6,22},{8,24},{10,26},{12,28},{14,30},{16,0},... | collective-permute-start | bytes 196616 | tf_op jit(solution)/shard_map/ppermute | solution.py:60
  133.2 7.6 %collective-permute-start.20 = (bf16[2,32,1024]{2,1,0:T(8,128)(2,1)S(1)}, bf16[2,32,1024]{2,1,0:T(8,128)(2,1)S(1)}, u32[]{:S(2)}, u32[]{:S(2)}) collective-permute-start(bf16[2,32,1024]{2,1,0:T(8,128)(2,1)S(1)} %add_convert_fusion.5), channel_id=1, source_target_pairs={{0,8},{2,10},{4,12},{6,14},{8,0},{10,2},{12,4},{14,6},{16,24},{18,... | collective-permute-start | bytes 393224 | tf_op jit(solution)/shard_map/ppermute | solution.py:60
  133.5 7.4 %collective-permute-start.23 = (bf16[128,1024]{1,0:T(8,128)(2,1)S(1)}, bf16[128,1024]{1,0:T(8,128)(2,1)S(1)}, u32[]{:S(2)}, u32[]{:S(2)}) collective-permute-start(bf16[128,1024]{1,0:T(8,128)(2,1)S(1)} %add_convert_fusion.3), channel_id=1, source_target_pairs={{0,4},{2,6},{4,0},{6,2},{8,12},{10,14},{12,8},{14,10},{16,20},{18,... | collective-permute-start | bytes 786440 | tf_op jit(solution)/shard_map/ppermute | solution.py:60
  140.9 14.8 %collective-permute-start.24 = (bf16[128,1024]{1,0:T(8,128)(2,1)S(1)}, bf16[128,1024]{1,0:T(8,128)(2,1)S(1)}, u32[]{:S(2)}, u32[]{:S(2)}) collective-permute-start(bf16[128,1024]{1,0:T(8,128)(2,1)S(1)} %add_convert_fusion.2), channel_id=1, source_target_pairs={{0,8},{2,10},{4,12},{6,14},{8,0},{10,2},{12,4},{14,6},{16,24},{18,... | collective-permute-start | bytes 786440 | tf_op jit(solution)/shard_map/ppermute | solution.py:60
  141.0 16.3 %collective-permute-start.27 = (bf16[128,1024]{1,0:T(8,128)(2,1)S(1)}, bf16[128,1024]{1,0:T(8,128)(2,1)S(1)}, u32[]{:S(2)}, u32[]{:S(2)}) collective-permute-start(bf16[128,1024]{1,0:T(8,128)(2,1)S(1)} %add_convert_fusion.1), channel_id=1, source_target_pairs={{0,16},{2,18},{4,20},{6,22},{8,24},{10,26},{12,28},{14,30},{16,0},... | collective-permute-start | bytes 786440 | tf_op jit(solution)/shard_map/ppermute | solution.py:60
  155.7 14.0 %collective-permute-start.25 = (bf16[256,1024]{1,0:T(8,128)(2,1)S(1)}, bf16[256,1024]{1,0:T(8,128)(2,1)S(1)}, u32[]{:S(2)}, u32[]{:S(2)}) collective-permute-start(bf16[256,1024]{1,0:T(8,128)(2,1)S(1)} %constant_dynamic-update-slice_fusion.5), channel_id=1, source_target_pairs={{0,4},{2,6},{4,0},{6,2},{8,12},{10,14},{12,8},{14,10},{16,20},{18,... | collective-permute-start | bytes 1572872 | tf_op jit(solution)/shard_map/ppermute | solution.py:60
  157.3 12.5 %collective-permute-start.28 = (bf16[256,1024]{1,0:T(8,128)(2,1)S(1)}, bf16[256,1024]{1,0:T(8,128)(2,1)S(1)}, u32[]{:S(2)}, u32[]{:S(2)}) collective-permute-start(bf16[256,1024]{1,0:T(8,128)(2,1)S(1)} %constant_dynamic-update-slice_fusion.9), channel_id=1, source_target_pairs={{0,8},{2,10},{4,12},{6,14},{8,0},{10,2},{12,4},{14,6},{16,24},{18,... | collective-permute-start | bytes 1572872 | tf_op jit(solution)/shard_map/ppermute | solution.py:60
  169.8 2.9 %collective-permute-start.26 = (bf16[512,1024]{1,0:T(8,128)(2,1)S(1)}, bf16[512,1024]{1,0:T(8,128)(2,1)S(1)}, u32[]{:S(2)}, u32[]{:S(2)}) collective-permute-start(bf16[512,1024]{1,0:T(8,128)(2,1)S(1)} %constant_dynamic-update-slice_fusion.7.first_ref), channel_id=1, source_target_pairs={{0,2},{2,0},{4,6},{6,4},{8,10},{10,8},{12,14},{14,12},{16,18},{18,... | collective-permute-start | bytes 3145736 | tf_op jit(solution)/shard_map/ppermute | solution.py:60
  169.9 4.2 %collective-permute-start.29 = (bf16[512,1024]{1,0:T(8,128)(2,1)S(1)}, bf16[512,1024]{1,0:T(8,128)(2,1)}, u32[]{:S(2)}, u32[]{:S(2)}) collective-permute-start(bf16[512,1024]{1,0:T(8,128)(2,1)S(1)} %constant_dynamic-update-slice_fusion.11.second_ref), channel_id=1, source_target_pairs={{0,2},{2,0},{4,6},{6,4},{8,10},{10,8},{12,14},{14,12},{16,18},{18,... | collective-permute-start | bytes 3145736 | tf_op jit(solution)/shard_map/ppermute | solution.py:60
  (5 other events, 4.0 us)

commit v3 on v2

--- a/solution.py
+++ b/solution.py
@@ -84,8 +84,8 @@
     return [slice(start, start + BLOCK) for start in range(0, ref.shape[0], BLOCK)]
 
 
-def step_heads(features):
-    return min(features // HEAD_DIM, 2)
+def step_heads(features, most=2):
+    return min(features // HEAD_DIM, most)
 
 
 def pool_kernel(local, cross, key_ref, value_ref, coarse_ref, *refs):
@@ -197,7 +197,7 @@
 
 def near_forward(queries, key_states, value_states, coarse, local):
     rows, features = queries.shape
-    heads = step_heads(features)
+    heads = step_heads(features, 4)
     width = heads * HEAD_DIM
     return pl.pallas_call(
         functools.partial(near_kernel, local),
@@ -423,6 +423,7 @@
         + ([] if arrived is None else [out]),
         out, jax.ShapeDtypeStruct((rows, features), BF16),
         (mixed, out_weight) if arrived is None else (mixed, out_weight, arrived),
+        limit=WIDE_VMEM,
     )
 
 
@@ -516,7 +517,7 @@
         def copy(index=index, ref=ref):
             size = ref.shape[0] // chunks
             for chunk in range(chunks):
-                start = pl.multiple_of((chunk ^ where_ref[index]) * size, size)
+                start = pl.multiple_of((chunk ^ where_ref[0]) * size, size)
                 out_ref[pl.ds(start, size), :] = ref[chunk * size : (chunk + 1) * size, :]
 
 
@@ -526,7 +527,7 @@
     return index_call(
         functools.partial(place_kernel, chunks), "place", 2, where, (2,),
         [spec, spec] + ([] if held is None else [pl.BlockSpec(memory_space=pl.ANY)]),
-        pl.BlockSpec((half, columns), lambda step, where: (where[2], step ^ where[3])),
+        pl.BlockSpec((half, columns), lambda step, where: (step ^ where[1], where[2])),
         jax.ShapeDtypeStruct((2 * half, 2 * columns), BF16),
         (first, second) if held is None else (first, second, held),
         aliases={} if held is None else {3: 0},
@@ -642,7 +643,7 @@
     first_halves = weight_halves(mixed, first, seq_bit(0))
     first_sum = Chain(sum_rows(*first_halves, first_bits, 1), 2 * cross - 2)
     second_halves = weight_halves(mixed, tie(second, *first_halves), seq_bit(0))
-    second_sum = Chain(sum_rows(*second_halves, second_bits, 400), 2 * cross - 2)
+    second_sum = Chain(sum_rows(*second_halves, second_bits, 200), 2 * cross - 2)
     first_sum.advance()
     second_sum.advance()
     if groups == 2:
@@ -650,10 +651,10 @@
         grad_mixed = mix_back(ready, other, out_weight, group[None])
     *grad_far, far_query, inner = far_backward(queries, far, mixed, grad_mixed, lse)
     far_sum = Chain(scatter_far(*grad_far, cross), cross - 1)
-    arrivals = (inner, shared) if groups == 2 else (inner,)
-    first_sum.advance(*arrivals)
-    second_sum.advance(*arrivals)
-    far_sum.advance(first_sum.kept, second_sum.kept)
+    first_sum.advance(inner)
+    second_sum.advance(inner)
+    arrivals = (shared,) if groups == 2 else ()
+    far_sum.advance(first_sum.kept, second_sum.kept, *arrivals)
     if groups == 2:
         attended = project(tie(mixed, far_sum.kept), out_weight, group[None], shared)
     far_sum.advance(*([attended] if groups == 2 else []))
@@ -679,15 +680,15 @@
     for chain in (first_sum, second_sum):
         while chain.left:
             chain.advance()
-    spots = [chunk_index(first_bits), chunk_index(second_bits)]
+    core = seq_bit(0)
     flip = jnp.asarray(flip, jnp.int32)
     chunks = 1 << (cross - 2)
-    (first_mine, first_other), (second_mine, second_other) = first_sum.moving, second_sum.moving
     grad_weight = place(
-        first_mine, second_mine, chunks, jnp.stack([*spots, seq_bit(0), flip])
+        *first_sum.moving, chunks, jnp.stack([chunk_index(first_bits), core, flip])
     )
     grad_weight = place(
-        first_other, second_other, chunks, jnp.stack([*spots, 1 - seq_bit(0), flip]), grad_weight
+        *second_sum.moving, chunks, jnp.stack([chunk_index(second_bits), core, 1 - flip]),
+        grad_weight,
     )
     return attended, grad_queries, grad_keys, grad_values, grad_weight
 

time: 178 us -> 176 us (0.989)
    ppermute x1, waiting for transfers between devices: 4.68 us -> 0.01 us  [solution_body(): shared = lax.ppermute(share, 'head', swap)]
    ppermute x28, waiting for transfers between devices: 26.8 us -> 29.9 us  [from_partner(): lax.ppermute(block, 'seq', [(low, low ^ 1 << bit) for low in range(count)])]
    unnamed x54 -> x50, local copies, waits for them, and re-layouts: 9.77 us -> 8.29 us
  transfers between devices with their start and end apart: 30 -> 30, of which waited for: 11 -> 9; matrix products, arithmetic and copies ran while one was open for 1% -> 1% of each run, Pallas kernels for 55% -> 56%
where the time goes in v3:
time: 176 us
  Pallas kernels  107 us (61%)
  waiting for transfers between devices  29.9 us (17%)
  starting transfers between devices  28.3 us (16%)
  local copies, waits for them, and re-layouts  8.5 us (5%)
    pallas_call x11, Pallas kernels, index_call(): pl.pallas_call(kernel, grid_spec=pltpu.PrefetchScalarGridSpec(num_scalar_...  45 us
    ppermute x28, waiting for transfers between devices, from_partner(): lax.ppermute(block, 'seq', [(low, low ^ 1 << bit) for low in range(count)])  29.9 us
    ppermute x28, starting transfers between devices, from_partner(): lax.ppermute(block, 'seq', [(low, low ^ 1 << bit) for low in range(count)])  26.3 us
    pallas_call x2, Pallas kernels, near_backward(): pl.pallas_call(functools.partial(near_back_kernel, local, len(pooled)), g...  24.2 us
    pallas_call x1, Pallas kernels, far_backward(): pl.pallas_call(functools.partial(far_back_kernel, len(far)), grid=(featur...  13.3 us
    pallas_call x1, Pallas kernels, far_forward(): pl.pallas_call(functools.partial(far_kernel, len(far)), grid=(features //...  10.5 us
    unnamed x50, local copies, waits for them, and re-layouts  8.29 us
    pallas_call x1, Pallas kernels, near_forward(): pl.pallas_call(functools.partial(near_kernel, local), grid=(features // w...  7.82 us
  transfers between devices with their start and end apart: 30, of which 9 were waited for; matrix products, arithmetic and copies ran while one was open for 1% of the time, Pallas kernels for 56%

profile of v3, /device:TPU:0, one launch (start us, length us, event | category | flops | bytes accessed | tf_op | source)
XLA Modules:
  0.0 175.6 jit_solution(17220139322400031044)
XLA Ops:
  0.6 6.0 %pool.1 = (bf16[2,768,1024]{2,1,0:T(8,128)(2,1)}, bf16[2,128,1024]{2,1,0:T(8,128)(2,1)}, bf16[2,64,1024]{2,1,0:T(8,128)(2,1)}, bf16[2,32,1024]{2,1,0:T(8,128)(2,1)}, bf16[2,16,1024]{2,1,0:T(8,128)(2,1)}) custom-call(bf16[1024,1024]{1,0:T(8,128)(2,1)} %key_ref.7, bf16[1024,1024]{1,0:T(8,128)(2,1)} %value_ref.7), custom_call_target="tpu_custom_call" | custom-call | flops 287500000 | bytes 900000 | tf_op jit(solution)/shard_map/pool/pallas_call | solution.py:118
  6.6 3.0 %collective-permute-start.1 = (bf16[2,64,1024]{2,1,0:T(8,128)(2,1)}, bf16[2,64,1024]{2,1,0:T(8,128)(2,1)S(1)}, u32[]{:S(2)}, u32[]{:S(2)}) collective-permute-start(bf16[2,64,1024]{2,1,0:T(8,128)(2,1)} %get-tuple-element.61), channel_id=1, source_target_pairs={{0,4},{2,6},{4,0},{6,2},{8,12},{10,14},{12,8},{14,10},{16,20},{18,... | collective-permute-start | bytes 786440 | tf_op jit(solution)/shard_map/ppermute | solution.py:60
  9.6 1.6 collective-permute-start.2
  11.2 2.6 %collective-permute-start.3 = (bf16[2,16,1024]{2,1,0:T(8,128)(2,1)}, bf16[2,16,1024]{2,1,0:T(8,128)(2,1)S(1)}, u32[]{:S(2)}, u32[]{:S(2)}) collective-permute-start(bf16[2,16,1024]{2,1,0:T(8,128)(2,1)} %get-tuple-element.63), channel_id=1, source_target_pairs={{0,16},{2,18},{4,20},{6,22},{8,24},{10,26},{12,28},{14,30},{16,0},... | collective-permute-start | bytes 196616 | tf_op jit(solution)/shard_map/ppermute | solution.py:60
  13.8 1.5 collective-permute-start.8
  15.3 7.8 %near_forward.1 = (bf16[1024,1024]{1,0:T(8,128)(2,1)S(1)}, f32[8,8,1024]{2,1,0:T(8,128)S(1)}) custom-call(bf16[1024,1024]{1,0:T(8,128)(2,1)S(1)} %copy-done.1, bf16[1024,1024]{1,0:T(8,128)(2,1)} %key_ref.7, bf16[1024,1024]{1,0:T(8,128)(2,1)} %value_ref.7, bf16[2,768,1024]{2,1,0:T(8,128)(2,1)} %get-tuple-element.64.coarse_ref), custom_call_target="tpu_custom_call" | custom-call | flops 517500000 | bytes 1620000 | tf_op jit(solution)/shard_map/near_forward/pallas_call | solution.py:202
  23.1 1.3 copy-done.7
  24.5 0.7 copy-done.11
  25.2 0.6 collective-permute-start.4
  25.8 5.1 %collective-permute-done.4 = bf16[2,48,1024]{2,1,0:T(8,128)(2,1)S(1)} collective-permute-done((bf16[2,48,1024]{2,1,0:T(8,128)(2,1)S(1)}, bf16[2,48,1024]{2,1,0:T(8,128)(2,1)S(1)}, u32[]{:S(2)}, u32[]{:S(2)}) %collective-permute-start.4) | collective-permute-done | bytes 196640 | tf_op jit(solution)/shard_map/ppermute | solution.py:60
  31.5 4.5 %collective-permute-done.5 = bf16[2,32,1024]{2,1,0:T(8,128)(2,1)S(1)} collective-permute-done((bf16[2,32,1024]{2,1,0:T(8,128)(2,1)S(1)}, bf16[2,32,1024]{2,1,0:T(8,128)(2,1)S(1)}, u32[]{:S(2)}, u32[]{:S(2)}) %collective-permute-start.5) | collective-permute-done | bytes 131104 | tf_op jit(solution)/shard_map/ppermute | solution.py:60
  36.6 2.5 %collective-permute-done.refs_0_ = bf16[2,128,1024]{2,1,0:T(8,128)(2,1)S(1)} collective-permute-done((bf16[2,128,1024]{2,1,0:T(8,128)(2,1)S(1)}, bf16[2,128,1024]{2,1,0:T(8,128)(2,1)S(1)}, u32[]{:S(2)}, u32[]{:S(2)}) %collective-permute-start) | collective-permute-done | bytes 524320 | tf_op jit(solution)/shard_map/ppermute | solution.py:60
  39.2 0.8 copy-done.14
  40.2 10.5 %far_forward.1 = (bf16[1024,1024]{1,0:T(8,128)(2,1)}, f32[8,8,1024]{2,1,0:T(8,128)}) custom-call(bf16[1024,1024]{1,0:T(8,128)(2,1)} %query_ref.9, bf16[2,128,1024]{2,1,0:T(8,128)(2,1)} %copy-done.14, bf16[2,192,1024]{2,1,0:T(8,128)(2,1)} %copy-done.12, bf16[2,192,1024]{2,1,0:T(8,128)(2,1)} %copy-done.13, bf16[1024,1024]{1,0:T(8,128)(2,1)} %copy-done.7, ...), custom_call_target="tpu_custom_call" | custom-call | flops 575000000 | bytes 1800000 | tf_op jit(solution)/shard_map/far_forward/pallas_call | solution.py:221
  50.8 5.6 %project.2 = bf16[1024,1024]{1,0:T(8,128)(2,1)} custom-call(s32[1]{0:T(128)} %bitcast.3.which_ref, bf16[1024,1024]{1,0:T(8,128)(2,1)} %get-tuple-element.89.mixed_ref, bf16[1024,2048]{1,0:T(8,128)(2,1)} %weight_ref.3), custom_call_target="tpu_custom_call" | custom-call | flops 287500000 | bytes 900000 | tf_op jit(solution)/shard_map/project/pallas_call | solution.py:392
  56.3 0.5 collective-permute-start.12
  56.9 6.0 %weight_halves.2 = (bf16[512,1024]{1,0:T(8,128)(2,1)S(1)}, bf16[512,1024]{1,0:T(8,128)(2,1)}) custom-call(s32[1]{0:T(128)} %bitcast.2.which_ref, bf16[1024,1024]{1,0:T(8,128)(2,1)S(1)} %copy-done, bf16[1024,1024]{1,0:T(8,128)(2,1)} %own_ref), custom_call_target="tpu_custom_call" | custom-call | flops 230000000 | bytes 720000 | tf_op jit(solution)/shard_map/weight_halves/pallas_call | solution.py:392
  62.9 1.0 copy-done.9
  63.9 5.2 %weight_halves.3 = (bf16[512,1024]{1,0:T(8,128)(2,1)S(1)}, bf16[512,1024]{1,0:T(8,128)(2,1)S(1)}) custom-call(s32[1]{0:T(128)} %bitcast.2.which_ref, bf16[1024,1024]{1,0:T(8,128)(2,1)S(1)} %copy-done, bf16[1024,1024]{1,0:T(8,128)(2,1)} %collective-permute-done.8.grad_ref.other_ref), custom_call_target="tpu_custom_call" | custom-call | flops 230000000 | bytes 720000 | tf_op jit(solution)/shard_map/weight_halves/pallas_call | solution.py:392
  69.2 1.0 copy-done.8
  70.6 2.9 %add_halves.4 = (bf16[256,1024]{1,0:T(8,128)(2,1)}, bf16[256,1024]{1,0:T(8,128)(2,1)}) custom-call(s32[1]{0:T(128)} %bitcast.1.which_ref, bf16[512,1024]{1,0:T(8,128)(2,1)} %copy-done.9, bf16[512,1024]{1,0:T(8,128)(2,1)} %collective-permute-done.7.second_ref), custom_call_target="tpu_custom_call" | custom-call | flops 28750000 | bytes 90000 | tf_op jit(solution)/shard_map/add_halves/pallas_call | solution.py:392
  74.1 2.7 %add_halves.5 = (bf16[256,1024]{1,0:T(8,128)(2,1)}, bf16[256,1024]{1,0:T(8,128)(2,1)}) custom-call(s32[1]{0:T(128)} %bitcast.4.which_ref, bf16[512,1024]{1,0:T(8,128)(2,1)} %copy-done.8, bf16[512,1024]{1,0:T(8,128)(2,1)} %collective-permute-done.9.second_ref), custom_call_target="tpu_custom_call" | custom-call | flops 28750000 | bytes 90000 | tf_op jit(solution)/shard_map/add_halves/pallas_call | solution.py:392
  77.3 7.2 %mix_back.1.grad_ref = bf16[1024,1024]{1,0:T(8,128)(2,1)S(1)} custom-call(s32[1]{0:T(128)} %bitcast.which_ref, bf16[1024,1024]{1,0:T(8,128)(2,1)S(1)} %copy-done.5, bf16[1024,1024]{1,0:T(8,128)(2,1)} %collective-permute-done.8.grad_ref.other_ref, bf16[1024,2048]{1,0:T(8,128)(2,1)} %weight_ref.3, bf16[1024,2048]{1,0:T(8,128)(2,1)} %weight_ref.3), custom_call_target="tpu_custom_call" | custom-call | flops 460000000 | bytes 1440000 | tf_op jit(solution)/shard_map/mix_back/pallas_call | solution.py:392
  84.4 1.4 copy-done.4
  85.8 13.3 %far_backward.1 = (bf16[2,128,1024]{2,1,0:T(8,128)(2,1)}, bf16[2,192,1024]{2,1,0:T(8,128)(2,1)}, bf16[2,192,1024]{2,1,0:T(8,128)(2,1)}, bf16[1024,1024]{1,0:T(8,128)(2,1)}, f32[8,8,1024]{2,1,0:T(8,128)}) custom-call(bf16[1024,1024]{1,0:T(8,128)(2,1)} %query_ref.9, bf16[1024,1024]{1,0:T(8,128)(2,1)} %get-tuple-element.89.mixed_ref, ...), custom_call_target="tpu_custom_call" | custom-call | flops 805000000 | bytes 2520000 | tf_op jit(solution)/shard_map/far_backward/pallas_call | solution.py:283
  99.2 0.8 copy-done.16
  100.0 2.1 %add_halves.6 = (bf16[128,1024]{1,0:T(8,128)(2,1)}, bf16[128,1024]{1,0:T(8,128)(2,1)}) custom-call(s32[1]{0:T(128)} %bitcast.4.which_ref, bf16[256,1024]{1,0:T(8,128)(2,1)} %get-tuple-element.81.first_ref, bf16[256,1024]{1,0:T(8,128)(2,1)} %copy-done.16), custom_call_target="tpu_custom_call" | custom-call | flops 14375000 | bytes 45000 | tf_op jit(solution)/shard_map/add_halves/pallas_call | solution.py:392
  102.1 1.6 collective-permute-start.15
  103.9 0.8 copy-done.20
  104.8 2.2 %add_halves.7 = (bf16[128,1024]{1,0:T(8,128)(2,1)}, bf16[128,1024]{1,0:T(8,128)(2,1)}) custom-call(s32[1]{0:T(128)} %bitcast.5.which_ref, bf16[256,1024]{1,0:T(8,128)(2,1)} %get-tuple-element.84.first_ref, bf16[256,1024]{1,0:T(8,128)(2,1)} %copy-done.20), custom_call_target="tpu_custom_call" | custom-call | flops 2875000064 | bytes 9000000 | tf_op jit(solution)/shard_map/add_halves/pallas_call | solution.py:392
  108.1 5.9 %project.3 = bf16[1024,1024]{1,0:T(8,128)(2,1)} custom-call(s32[1]{0:T(128)} %bitcast.which_ref, bf16[1024,1024]{1,0:T(8,128)(2,1)} %get-tuple-element.89.mixed_ref, bf16[1024,2048]{1,0:T(8,128)(2,1)} %weight_ref.3, bf16[1024,1024]{1,0:T(8,128)(2,1)} %collective-permute-done.12.refs_0_), custom_call_target="tpu_custom_call" | custom-call | flops 287500000 | bytes 900000 | tf_op jit(solution)/shard_map/project/pallas_call | solution.py:392
  114.0 4.6 %collective-permute-done.14 = bf16[2,32,1024]{2,1,0:T(8,128)(2,1)S(1)} collective-permute-done((bf16[2,32,1024]{2,1,0:T(8,128)(2,1)S(1)}, bf16[2,32,1024]{2,1,0:T(8,128)(2,1)S(1)}, u32[]{:S(2)}, u32[]{:S(2)}) %collective-permute-start.14) | collective-permute-done | bytes 131104 | tf_op jit(solution)/shard_map/ppermute | solution.py:60
  118.7 1.6 collective-permute-start.16
  120.4 1.4 collective-permute-start.22
  122.3 4.3 %collective-permute-done.16 = bf16[2,48,1024]{2,1,0:T(8,128)(2,1)S(1)} collective-permute-done((bf16[2,48,1024]{2,1,0:T(8,128)(2,1)S(1)}, bf16[2,48,1024]{2,1,0:T(8,128)(2,1)S(1)}, u32[]{:S(2)}, u32[]{:S(2)}) %collective-permute-start.16) | collective-permute-done | bytes 196640 | tf_op jit(solution)/shard_map/ppermute | solution.py:60
  126.6 1.2 collective-permute-start.21
  127.8 1.5 collective-permute-start.20
  129.4 1.6 collective-permute-start.23
  131.0 1.2 collective-permute-done.19.refs_1_
  132.2 5.3 %collective-permute-done.21.refs_3_ = bf16[2,16,1024]{2,1,0:T(8,128)(2,1)S(1)} collective-permute-done((bf16[2,16,1024]{2,1,0:T(8,128)(2,1)S(1)}, bf16[2,16,1024]{2,1,0:T(8,128)(2,1)S(1)}, u32[]{:S(2)}, u32[]{:S(2)}) %collective-permute-start.21) | collective-permute-done | bytes 65568 | tf_op jit(solution)/shard_map/ppermute | solution.py:60
  138.0 4.0 %collective-permute-start.24 = (bf16[128,1024]{1,0:T(8,128)(2,1)S(1)}, bf16[128,1024]{1,0:T(8,128)(2,1)S(1)}, u32[]{:S(2)}, u32[]{:S(2)}) collective-permute-start(bf16[128,1024]{1,0:T(8,128)(2,1)S(1)} %add_convert_fusion.1), channel_id=1, source_target_pairs={{0,16},{2,18},{4,20},{6,22},{8,24},{10,26},{12,28},{14,30},{16,0},... | collective-permute-start | bytes 786440 | tf_op jit(solution)/shard_map/ppermute | solution.py:60
  142.0 12.0 %near_backward.2 = (bf16[1024,1024]{1,0:T(8,128)(2,1)}, bf16[1024,1024]{1,0:T(8,128)(2,1)}, bf16[1024,1024]{1,0:T(8,128)(2,1)}) custom-call(bf16[1024,1024]{1,0:T(8,128)(2,1)S(1)} %copy-done.2, bf16[1024,1024]{1,0:T(8,128)(2,1)S(1)} %copy-done.3, bf16[1024,1024]{1,0:T(8,128)(2,1)} %value_ref.7, bf16[2,768,1024]{2,1,0:T(8,128)(2,1)} %get-tuple-element.64.coarse_ref, ...), custom_call_target="tpu_custom_call" | custom-call | flops 517500000 | bytes 1620000 | tf_op jit(solution)/shard_map/near_backward/pallas_call | solution.py:373
  154.1 1.0 collective-permute-start.28
  155.2 12.2 %near_backward.3 = (bf16[1024,1024]{1,0:T(8,128)(2,1)}, bf16[1024,1024]{1,0:T(8,128)(2,1)}, bf16[1024,1024]{1,0:T(8,128)(2,1)}) custom-call(bf16[1024,1024]{1,0:T(8,128)(2,1)S(1)} %copy-done.2, bf16[1024,1024]{1,0:T(8,128)(2,1)S(1)} %copy-done.3, bf16[1024,1024]{1,0:T(8,128)(2,1)} %value_ref.7, ...), custom_call_target="tpu_custom_call", output_to_operand_aliasing={{0}: (12, {}), {1}: (13, {}), {2}: (14, {})} | custom-call | flops 517500000 | bytes 1620000 | tf_op jit(solution)/shard_map/near_backward/pallas_call | solution.py:373
  167.6 0.5 collective-permute-start.26
  168.4 2.1 %collective-permute-done.29.second_ref = bf16[512,1024]{1,0:T(8,128)(2,1)S(1)} collective-permute-done((bf16[512,1024]{1,0:T(8,128)(2,1)S(1)}, bf16[512,1024]{1,0:T(8,128)(2,1)S(1)}, u32[]{:S(2)}, u32[]{:S(2)}) %collective-permute-start.29) | collective-permute-done | bytes 1048608 | tf_op jit(solution)/shard_map/ppermute | solution.py:60
  170.4 2.0 %place.2.refs_0_ = bf16[1024,2048]{1,0:T(8,128)(2,1)} custom-call(s32[3]{0:T(128)S(1)} %pad_add_fusion.1.where_ref, bf16[512,1024]{1,0:T(8,128)(2,1)S(1)} %constant_dynamic-update-slice_fusion.11.first_ref, bf16[512,1024]{1,0:T(8,128)(2,1)S(1)} %collective-permute-done.29.second_ref), custom_call_target="tpu_custom_call" | custom-call | flops 57500000 | bytes 180000 | tf_op jit(solution)/shard_map/place/pallas_call | solution.py:392
  172.4 3.2 %place.3 = bf16[1024,2048]{1,0:T(8,128)(2,1)} custom-call(s32[3]{0:T(128)S(1)} %pad_add_fusion.where_ref, bf16[512,1024]{1,0:T(8,128)(2,1)S(1)} %constant_dynamic-update-slice_fusion.7.first_ref, bf16[512,1024]{1,0:T(8,128)(2,1)} %collective-permute-done.26.second_ref, bf16[1024,2048]{1,0:T(8,128)(2,1)} %place.2.refs_0_), custom_call_target="tpu_custom_call", output_to_operand_aliasing={{}: (3, {})} | custom-call | flops 57500000 | bytes 180000 | tf_op jit(solution)/shard_map/place/pallas_call | solution.py:392
  (102 shorter events, 6.1 us)
Async XLA Ops:
  0.6 14.7 %copy-start.1 = (bf16[1024,1024]{1,0:T(8,128)(2,1)S(1)}, bf16[1024,1024]{1,0:T(8,128)(2,1)}, u32[]{:S(2)}) copy-start(bf16[1024,1024]{1,0:T(8,128)(2,1)} %query_ref.9) | copy-start | bytes 6291460
  6.6 19.1 %collective-permute-start.1 = (bf16[2,64,1024]{2,1,0:T(8,128)(2,1)}, bf16[2,64,1024]{2,1,0:T(8,128)(2,1)S(1)}, u32[]{:S(2)}, u32[]{:S(2)}) collective-permute-start(bf16[2,64,1024]{2,1,0:T(8,128)(2,1)} %get-tuple-element.61), channel_id=1, source_target_pairs={{0,4},{2,6},{4,0},{6,2},{8,12},{10,14},{12,8},{14,10},{16,20},{18,... | collective-permute-start | bytes 786440 | tf_op jit(solution)/shard_map/ppermute | solution.py:60
  9.6 15.5 %collective-permute-start.2 = (bf16[2,32,1024]{2,1,0:T(8,128)(2,1)}, bf16[2,32,1024]{2,1,0:T(8,128)(2,1)S(1)}, u32[]{:S(2)}, u32[]{:S(2)}) collective-permute-start(bf16[2,32,1024]{2,1,0:T(8,128)(2,1)} %get-tuple-element.62), channel_id=1, source_target_pairs={{0,8},{2,10},{4,12},{6,14},{8,0},{10,2},{12,4},{14,6},{16,24},{18,... | collective-permute-start | bytes 393224 | tf_op jit(solution)/shard_map/ppermute | solution.py:60
  11.2 13.9 %collective-permute-start.3 = (bf16[2,16,1024]{2,1,0:T(8,128)(2,1)}, bf16[2,16,1024]{2,1,0:T(8,128)(2,1)S(1)}, u32[]{:S(2)}, u32[]{:S(2)}) collective-permute-start(bf16[2,16,1024]{2,1,0:T(8,128)(2,1)} %get-tuple-element.63), channel_id=1, source_target_pairs={{0,16},{2,18},{4,20},{6,22},{8,24},{10,26},{12,28},{14,30},{16,0},... | collective-permute-start | bytes 196616 | tf_op jit(solution)/shard_map/ppermute | solution.py:60
  13.8 50.1 %collective-permute-start.8 = (bf16[1024,1024]{1,0:T(8,128)(2,1)}, bf16[1024,1024]{1,0:T(8,128)(2,1)}, u32[]{:S(2)}, u32[]{:S(2)}) collective-permute-start(bf16[1024,1024]{1,0:T(8,128)(2,1)} %own_ref), channel_id=1, source_target_pairs={{0,1},{1,0},{2,3},{3,2},{4,5},{5,4},{6,7},{7,6},{8,9},{9,8},{10,11... | collective-permute-start | bytes 6291464 | tf_op jit(solution)/shard_map/ppermute | solution.py:624
  23.1 1.3 copy-start.7
  25.2 11.0 %copy-start.19 = (bf16[2,128,1024]{2,1,0:T(8,128)(2,1)S(1)}, bf16[2,128,1024]{2,1,0:T(8,128)(2,1)}, u32[]{:S(2)}) copy-start(bf16[2,128,1024]{2,1,0:T(8,128)(2,1)} %get-tuple-element.60) | copy-start | bytes 1572868
  25.2 5.7 %collective-permute-start.4 = (bf16[2,48,1024]{2,1,0:T(8,128)(2,1)S(1)}, bf16[2,48,1024]{2,1,0:T(8,128)(2,1)S(1)}, u32[]{:S(2)}, u32[]{:S(2)}) collective-permute-start(bf16[2,48,1024]{2,1,0:T(8,128)(2,1)S(1)} %pad_maximum_fusion), channel_id=1, source_target_pairs={{0,4},{2,6},{4,0},{6,2},{8,12},{10,14},{12,8},{14,10},{16,20},{18,... | collective-permute-start | bytes 589832 | tf_op jit(solution)/shard_map/ppermute | solution.py:60
  31.0 5.0 %collective-permute-start.5 = (bf16[2,32,1024]{2,1,0:T(8,128)(2,1)S(1)}, bf16[2,32,1024]{2,1,0:T(8,128)(2,1)S(1)}, u32[]{:S(2)}, u32[]{:S(2)}) collective-permute-start(bf16[2,32,1024]{2,1,0:T(8,128)(2,1)S(1)} %pad_maximum_fusion.2), channel_id=1, source_target_pairs={{0,8},{2,10},{4,12},{6,14},{8,0},{10,2},{12,4},{14,6},{16,24},{18,... | collective-permute-start | bytes 393224 | tf_op jit(solution)/shard_map/ppermute | solution.py:60
  36.0 3.1 %copy-start.12 = (bf16[2,192,1024]{2,1,0:T(8,128)(2,1)}, bf16[2,192,1024]{2,1,0:T(8,128)(2,1)S(1)}, u32[]{:S(2)}) copy-start(bf16[2,192,1024]{2,1,0:T(8,128)(2,1)S(1)} %constant_dynamic-update-slice_fusion.refs_1_) | copy-start | bytes 2359300
  36.0 3.1 %collective-permute-start.6 = (bf16[2,192,1024]{2,1,0:T(8,128)(2,1)S(1)}, bf16[2,192,1024]{2,1,0:T(8,128)(2,1)S(1)}, u32[]{:S(2)}, u32[]{:S(2)}) collective-permute-start(bf16[2,192,1024]{2,1,0:T(8,128)(2,1)S(1)} %constant_dynamic-update-slice_fusion.refs_1_), channel_id=1, source_target_pairs={{0,2},{2,0},{4,6},{6,4},{8,10},{10,8},{12,14},{14,12},{16,18},{18,... | collective-permute-start | bytes 2359304 | tf_op jit(solution)/shard_map/ppermute | solution.py:60
  36.1 3.0 %collective-permute-start = (bf16[2,128,1024]{2,1,0:T(8,128)(2,1)S(1)}, bf16[2,128,1024]{2,1,0:T(8,128)(2,1)S(1)}, u32[]{:S(2)}, u32[]{:S(2)}) collective-permute-start(bf16[2,128,1024]{2,1,0:T(8,128)(2,1)S(1)} %copy-done.19), channel_id=1, source_target_pairs={{0,2},{2,0},{4,6},{6,4},{8,10},{10,8},{12,14},{14,12},{16,18},{18,... | collective-permute-start | bytes 1572872 | tf_op jit(solution)/shard_map/ppermute | solution.py:60
  39.2 1.1 copy-start.13
  50.8 6.1 %copy-start = (bf16[1024,1024]{1,0:T(8,128)(2,1)S(1)}, bf16[1024,1024]{1,0:T(8,128)(2,1)}, u32[]{:S(2)}) copy-start(bf16[1024,1024]{1,0:T(8,128)(2,1)} %get-tuple-element.89.mixed_ref) | copy-start | bytes 6291460
  56.3 50.7 %collective-permute-start.12 = (bf16[1024,1024]{1,0:T(8,128)(2,1)}, bf16[1024,1024]{1,0:T(8,128)(2,1)}, u32[]{:S(2)}, u32[]{:S(2)}) collective-permute-start(bf16[1024,1024]{1,0:T(8,128)(2,1)} %project.2), channel_id=1, source_target_pairs={{0,1},{1,0},{2,3},{3,2},{4,5},{5,4},{6,7},{7,6},{8,9},{9,8},{10,11... | collective-permute-start | bytes 6291464 | tf_op jit(solution)/shard_map/ppermute | solution.py:633
  62.9 1.0 copy-start.9
  63.9 6.8 %collective-permute-start.7 = (bf16[512,1024]{1,0:T(8,128)(2,1)}, bf16[512,1024]{1,0:T(8,128)(2,1)}, u32[]{:S(2)}, u32[]{:S(2)}) collective-permute-start(bf16[512,1024]{1,0:T(8,128)(2,1)} %get-tuple-element.71), channel_id=1, source_target_pairs={{0,2},{2,0},{4,6},{6,4},{8,10},{10,8},{12,14},{14,12},{16,18},{18,... | collective-permute-start | bytes 3145736 | tf_op jit(solution)/shard_map/ppermute | solution.py:60
  69.1 1.0 copy-start.8
  70.1 4.0 %collective-permute-start.9 = (bf16[512,1024]{1,0:T(8,128)(2,1)S(1)}, bf16[512,1024]{1,0:T(8,128)(2,1)}, u32[]{:S(2)}, u32[]{:S(2)}) collective-permute-start(bf16[512,1024]{1,0:T(8,128)(2,1)S(1)} %get-tuple-element.75), channel_id=1, source_target_pairs={{0,2},{2,0},{4,6},{6,4},{8,10},{10,8},{12,14},{14,12},{16,18},{18,... | collective-permute-start | bytes 3145736 | tf_op jit(solution)/shard_map/ppermute | solution.py:60
  70.6 6.6 %copy-start.5 = (bf16[1024,1024]{1,0:T(8,128)(2,1)S(1)}, bf16[1024,1024]{1,0:T(8,128)(2,1)}, u32[]{:S(2)}) copy-start(bf16[1024,1024]{1,0:T(8,128)(2,1)} %own_ref) | copy-start | bytes 6291460
  73.6 25.6 %collective-permute-start.10 = (bf16[256,1024]{1,0:T(8,128)(2,1)}, bf16[256,1024]{1,0:T(8,128)(2,1)S(1)}, u32[]{:S(2)}, u32[]{:S(2)}) collective-permute-start(bf16[256,1024]{1,0:T(8,128)(2,1)} %get-tuple-element.82), channel_id=1, source_target_pairs={{0,4},{2,6},{4,0},{6,2},{8,12},{10,14},{12,8},{14,10},{16,20},{18,... | collective-permute-start | bytes 1572872 | tf_op jit(solution)/shard_map/ppermute | solution.py:60
  76.8 27.1 %collective-permute-start.11 = (bf16[256,1024]{1,0:T(8,128)(2,1)}, bf16[256,1024]{1,0:T(8,128)(2,1)S(1)}, u32[]{:S(2)}, u32[]{:S(2)}) collective-permute-start(bf16[256,1024]{1,0:T(8,128)(2,1)} %get-tuple-element.85), channel_id=1, source_target_pairs={{0,8},{2,10},{4,12},{6,14},{8,0},{10,2},{12,4},{14,6},{16,24},{18,... | collective-permute-start | bytes 1572872 | tf_op jit(solution)/shard_map/ppermute | solution.py:60
  84.4 1.4 copy-start.4
  99.1 8.3 %collective-permute-start.13 = (bf16[2,192,1024]{2,1,0:T(8,128)(2,1)}, bf16[2,192,1024]{2,1,0:T(8,128)(2,1)S(1)}, u32[]{:S(2)}, u32[]{:S(2)}) collective-permute-start(bf16[2,192,1024]{2,1,0:T(8,128)(2,1)} %get-tuple-element.88), channel_id=1, source_target_pairs={{0,2},{2,0},{4,6},{6,4},{8,10},{10,8},{12,14},{14,12},{16,18},{18,... | collective-permute-start | bytes 2359304 | tf_op jit(solution)/shard_map/ppermute | solution.py:60
  99.2 0.8 copy-start.16
  102.1 18.2 %collective-permute-start.15 = (bf16[128,1024]{1,0:T(8,128)(2,1)}, bf16[128,1024]{1,0:T(8,128)(2,1)S(1)}, u32[]{:S(2)}, u32[]{:S(2)}) collective-permute-start(bf16[128,1024]{1,0:T(8,128)(2,1)} %get-tuple-element.92), channel_id=1, source_target_pairs={{0,8},{2,10},{4,12},{6,14},{8,0},{10,2},{12,4},{14,6},{16,24},{18,... | collective-permute-start | bytes 786440 | tf_op jit(solution)/shard_map/ppermute | solution.py:60
  103.7 25.6 %collective-permute-start.18 = (bf16[2,128,1024]{2,1,0:T(8,128)(2,1)}, bf16[2,128,1024]{2,1,0:T(8,128)(2,1)S(1)}, u32[]{:S(2)}, u32[]{:S(2)}) collective-permute-start(bf16[2,128,1024]{2,1,0:T(8,128)(2,1)} %get-tuple-element.98), channel_id=1, source_target_pairs={{0,2},{2,0},{4,6},{6,4},{8,10},{10,8},{12,14},{14,12},{16,18},{18,... | collective-permute-start | bytes 1572872 | tf_op jit(solution)/shard_map/ppermute | solution.py:60
  104.8 2.6 %copy-start.15 = (bf16[2,192,1024]{2,1,0:T(8,128)(2,1)S(1)}, bf16[2,192,1024]{2,1,0:T(8,128)(2,1)}, u32[]{:S(2)}) copy-start(bf16[2,192,1024]{2,1,0:T(8,128)(2,1)} %get-tuple-element.87) | copy-start | bytes 2359300
  107.0 20.8 %collective-permute-start.17 = (bf16[128,1024]{1,0:T(8,128)(2,1)}, bf16[128,1024]{1,0:T(8,128)(2,1)S(1)}, u32[]{:S(2)}, u32[]{:S(2)}) collective-permute-start(bf16[128,1024]{1,0:T(8,128)(2,1)} %get-tuple-element.97), channel_id=1, source_target_pairs={{0,16},{2,18},{4,20},{6,22},{8,24},{10,26},{12,28},{14,30},{16,0},... | collective-permute-start | bytes 786440 | tf_op jit(solution)/shard_map/ppermute | solution.py:60
  107.7 10.9 %collective-permute-start.14 = (bf16[2,32,1024]{2,1,0:T(8,128)(2,1)S(1)}, bf16[2,32,1024]{2,1,0:T(8,128)(2,1)S(1)}, u32[]{:S(2)}, u32[]{:S(2)}) collective-permute-start(bf16[2,32,1024]{2,1,0:T(8,128)(2,1)S(1)} %slice.58), channel_id=1, source_target_pairs={{0,8},{2,10},{4,12},{6,14},{8,0},{10,2},{12,4},{14,6},{16,24},{18,... | collective-permute-start | bytes 393224 | tf_op jit(solution)/shard_map/ppermute | solution.py:60
  108.1 12.2 %copy-start.18 = (bf16[128,1024]{1,0:T(8,128)(2,1)S(1)}, bf16[128,1024]{1,0:T(8,128)(2,1)}, u32[]{:S(2)}) copy-start(bf16[128,1024]{1,0:T(8,128)(2,1)} %get-tuple-element.91) | copy-start | bytes 786436
  108.1 21.2 %copy-start.17 = (bf16[128,1024]{1,0:T(8,128)(2,1)S(1)}, bf16[128,1024]{1,0:T(8,128)(2,1)}, u32[]{:S(2)}) copy-start(bf16[128,1024]{1,0:T(8,128)(2,1)} %get-tuple-element.96) | copy-start | bytes 786436
  114.0 28.0 %copy-start.10 = (f32[8,8,1024]{2,1,0:T(8,128)S(1)}, f32[8,8,1024]{2,1,0:T(8,128)}, u32[]{:S(2)}) copy-start(f32[8,8,1024]{2,1,0:T(8,128)} %get-tuple-element.103.inner_ref) | copy-start | bytes 786436
  118.6 23.4 %copy-start.6 = (f32[8,8,1024]{2,1,0:T(8,128)S(1)}, f32[8,8,1024]{2,1,0:T(8,128)}, u32[]{:S(2)}) copy-start(f32[8,8,1024]{2,1,0:T(8,128)} %get-tuple-element.78.lse_ref) | copy-start | bytes 786436
  118.6 23.4 %copy-start.3 = (bf16[1024,1024]{1,0:T(8,128)(2,1)S(1)}, bf16[1024,1024]{1,0:T(8,128)(2,1)}, u32[]{:S(2)}) copy-start(bf16[1024,1024]{1,0:T(8,128)(2,1)} %key_ref.7) | copy-start | bytes 6291460
  118.7 23.3 %copy-start.2 = (bf16[1024,1024]{1,0:T(8,128)(2,1)S(1)}, bf16[1024,1024]{1,0:T(8,128)(2,1)}, u32[]{:S(2)}) copy-start(bf16[1024,1024]{1,0:T(8,128)(2,1)} %query_ref.9) | copy-start | bytes 6291460
  118.7 7.9 %collective-permute-start.16 = (bf16[2,48,1024]{2,1,0:T(8,128)(2,1)S(1)}, bf16[2,48,1024]{2,1,0:T(8,128)(2,1)S(1)}, u32[]{:S(2)}, u32[]{:S(2)}) collective-permute-start(bf16[2,48,1024]{2,1,0:T(8,128)(2,1)S(1)} %pad_maximum_fusion.1), channel_id=1, source_target_pairs={{0,4},{2,6},{4,0},{6,2},{8,12},{10,14},{12,8},{14,10},{16,20},{18,... | collective-permute-start | bytes 589832 | tf_op jit(solution)/shard_map/ppermute | solution.py:60
  120.4 17.3 %collective-permute-start.22 = (bf16[128,1024]{1,0:T(8,128)(2,1)S(1)}, bf16[128,1024]{1,0:T(8,128)(2,1)S(1)}, u32[]{:S(2)}, u32[]{:S(2)}) collective-permute-start(bf16[128,1024]{1,0:T(8,128)(2,1)S(1)} %add_convert_fusion.4), channel_id=1, source_target_pairs={{0,16},{2,18},{4,20},{6,22},{8,24},{10,26},{12,28},{14,30},{16,0},... | collective-permute-start | bytes 786440 | tf_op jit(solution)/shard_map/ppermute | solution.py:60
  121.8 10.4 %collective-permute-start.19 = (bf16[2,64,1024]{2,1,0:T(8,128)(2,1)S(1)}, bf16[2,64,1024]{2,1,0:T(8,128)(2,1)S(1)}, u32[]{:S(2)}, u32[]{:S(2)}) collective-permute-start(bf16[2,64,1024]{2,1,0:T(8,128)(2,1)S(1)} %get-tuple-element.99), channel_id=1, source_target_pairs={{0,4},{2,6},{4,0},{6,2},{8,12},{10,14},{12,8},{14,10},{16,20},{18,... | collective-permute-start | bytes 786440 | tf_op jit(solution)/shard_map/ppermute | solution.py:60
  126.6 10.9 %collective-permute-start.21 = (bf16[2,16,1024]{2,1,0:T(8,128)(2,1)S(1)}, bf16[2,16,1024]{2,1,0:T(8,128)(2,1)S(1)}, u32[]{:S(2)}, u32[]{:S(2)}) collective-permute-start(bf16[2,16,1024]{2,1,0:T(8,128)(2,1)S(1)} %add_convert_fusion.7), channel_id=1, source_target_pairs={{0,16},{2,18},{4,20},{6,22},{8,24},{10,26},{12,28},{14,30},{16,0},... | collective-permute-start | bytes 196616 | tf_op jit(solution)/shard_map/ppermute | solution.py:60
  127.8 9.9 %collective-permute-start.20 = (bf16[2,32,1024]{2,1,0:T(8,128)(2,1)S(1)}, bf16[2,32,1024]{2,1,0:T(8,128)(2,1)S(1)}, u32[]{:S(2)}, u32[]{:S(2)}) collective-permute-start(bf16[2,32,1024]{2,1,0:T(8,128)(2,1)S(1)} %add_convert_fusion.5), channel_id=1, source_target_pairs={{0,8},{2,10},{4,12},{6,14},{8,0},{10,2},{12,4},{14,6},{16,24},{18,... | collective-permute-start | bytes 393224 | tf_op jit(solution)/shard_map/ppermute | solution.py:60
  129.4 8.5 %collective-permute-start.23 = (bf16[128,1024]{1,0:T(8,128)(2,1)S(1)}, bf16[128,1024]{1,0:T(8,128)(2,1)S(1)}, u32[]{:S(2)}, u32[]{:S(2)}) collective-permute-start(bf16[128,1024]{1,0:T(8,128)(2,1)S(1)} %add_convert_fusion.3), channel_id=1, source_target_pairs={{0,4},{2,6},{4,0},{6,2},{8,12},{10,14},{12,8},{14,10},{16,20},{18,... | collective-permute-start | bytes 786440 | tf_op jit(solution)/shard_map/ppermute | solution.py:60
  137.8 16.2 %collective-permute-start.27 = (bf16[128,1024]{1,0:T(8,128)(2,1)S(1)}, bf16[128,1024]{1,0:T(8,128)(2,1)S(1)}, u32[]{:S(2)}, u32[]{:S(2)}) collective-permute-start(bf16[128,1024]{1,0:T(8,128)(2,1)S(1)} %add_convert_fusion.2), channel_id=1, source_target_pairs={{0,8},{2,10},{4,12},{6,14},{8,0},{10,2},{12,4},{14,6},{16,24},{18,... | collective-permute-start | bytes 786440 | tf_op jit(solution)/shard_map/ppermute | solution.py:60
  138.0 17.1 %collective-permute-start.24 = (bf16[128,1024]{1,0:T(8,128)(2,1)S(1)}, bf16[128,1024]{1,0:T(8,128)(2,1)S(1)}, u32[]{:S(2)}, u32[]{:S(2)}) collective-permute-start(bf16[128,1024]{1,0:T(8,128)(2,1)S(1)} %add_convert_fusion.1), channel_id=1, source_target_pairs={{0,16},{2,18},{4,20},{6,22},{8,24},{10,26},{12,28},{14,30},{16,0},... | collective-permute-start | bytes 786440 | tf_op jit(solution)/shard_map/ppermute | solution.py:60
  154.1 13.4 %collective-permute-start.28 = (bf16[256,1024]{1,0:T(8,128)(2,1)S(1)}, bf16[256,1024]{1,0:T(8,128)(2,1)S(1)}, u32[]{:S(2)}, u32[]{:S(2)}) collective-permute-start(bf16[256,1024]{1,0:T(8,128)(2,1)S(1)} %constant_dynamic-update-slice_fusion.9), channel_id=1, source_target_pairs={{0,4},{2,6},{4,0},{6,2},{8,12},{10,14},{12,8},{14,10},{16,20},{18,... | collective-permute-start | bytes 1572872 | tf_op jit(solution)/shard_map/ppermute | solution.py:60
  155.1 12.5 %collective-permute-start.25 = (bf16[256,1024]{1,0:T(8,128)(2,1)S(1)}, bf16[256,1024]{1,0:T(8,128)(2,1)S(1)}, u32[]{:S(2)}, u32[]{:S(2)}) collective-permute-start(bf16[256,1024]{1,0:T(8,128)(2,1)S(1)} %constant_dynamic-update-slice_fusion.5), channel_id=1, source_target_pairs={{0,8},{2,10},{4,12},{6,14},{8,0},{10,2},{12,4},{14,6},{16,24},{18,... | collective-permute-start | bytes 1572872 | tf_op jit(solution)/shard_map/ppermute | solution.py:60
  167.5 2.9 %collective-permute-start.29 = (bf16[512,1024]{1,0:T(8,128)(2,1)S(1)}, bf16[512,1024]{1,0:T(8,128)(2,1)S(1)}, u32[]{:S(2)}, u32[]{:S(2)}) collective-permute-start(bf16[512,1024]{1,0:T(8,128)(2,1)S(1)} %constant_dynamic-update-slice_fusion.11.first_ref), channel_id=1, source_target_pairs={{0,2},{2,0},{4,6},{6,4},{8,10},{10,8},{12,14},{14,12},{16,18},{18,... | collective-permute-start | bytes 3145736 | tf_op jit(solution)/shard_map/ppermute | solution.py:60
  167.6 4.7 %collective-permute-start.26 = (bf16[512,1024]{1,0:T(8,128)(2,1)S(1)}, bf16[512,1024]{1,0:T(8,128)(2,1)}, u32[]{:S(2)}, u32[]{:S(2)}) collective-permute-start(bf16[512,1024]{1,0:T(8,128)(2,1)S(1)} %constant_dynamic-update-slice_fusion.7.first_ref), channel_id=1, source_target_pairs={{0,2},{2,0},{4,6},{6,4},{8,10},{10,8},{12,14},{14,12},{16,18},{18,... | collective-permute-start | bytes 3145736 | tf_op jit(solution)/shard_map/ppermute | solution.py:60
  (3 other events, 2.3 us)

commit v4 on v3

--- a/solution.py
+++ b/solution.py
@@ -654,7 +654,7 @@
     first_sum.advance(inner)
     second_sum.advance(inner)
     arrivals = (shared,) if groups == 2 else ()
-    far_sum.advance(first_sum.kept, second_sum.kept, *arrivals)
+    far_sum.advance(first_sum.kept, *arrivals)
     if groups == 2:
         attended = project(tie(mixed, far_sum.kept), out_weight, group[None], shared)
     far_sum.advance(*([attended] if groups == 2 else []))

time: 176 us -> 175 us (level)
    ppermute x28, waiting for transfers between devices: 29.9 us -> 27.6 us  [from_partner(): lax.ppermute(block, 'seq', [(low, low ^ 1 << bit) for low in range(count)])]
where the time goes in v4:
time: 175 us
  Pallas kernels  107 us (61%)
  waiting for transfers between devices  29.3 us (17%)
  starting transfers between devices  28.2 us (16%)
  local copies, waits for them, and re-layouts  8.45 us (5%)
    pallas_call x11, Pallas kernels, index_call(): pl.pallas_call(kernel, grid_spec=pltpu.PrefetchScalarGridSpec(num_scalar_...  45 us
    ppermute x28, waiting for transfers between devices, from_partner(): lax.ppermute(block, 'seq', [(low, low ^ 1 << bit) for low in range(count)])  27.6 us
    ppermute x28, starting transfers between devices, from_partner(): lax.ppermute(block, 'seq', [(low, low ^ 1 << bit) for low in range(count)])  26.2 us
    pallas_call x2, Pallas kernels, near_backward(): pl.pallas_call(functools.partial(near_back_kernel, local, len(pooled)), g...  24.2 us
    pallas_call x1, Pallas kernels, far_backward(): pl.pallas_call(functools.partial(far_back_kernel, len(far)), grid=(featur...  13.3 us
    pallas_call x1, Pallas kernels, far_forward(): pl.pallas_call(functools.partial(far_kernel, len(far)), grid=(features //...  10.5 us
    unnamed x50, local copies, waits for them, and re-layouts  8.24 us
    pallas_call x1, Pallas kernels, near_forward(): pl.pallas_call(functools.partial(near_kernel, local), grid=(features // w...  7.82 us
  transfers between devices with their start and end apart: 30, of which 9 were waited for; matrix products, arithmetic and copies ran while one was open for 1% of the time, Pallas kernels for 56%

profile of v4, /device:TPU:0, one launch (start us, length us, event | category | flops | bytes accessed | tf_op | source)
XLA Modules:
  0.0 174.7 jit_solution(18347113048614268512)
XLA Ops:
  0.6 6.0 %pool.1 = (bf16[2,768,1024]{2,1,0:T(8,128)(2,1)}, bf16[2,128,1024]{2,1,0:T(8,128)(2,1)}, bf16[2,64,1024]{2,1,0:T(8,128)(2,1)}, bf16[2,32,1024]{2,1,0:T(8,128)(2,1)}, bf16[2,16,1024]{2,1,0:T(8,128)(2,1)}) custom-call(bf16[1024,1024]{1,0:T(8,128)(2,1)} %key_ref.7, bf16[1024,1024]{1,0:T(8,128)(2,1)} %value_ref.7), custom_call_target="tpu_custom_call" | custom-call | flops 287500000 | bytes 900000 | tf_op jit(solution)/shard_map/pool/pallas_call | solution.py:118
  6.6 3.0 %collective-permute-start.1 = (bf16[2,64,1024]{2,1,0:T(8,128)(2,1)}, bf16[2,64,1024]{2,1,0:T(8,128)(2,1)S(1)}, u32[]{:S(2)}, u32[]{:S(2)}) collective-permute-start(bf16[2,64,1024]{2,1,0:T(8,128)(2,1)} %get-tuple-element.61), channel_id=1, source_target_pairs={{0,4},{2,6},{4,0},{6,2},{8,12},{10,14},{12,8},{14,10},{16,20},{18,... | collective-permute-start | bytes 786440 | tf_op jit(solution)/shard_map/ppermute | solution.py:60
  9.6 1.6 collective-permute-start.2
  11.2 2.6 %collective-permute-start.3 = (bf16[2,16,1024]{2,1,0:T(8,128)(2,1)}, bf16[2,16,1024]{2,1,0:T(8,128)(2,1)S(1)}, u32[]{:S(2)}, u32[]{:S(2)}) collective-permute-start(bf16[2,16,1024]{2,1,0:T(8,128)(2,1)} %get-tuple-element.63), channel_id=1, source_target_pairs={{0,16},{2,18},{4,20},{6,22},{8,24},{10,26},{12,28},{14,30},{16,0},... | collective-permute-start | bytes 196616 | tf_op jit(solution)/shard_map/ppermute | solution.py:60
  13.8 1.5 collective-permute-start.8
  15.3 7.8 %near_forward.1 = (bf16[1024,1024]{1,0:T(8,128)(2,1)S(1)}, f32[8,8,1024]{2,1,0:T(8,128)S(1)}) custom-call(bf16[1024,1024]{1,0:T(8,128)(2,1)S(1)} %copy-done.1, bf16[1024,1024]{1,0:T(8,128)(2,1)} %key_ref.7, bf16[1024,1024]{1,0:T(8,128)(2,1)} %value_ref.7, bf16[2,768,1024]{2,1,0:T(8,128)(2,1)} %get-tuple-element.64.coarse_ref), custom_call_target="tpu_custom_call" | custom-call | flops 517500000 | bytes 1620000 | tf_op jit(solution)/shard_map/near_forward/pallas_call | solution.py:202
  23.1 1.3 copy-done.7
  24.5 0.7 copy-done.11
  25.2 0.6 collective-permute-start.4
  25.8 5.1 %collective-permute-done.4 = bf16[2,48,1024]{2,1,0:T(8,128)(2,1)S(1)} collective-permute-done((bf16[2,48,1024]{2,1,0:T(8,128)(2,1)S(1)}, bf16[2,48,1024]{2,1,0:T(8,128)(2,1)S(1)}, u32[]{:S(2)}, u32[]{:S(2)}) %collective-permute-start.4) | collective-permute-done | bytes 196640 | tf_op jit(solution)/shard_map/ppermute | solution.py:60
  31.5 4.5 %collective-permute-done.5 = bf16[2,32,1024]{2,1,0:T(8,128)(2,1)S(1)} collective-permute-done((bf16[2,32,1024]{2,1,0:T(8,128)(2,1)S(1)}, bf16[2,32,1024]{2,1,0:T(8,128)(2,1)S(1)}, u32[]{:S(2)}, u32[]{:S(2)}) %collective-permute-start.5) | collective-permute-done | bytes 131104 | tf_op jit(solution)/shard_map/ppermute | solution.py:60
  36.6 2.5 %collective-permute-done.refs_0_ = bf16[2,128,1024]{2,1,0:T(8,128)(2,1)S(1)} collective-permute-done((bf16[2,128,1024]{2,1,0:T(8,128)(2,1)S(1)}, bf16[2,128,1024]{2,1,0:T(8,128)(2,1)S(1)}, u32[]{:S(2)}, u32[]{:S(2)}) %collective-permute-start) | collective-permute-done | bytes 524320 | tf_op jit(solution)/shard_map/ppermute | solution.py:60
  39.2 0.8 copy-done.14
  40.2 10.5 %far_forward.1 = (bf16[1024,1024]{1,0:T(8,128)(2,1)}, f32[8,8,1024]{2,1,0:T(8,128)}) custom-call(bf16[1024,1024]{1,0:T(8,128)(2,1)} %query_ref.9, bf16[2,128,1024]{2,1,0:T(8,128)(2,1)} %copy-done.14, bf16[2,192,1024]{2,1,0:T(8,128)(2,1)} %copy-done.12, bf16[2,192,1024]{2,1,0:T(8,128)(2,1)} %copy-done.13, bf16[1024,1024]{1,0:T(8,128)(2,1)} %copy-done.7, ...), custom_call_target="tpu_custom_call" | custom-call | flops 575000000 | bytes 1800000 | tf_op jit(solution)/shard_map/far_forward/pallas_call | solution.py:221
  50.8 5.6 %project.2 = bf16[1024,1024]{1,0:T(8,128)(2,1)} custom-call(s32[1]{0:T(128)} %bitcast.3.which_ref, bf16[1024,1024]{1,0:T(8,128)(2,1)} %get-tuple-element.86.mixed_ref, bf16[1024,2048]{1,0:T(8,128)(2,1)} %weight_ref.3), custom_call_target="tpu_custom_call" | custom-call | flops 287500000 | bytes 900000 | tf_op jit(solution)/shard_map/project/pallas_call | solution.py:392
  56.9 6.0 %weight_halves.2 = (bf16[512,1024]{1,0:T(8,128)(2,1)S(1)}, bf16[512,1024]{1,0:T(8,128)(2,1)}) custom-call(s32[1]{0:T(128)} %bitcast.2.which_ref, bf16[1024,1024]{1,0:T(8,128)(2,1)S(1)} %copy-done, bf16[1024,1024]{1,0:T(8,128)(2,1)} %own_ref), custom_call_target="tpu_custom_call" | custom-call | flops 230000000 | bytes 720000 | tf_op jit(solution)/shard_map/weight_halves/pallas_call | solution.py:392
  62.9 1.0 copy-done.9
  63.9 5.2 %weight_halves.3 = (bf16[512,1024]{1,0:T(8,128)(2,1)S(1)}, bf16[512,1024]{1,0:T(8,128)(2,1)S(1)}) custom-call(s32[1]{0:T(128)} %bitcast.2.which_ref, bf16[1024,1024]{1,0:T(8,128)(2,1)S(1)} %copy-done, bf16[1024,1024]{1,0:T(8,128)(2,1)} %collective-permute-done.8.grad_ref.other_ref), custom_call_target="tpu_custom_call" | custom-call | flops 230000000 | bytes 720000 | tf_op jit(solution)/shard_map/weight_halves/pallas_call | solution.py:392
  69.2 1.0 copy-done.8
  70.6 2.9 %add_halves.4 = (bf16[256,1024]{1,0:T(8,128)(2,1)}, bf16[256,1024]{1,0:T(8,128)(2,1)}) custom-call(s32[1]{0:T(128)} %bitcast.1.which_ref, bf16[512,1024]{1,0:T(8,128)(2,1)} %copy-done.9, bf16[512,1024]{1,0:T(8,128)(2,1)} %collective-permute-done.7.second_ref), custom_call_target="tpu_custom_call" | custom-call | flops 28750000 | bytes 90000 | tf_op jit(solution)/shard_map/add_halves/pallas_call | solution.py:392
  74.1 2.7 %add_halves.5 = (bf16[256,1024]{1,0:T(8,128)(2,1)}, bf16[256,1024]{1,0:T(8,128)(2,1)}) custom-call(s32[1]{0:T(128)} %bitcast.4.which_ref, bf16[512,1024]{1,0:T(8,128)(2,1)} %copy-done.8, bf16[512,1024]{1,0:T(8,128)(2,1)} %collective-permute-done.9.second_ref), custom_call_target="tpu_custom_call" | custom-call | flops 28750000 | bytes 90000 | tf_op jit(solution)/shard_map/add_halves/pallas_call | solution.py:392
  77.3 7.2 %mix_back.1.grad_ref = bf16[1024,1024]{1,0:T(8,128)(2,1)S(1)} custom-call(s32[1]{0:T(128)} %bitcast.which_ref, bf16[1024,1024]{1,0:T(8,128)(2,1)S(1)} %copy-done.5, bf16[1024,1024]{1,0:T(8,128)(2,1)} %collective-permute-done.8.grad_ref.other_ref, bf16[1024,2048]{1,0:T(8,128)(2,1)} %weight_ref.3, bf16[1024,2048]{1,0:T(8,128)(2,1)} %weight_ref.3), custom_call_target="tpu_custom_call" | custom-call | flops 460000000 | bytes 1440000 | tf_op jit(solution)/shard_map/mix_back/pallas_call | solution.py:392
  84.4 1.4 copy-done.4
  85.8 13.3 %far_backward.1 = (bf16[2,128,1024]{2,1,0:T(8,128)(2,1)}, bf16[2,192,1024]{2,1,0:T(8,128)(2,1)}, bf16[2,192,1024]{2,1,0:T(8,128)(2,1)}, bf16[1024,1024]{1,0:T(8,128)(2,1)}, f32[8,8,1024]{2,1,0:T(8,128)}) custom-call(bf16[1024,1024]{1,0:T(8,128)(2,1)} %query_ref.9, bf16[1024,1024]{1,0:T(8,128)(2,1)} %get-tuple-element.86.mixed_ref, ...), custom_call_target="tpu_custom_call" | custom-call | flops 805000000 | bytes 2520000 | tf_op jit(solution)/shard_map/far_backward/pallas_call | solution.py:283
  99.2 0.8 copy-done.16
  100.0 2.1 %add_halves.6 = (bf16[128,1024]{1,0:T(8,128)(2,1)}, bf16[128,1024]{1,0:T(8,128)(2,1)}) custom-call(s32[1]{0:T(128)} %bitcast.4.which_ref, bf16[256,1024]{1,0:T(8,128)(2,1)} %get-tuple-element.81.first_ref, bf16[256,1024]{1,0:T(8,128)(2,1)} %copy-done.16), custom_call_target="tpu_custom_call" | custom-call | flops 14375000 | bytes 45000 | tf_op jit(solution)/shard_map/add_halves/pallas_call | solution.py:392
  102.1 1.6 collective-permute-start.14
  103.9 1.7 collective-permute-done.11.refs_0_
  105.6 0.8 copy-done.20
  106.4 2.2 %add_halves.7 = (bf16[128,1024]{1,0:T(8,128)(2,1)}, bf16[128,1024]{1,0:T(8,128)(2,1)}) custom-call(s32[1]{0:T(128)} %bitcast.5.which_ref, bf16[256,1024]{1,0:T(8,128)(2,1)} %get-tuple-element.90.first_ref, bf16[256,1024]{1,0:T(8,128)(2,1)} %copy-done.20), custom_call_target="tpu_custom_call" | custom-call | flops 2875000064 | bytes 9000000 | tf_op jit(solution)/shard_map/add_halves/pallas_call | solution.py:392
  109.9 5.9 %project.3 = bf16[1024,1024]{1,0:T(8,128)(2,1)} custom-call(s32[1]{0:T(128)} %bitcast.which_ref, bf16[1024,1024]{1,0:T(8,128)(2,1)} %get-tuple-element.86.mixed_ref, bf16[1024,2048]{1,0:T(8,128)(2,1)} %weight_ref.3, bf16[1024,1024]{1,0:T(8,128)(2,1)} %collective-permute-done.11.refs_0_), custom_call_target="tpu_custom_call" | custom-call | flops 287500000 | bytes 900000 | tf_op jit(solution)/shard_map/project/pallas_call | solution.py:392
  115.8 2.8 %collective-permute-done.13 = bf16[2,32,1024]{2,1,0:T(8,128)(2,1)S(1)} collective-permute-done((bf16[2,32,1024]{2,1,0:T(8,128)(2,1)S(1)}, bf16[2,32,1024]{2,1,0:T(8,128)(2,1)S(1)}, u32[]{:S(2)}, u32[]{:S(2)}) %collective-permute-start.13) | collective-permute-done | bytes 131104 | tf_op jit(solution)/shard_map/ppermute | solution.py:60
  118.7 1.6 collective-permute-start.16
  120.4 1.3 collective-permute-start.22
  121.7 0.8 collective-permute-start.19
  122.5 4.1 %collective-permute-done.16 = bf16[2,48,1024]{2,1,0:T(8,128)(2,1)S(1)} collective-permute-done((bf16[2,48,1024]{2,1,0:T(8,128)(2,1)S(1)}, bf16[2,48,1024]{2,1,0:T(8,128)(2,1)S(1)}, u32[]{:S(2)}, u32[]{:S(2)}) %collective-permute-start.16) | collective-permute-done | bytes 196640 | tf_op jit(solution)/shard_map/ppermute | solution.py:60
  127.0 2.3 %collective-permute-start.20 = (bf16[2,32,1024]{2,1,0:T(8,128)(2,1)S(1)}, bf16[2,32,1024]{2,1,0:T(8,128)(2,1)S(1)}, u32[]{:S(2)}, u32[]{:S(2)}) collective-permute-start(bf16[2,32,1024]{2,1,0:T(8,128)(2,1)S(1)} %add_convert_fusion.5), channel_id=1, source_target_pairs={{0,8},{2,10},{4,12},{6,14},{8,0},{10,2},{12,4},{14,6},{16,24},{18,... | collective-permute-start | bytes 393224 | tf_op jit(solution)/shard_map/ppermute | solution.py:60
  129.4 1.6 collective-permute-start.23
  131.0 1.2 collective-permute-done.19.refs_1_
  132.2 5.2 %collective-permute-done.21.refs_3_ = bf16[2,16,1024]{2,1,0:T(8,128)(2,1)S(1)} collective-permute-done((bf16[2,16,1024]{2,1,0:T(8,128)(2,1)S(1)}, bf16[2,16,1024]{2,1,0:T(8,128)(2,1)S(1)}, u32[]{:S(2)}, u32[]{:S(2)}) %collective-permute-start.21) | collective-permute-done | bytes 65568 | tf_op jit(solution)/shard_map/ppermute | solution.py:60
  137.6 3.9 %collective-permute-start.24 = (bf16[128,1024]{1,0:T(8,128)(2,1)S(1)}, bf16[128,1024]{1,0:T(8,128)(2,1)S(1)}, u32[]{:S(2)}, u32[]{:S(2)}) collective-permute-start(bf16[128,1024]{1,0:T(8,128)(2,1)S(1)} %add_convert_fusion.1), channel_id=1, source_target_pairs={{0,16},{2,18},{4,20},{6,22},{8,24},{10,26},{12,28},{14,30},{16,0},... | collective-permute-start | bytes 786440 | tf_op jit(solution)/shard_map/ppermute | solution.py:60
  141.5 12.0 %near_backward.2 = (bf16[1024,1024]{1,0:T(8,128)(2,1)}, bf16[1024,1024]{1,0:T(8,128)(2,1)}, bf16[1024,1024]{1,0:T(8,128)(2,1)}) custom-call(bf16[1024,1024]{1,0:T(8,128)(2,1)S(1)} %copy-done.2, bf16[1024,1024]{1,0:T(8,128)(2,1)S(1)} %copy-done.3, bf16[1024,1024]{1,0:T(8,128)(2,1)} %value_ref.7, bf16[2,768,1024]{2,1,0:T(8,128)(2,1)} %get-tuple-element.64.coarse_ref, ...), custom_call_target="tpu_custom_call" | custom-call | flops 517500000 | bytes 1620000 | tf_op jit(solution)/shard_map/near_backward/pallas_call | solution.py:373
  153.6 0.6 collective-permute-start.28
  154.3 12.2 %near_backward.3 = (bf16[1024,1024]{1,0:T(8,128)(2,1)}, bf16[1024,1024]{1,0:T(8,128)(2,1)}, bf16[1024,1024]{1,0:T(8,128)(2,1)}) custom-call(bf16[1024,1024]{1,0:T(8,128)(2,1)S(1)} %copy-done.2, bf16[1024,1024]{1,0:T(8,128)(2,1)S(1)} %copy-done.3, bf16[1024,1024]{1,0:T(8,128)(2,1)} %value_ref.7, ...), custom_call_target="tpu_custom_call", output_to_operand_aliasing={{0}: (12, {}), {1}: (13, {}), {2}: (14, {})} | custom-call | flops 517500000 | bytes 1620000 | tf_op jit(solution)/shard_map/near_backward/pallas_call | solution.py:373
  166.8 0.5 collective-permute-start.26
  167.5 2.1 %collective-permute-done.29.second_ref = bf16[512,1024]{1,0:T(8,128)(2,1)S(1)} collective-permute-done((bf16[512,1024]{1,0:T(8,128)(2,1)S(1)}, bf16[512,1024]{1,0:T(8,128)(2,1)S(1)}, u32[]{:S(2)}, u32[]{:S(2)}) %collective-permute-start.29) | collective-permute-done | bytes 1048608 | tf_op jit(solution)/shard_map/ppermute | solution.py:60
  169.6 2.0 %place.2.refs_0_ = bf16[1024,2048]{1,0:T(8,128)(2,1)} custom-call(s32[3]{0:T(128)S(1)} %pad_add_fusion.1.where_ref, bf16[512,1024]{1,0:T(8,128)(2,1)S(1)} %constant_dynamic-update-slice_fusion.11.first_ref, bf16[512,1024]{1,0:T(8,128)(2,1)S(1)} %collective-permute-done.29.second_ref), custom_call_target="tpu_custom_call" | custom-call | flops 57500000 | bytes 180000 | tf_op jit(solution)/shard_map/place/pallas_call | solution.py:392
  171.5 3.2 %place.3 = bf16[1024,2048]{1,0:T(8,128)(2,1)} custom-call(s32[3]{0:T(128)S(1)} %pad_add_fusion.where_ref, bf16[512,1024]{1,0:T(8,128)(2,1)S(1)} %constant_dynamic-update-slice_fusion.7.first_ref, bf16[512,1024]{1,0:T(8,128)(2,1)} %collective-permute-done.26.second_ref, bf16[1024,2048]{1,0:T(8,128)(2,1)} %place.2.refs_0_), custom_call_target="tpu_custom_call", output_to_operand_aliasing={{}: (3, {})} | custom-call | flops 57500000 | bytes 180000 | tf_op jit(solution)/shard_map/place/pallas_call | solution.py:392
  (102 shorter events, 6.4 us)
Async XLA Ops:
  0.6 14.7 %copy-start.1 = (bf16[1024,1024]{1,0:T(8,128)(2,1)S(1)}, bf16[1024,1024]{1,0:T(8,128)(2,1)}, u32[]{:S(2)}) copy-start(bf16[1024,1024]{1,0:T(8,128)(2,1)} %query_ref.9) | copy-start | bytes 6291460
  6.6 19.1 %collective-permute-start.1 = (bf16[2,64,1024]{2,1,0:T(8,128)(2,1)}, bf16[2,64,1024]{2,1,0:T(8,128)(2,1)S(1)}, u32[]{:S(2)}, u32[]{:S(2)}) collective-permute-start(bf16[2,64,1024]{2,1,0:T(8,128)(2,1)} %get-tuple-element.61), channel_id=1, source_target_pairs={{0,4},{2,6},{4,0},{6,2},{8,12},{10,14},{12,8},{14,10},{16,20},{18,... | collective-permute-start | bytes 786440 | tf_op jit(solution)/shard_map/ppermute | solution.py:60
  9.6 15.5 %collective-permute-start.2 = (bf16[2,32,1024]{2,1,0:T(8,128)(2,1)}, bf16[2,32,1024]{2,1,0:T(8,128)(2,1)S(1)}, u32[]{:S(2)}, u32[]{:S(2)}) collective-permute-start(bf16[2,32,1024]{2,1,0:T(8,128)(2,1)} %get-tuple-element.62), channel_id=1, source_target_pairs={{0,8},{2,10},{4,12},{6,14},{8,0},{10,2},{12,4},{14,6},{16,24},{18,... | collective-permute-start | bytes 393224 | tf_op jit(solution)/shard_map/ppermute | solution.py:60
  11.2 13.9 %collective-permute-start.3 = (bf16[2,16,1024]{2,1,0:T(8,128)(2,1)}, bf16[2,16,1024]{2,1,0:T(8,128)(2,1)S(1)}, u32[]{:S(2)}, u32[]{:S(2)}) collective-permute-start(bf16[2,16,1024]{2,1,0:T(8,128)(2,1)} %get-tuple-element.63), channel_id=1, source_target_pairs={{0,16},{2,18},{4,20},{6,22},{8,24},{10,26},{12,28},{14,30},{16,0},... | collective-permute-start | bytes 196616 | tf_op jit(solution)/shard_map/ppermute | solution.py:60
  13.8 50.1 %collective-permute-start.8 = (bf16[1024,1024]{1,0:T(8,128)(2,1)}, bf16[1024,1024]{1,0:T(8,128)(2,1)}, u32[]{:S(2)}, u32[]{:S(2)}) collective-permute-start(bf16[1024,1024]{1,0:T(8,128)(2,1)} %own_ref), channel_id=1, source_target_pairs={{0,1},{1,0},{2,3},{3,2},{4,5},{5,4},{6,7},{7,6},{8,9},{9,8},{10,11... | collective-permute-start | bytes 6291464 | tf_op jit(solution)/shard_map/ppermute | solution.py:624
  23.1 1.3 copy-start.7
  25.2 11.0 %copy-start.19 = (bf16[2,128,1024]{2,1,0:T(8,128)(2,1)S(1)}, bf16[2,128,1024]{2,1,0:T(8,128)(2,1)}, u32[]{:S(2)}) copy-start(bf16[2,128,1024]{2,1,0:T(8,128)(2,1)} %get-tuple-element.60) | copy-start | bytes 1572868
  25.2 5.7 %collective-permute-start.4 = (bf16[2,48,1024]{2,1,0:T(8,128)(2,1)S(1)}, bf16[2,48,1024]{2,1,0:T(8,128)(2,1)S(1)}, u32[]{:S(2)}, u32[]{:S(2)}) collective-permute-start(bf16[2,48,1024]{2,1,0:T(8,128)(2,1)S(1)} %pad_maximum_fusion), channel_id=1, source_target_pairs={{0,4},{2,6},{4,0},{6,2},{8,12},{10,14},{12,8},{14,10},{16,20},{18,... | collective-permute-start | bytes 589832 | tf_op jit(solution)/shard_map/ppermute | solution.py:60
  31.0 5.0 %collective-permute-start.5 = (bf16[2,32,1024]{2,1,0:T(8,128)(2,1)S(1)}, bf16[2,32,1024]{2,1,0:T(8,128)(2,1)S(1)}, u32[]{:S(2)}, u32[]{:S(2)}) collective-permute-start(bf16[2,32,1024]{2,1,0:T(8,128)(2,1)S(1)} %pad_maximum_fusion.2), channel_id=1, source_target_pairs={{0,8},{2,10},{4,12},{6,14},{8,0},{10,2},{12,4},{14,6},{16,24},{18,... | collective-permute-start | bytes 393224 | tf_op jit(solution)/shard_map/ppermute | solution.py:60
  36.0 3.1 %copy-start.12 = (bf16[2,192,1024]{2,1,0:T(8,128)(2,1)}, bf16[2,192,1024]{2,1,0:T(8,128)(2,1)S(1)}, u32[]{:S(2)}) copy-start(bf16[2,192,1024]{2,1,0:T(8,128)(2,1)S(1)} %constant_dynamic-update-slice_fusion.refs_1_) | copy-start | bytes 2359300
  36.0 3.1 %collective-permute-start.6 = (bf16[2,192,1024]{2,1,0:T(8,128)(2,1)S(1)}, bf16[2,192,1024]{2,1,0:T(8,128)(2,1)S(1)}, u32[]{:S(2)}, u32[]{:S(2)}) collective-permute-start(bf16[2,192,1024]{2,1,0:T(8,128)(2,1)S(1)} %constant_dynamic-update-slice_fusion.refs_1_), channel_id=1, source_target_pairs={{0,2},{2,0},{4,6},{6,4},{8,10},{10,8},{12,14},{14,12},{16,18},{18,... | collective-permute-start | bytes 2359304 | tf_op jit(solution)/shard_map/ppermute | solution.py:60
  36.1 3.0 %collective-permute-start = (bf16[2,128,1024]{2,1,0:T(8,128)(2,1)S(1)}, bf16[2,128,1024]{2,1,0:T(8,128)(2,1)S(1)}, u32[]{:S(2)}, u32[]{:S(2)}) collective-permute-start(bf16[2,128,1024]{2,1,0:T(8,128)(2,1)S(1)} %copy-done.19), channel_id=1, source_target_pairs={{0,2},{2,0},{4,6},{6,4},{8,10},{10,8},{12,14},{14,12},{16,18},{18,... | collective-permute-start | bytes 1572872 | tf_op jit(solution)/shard_map/ppermute | solution.py:60
  39.2 1.1 copy-start.13
  50.8 6.1 %copy-start = (bf16[1024,1024]{1,0:T(8,128)(2,1)S(1)}, bf16[1024,1024]{1,0:T(8,128)(2,1)}, u32[]{:S(2)}) copy-start(bf16[1024,1024]{1,0:T(8,128)(2,1)} %get-tuple-element.86.mixed_ref) | copy-start | bytes 6291460
  56.3 49.2 %collective-permute-start.11 = (bf16[1024,1024]{1,0:T(8,128)(2,1)}, bf16[1024,1024]{1,0:T(8,128)(2,1)}, u32[]{:S(2)}, u32[]{:S(2)}) collective-permute-start(bf16[1024,1024]{1,0:T(8,128)(2,1)} %project.2), channel_id=1, source_target_pairs={{0,1},{1,0},{2,3},{3,2},{4,5},{5,4},{6,7},{7,6},{8,9},{9,8},{10,11... | collective-permute-start | bytes 6291464 | tf_op jit(solution)/shard_map/ppermute | solution.py:633
  62.9 1.0 copy-start.9
  63.9 6.8 %collective-permute-start.7 = (bf16[512,1024]{1,0:T(8,128)(2,1)}, bf16[512,1024]{1,0:T(8,128)(2,1)}, u32[]{:S(2)}, u32[]{:S(2)}) collective-permute-start(bf16[512,1024]{1,0:T(8,128)(2,1)} %get-tuple-element.71), channel_id=1, source_target_pairs={{0,2},{2,0},{4,6},{6,4},{8,10},{10,8},{12,14},{14,12},{16,18},{18,... | collective-permute-start | bytes 3145736 | tf_op jit(solution)/shard_map/ppermute | solution.py:60
  69.1 1.0 copy-start.8
  70.1 4.0 %collective-permute-start.9 = (bf16[512,1024]{1,0:T(8,128)(2,1)S(1)}, bf16[512,1024]{1,0:T(8,128)(2,1)}, u32[]{:S(2)}, u32[]{:S(2)}) collective-permute-start(bf16[512,1024]{1,0:T(8,128)(2,1)S(1)} %get-tuple-element.75), channel_id=1, source_target_pairs={{0,2},{2,0},{4,6},{6,4},{8,10},{10,8},{12,14},{14,12},{16,18},{18,... | collective-permute-start | bytes 3145736 | tf_op jit(solution)/shard_map/ppermute | solution.py:60
  70.6 6.6 %copy-start.5 = (bf16[1024,1024]{1,0:T(8,128)(2,1)S(1)}, bf16[1024,1024]{1,0:T(8,128)(2,1)}, u32[]{:S(2)}) copy-start(bf16[1024,1024]{1,0:T(8,128)(2,1)} %own_ref) | copy-start | bytes 6291460
  73.6 25.6 %collective-permute-start.10 = (bf16[256,1024]{1,0:T(8,128)(2,1)}, bf16[256,1024]{1,0:T(8,128)(2,1)S(1)}, u32[]{:S(2)}, u32[]{:S(2)}) collective-permute-start(bf16[256,1024]{1,0:T(8,128)(2,1)} %get-tuple-element.82), channel_id=1, source_target_pairs={{0,4},{2,6},{4,0},{6,2},{8,12},{10,14},{12,8},{14,10},{16,20},{18,... | collective-permute-start | bytes 1572872 | tf_op jit(solution)/shard_map/ppermute | solution.py:60
  76.8 28.8 %collective-permute-start.15 = (bf16[256,1024]{1,0:T(8,128)(2,1)}, bf16[256,1024]{1,0:T(8,128)(2,1)S(1)}, u32[]{:S(2)}, u32[]{:S(2)}) collective-permute-start(bf16[256,1024]{1,0:T(8,128)(2,1)} %get-tuple-element.91), channel_id=1, source_target_pairs={{0,8},{2,10},{4,12},{6,14},{8,0},{10,2},{12,4},{14,6},{16,24},{18,... | collective-permute-start | bytes 1572872 | tf_op jit(solution)/shard_map/ppermute | solution.py:60
  84.4 1.4 copy-start.4
  99.1 9.9 %collective-permute-start.12 = (bf16[2,192,1024]{2,1,0:T(8,128)(2,1)}, bf16[2,192,1024]{2,1,0:T(8,128)(2,1)S(1)}, u32[]{:S(2)}, u32[]{:S(2)}) collective-permute-start(bf16[2,192,1024]{2,1,0:T(8,128)(2,1)} %get-tuple-element.85), channel_id=1, source_target_pairs={{0,2},{2,0},{4,6},{6,4},{8,10},{10,8},{12,14},{14,12},{16,18},{18,... | collective-permute-start | bytes 2359304 | tf_op jit(solution)/shard_map/ppermute | solution.py:60
  99.2 0.8 copy-start.16
  102.1 18.2 %collective-permute-start.14 = (bf16[128,1024]{1,0:T(8,128)(2,1)}, bf16[128,1024]{1,0:T(8,128)(2,1)S(1)}, u32[]{:S(2)}, u32[]{:S(2)}) collective-permute-start(bf16[128,1024]{1,0:T(8,128)(2,1)} %get-tuple-element.89), channel_id=1, source_target_pairs={{0,8},{2,10},{4,12},{6,14},{8,0},{10,2},{12,4},{14,6},{16,24},{18,... | collective-permute-start | bytes 786440 | tf_op jit(solution)/shard_map/ppermute | solution.py:60
  103.7 25.6 %collective-permute-start.18 = (bf16[2,128,1024]{2,1,0:T(8,128)(2,1)}, bf16[2,128,1024]{2,1,0:T(8,128)(2,1)S(1)}, u32[]{:S(2)}, u32[]{:S(2)}) collective-permute-start(bf16[2,128,1024]{2,1,0:T(8,128)(2,1)} %get-tuple-element.98), channel_id=1, source_target_pairs={{0,2},{2,0},{4,6},{6,4},{8,10},{10,8},{12,14},{14,12},{16,18},{18,... | collective-permute-start | bytes 1572872 | tf_op jit(solution)/shard_map/ppermute | solution.py:60
  106.4 2.6 %copy-start.15 = (bf16[2,192,1024]{2,1,0:T(8,128)(2,1)S(1)}, bf16[2,192,1024]{2,1,0:T(8,128)(2,1)}, u32[]{:S(2)}) copy-start(bf16[2,192,1024]{2,1,0:T(8,128)(2,1)} %get-tuple-element.84) | copy-start | bytes 2359300
  108.6 18.4 %collective-permute-start.17 = (bf16[128,1024]{1,0:T(8,128)(2,1)}, bf16[128,1024]{1,0:T(8,128)(2,1)S(1)}, u32[]{:S(2)}, u32[]{:S(2)}) collective-permute-start(bf16[128,1024]{1,0:T(8,128)(2,1)} %get-tuple-element.97), channel_id=1, source_target_pairs={{0,16},{2,18},{4,20},{6,22},{8,24},{10,26},{12,28},{14,30},{16,0},... | collective-permute-start | bytes 786440 | tf_op jit(solution)/shard_map/ppermute | solution.py:60
  109.3 9.3 %collective-permute-start.13 = (bf16[2,32,1024]{2,1,0:T(8,128)(2,1)S(1)}, bf16[2,32,1024]{2,1,0:T(8,128)(2,1)S(1)}, u32[]{:S(2)}, u32[]{:S(2)}) collective-permute-start(bf16[2,32,1024]{2,1,0:T(8,128)(2,1)S(1)} %slice.58), channel_id=1, source_target_pairs={{0,8},{2,10},{4,12},{6,14},{8,0},{10,2},{12,4},{14,6},{16,24},{18,... | collective-permute-start | bytes 393224 | tf_op jit(solution)/shard_map/ppermute | solution.py:60
  109.9 10.4 %copy-start.18 = (bf16[128,1024]{1,0:T(8,128)(2,1)S(1)}, bf16[128,1024]{1,0:T(8,128)(2,1)}, u32[]{:S(2)}) copy-start(bf16[128,1024]{1,0:T(8,128)(2,1)} %get-tuple-element.88) | copy-start | bytes 786436
  109.9 19.4 %copy-start.17 = (bf16[128,1024]{1,0:T(8,128)(2,1)S(1)}, bf16[128,1024]{1,0:T(8,128)(2,1)}, u32[]{:S(2)}) copy-start(bf16[128,1024]{1,0:T(8,128)(2,1)} %get-tuple-element.96) | copy-start | bytes 786436
  115.8 25.8 %copy-start.10 = (f32[8,8,1024]{2,1,0:T(8,128)S(1)}, f32[8,8,1024]{2,1,0:T(8,128)}, u32[]{:S(2)}) copy-start(f32[8,8,1024]{2,1,0:T(8,128)} %get-tuple-element.103.inner_ref) | copy-start | bytes 786436
  118.6 22.9 %copy-start.6 = (f32[8,8,1024]{2,1,0:T(8,128)S(1)}, f32[8,8,1024]{2,1,0:T(8,128)}, u32[]{:S(2)}) copy-start(f32[8,8,1024]{2,1,0:T(8,128)} %get-tuple-element.78.lse_ref) | copy-start | bytes 786436
  118.6 22.9 %copy-start.3 = (bf16[1024,1024]{1,0:T(8,128)(2,1)S(1)}, bf16[1024,1024]{1,0:T(8,128)(2,1)}, u32[]{:S(2)}) copy-start(bf16[1024,1024]{1,0:T(8,128)(2,1)} %key_ref.7) | copy-start | bytes 6291460
  118.7 22.9 %copy-start.2 = (bf16[1024,1024]{1,0:T(8,128)(2,1)S(1)}, bf16[1024,1024]{1,0:T(8,128)(2,1)}, u32[]{:S(2)}) copy-start(bf16[1024,1024]{1,0:T(8,128)(2,1)} %query_ref.9) | copy-start | bytes 6291460
  118.7 7.9 %collective-permute-start.16 = (bf16[2,48,1024]{2,1,0:T(8,128)(2,1)S(1)}, bf16[2,48,1024]{2,1,0:T(8,128)(2,1)S(1)}, u32[]{:S(2)}, u32[]{:S(2)}) collective-permute-start(bf16[2,48,1024]{2,1,0:T(8,128)(2,1)S(1)} %pad_maximum_fusion.1), channel_id=1, source_target_pairs={{0,4},{2,6},{4,0},{6,2},{8,12},{10,14},{12,8},{14,10},{16,20},{18,... | collective-permute-start | bytes 589832 | tf_op jit(solution)/shard_map/ppermute | solution.py:60
  120.4 17.0 %collective-permute-start.22 = (bf16[128,1024]{1,0:T(8,128)(2,1)S(1)}, bf16[128,1024]{1,0:T(8,128)(2,1)S(1)}, u32[]{:S(2)}, u32[]{:S(2)}) collective-permute-start(bf16[128,1024]{1,0:T(8,128)(2,1)S(1)} %add_convert_fusion.4), channel_id=1, source_target_pairs={{0,16},{2,18},{4,20},{6,22},{8,24},{10,26},{12,28},{14,30},{16,0},... | collective-permute-start | bytes 786440 | tf_op jit(solution)/shard_map/ppermute | solution.py:60
  121.7 10.5 %collective-permute-start.19 = (bf16[2,64,1024]{2,1,0:T(8,128)(2,1)S(1)}, bf16[2,64,1024]{2,1,0:T(8,128)(2,1)S(1)}, u32[]{:S(2)}, u32[]{:S(2)}) collective-permute-start(bf16[2,64,1024]{2,1,0:T(8,128)(2,1)S(1)} %get-tuple-element.99), channel_id=1, source_target_pairs={{0,4},{2,6},{4,0},{6,2},{8,12},{10,14},{12,8},{14,10},{16,20},{18,... | collective-permute-start | bytes 786440 | tf_op jit(solution)/shard_map/ppermute | solution.py:60
  126.6 10.8 %collective-permute-start.21 = (bf16[2,16,1024]{2,1,0:T(8,128)(2,1)S(1)}, bf16[2,16,1024]{2,1,0:T(8,128)(2,1)S(1)}, u32[]{:S(2)}, u32[]{:S(2)}) collective-permute-start(bf16[2,16,1024]{2,1,0:T(8,128)(2,1)S(1)} %add_convert_fusion.7), channel_id=1, source_target_pairs={{0,16},{2,18},{4,20},{6,22},{8,24},{10,26},{12,28},{14,30},{16,0},... | collective-permute-start | bytes 196616 | tf_op jit(solution)/shard_map/ppermute | solution.py:60
  127.0 10.4 %collective-permute-start.20 = (bf16[2,32,1024]{2,1,0:T(8,128)(2,1)S(1)}, bf16[2,32,1024]{2,1,0:T(8,128)(2,1)S(1)}, u32[]{:S(2)}, u32[]{:S(2)}) collective-permute-start(bf16[2,32,1024]{2,1,0:T(8,128)(2,1)S(1)} %add_convert_fusion.5), channel_id=1, source_target_pairs={{0,8},{2,10},{4,12},{6,14},{8,0},{10,2},{12,4},{14,6},{16,24},{18,... | collective-permute-start | bytes 393224 | tf_op jit(solution)/shard_map/ppermute | solution.py:60
  129.4 8.2 %collective-permute-start.23 = (bf16[128,1024]{1,0:T(8,128)(2,1)S(1)}, bf16[128,1024]{1,0:T(8,128)(2,1)S(1)}, u32[]{:S(2)}, u32[]{:S(2)}) collective-permute-start(bf16[128,1024]{1,0:T(8,128)(2,1)S(1)} %add_convert_fusion.3), channel_id=1, source_target_pairs={{0,4},{2,6},{4,0},{6,2},{8,12},{10,14},{12,8},{14,10},{16,20},{18,... | collective-permute-start | bytes 786440 | tf_op jit(solution)/shard_map/ppermute | solution.py:60
  137.5 16.1 %collective-permute-start.27 = (bf16[128,1024]{1,0:T(8,128)(2,1)S(1)}, bf16[128,1024]{1,0:T(8,128)(2,1)S(1)}, u32[]{:S(2)}, u32[]{:S(2)}) collective-permute-start(bf16[128,1024]{1,0:T(8,128)(2,1)S(1)} %add_convert_fusion.2), channel_id=1, source_target_pairs={{0,8},{2,10},{4,12},{6,14},{8,0},{10,2},{12,4},{14,6},{16,24},{18,... | collective-permute-start | bytes 786440 | tf_op jit(solution)/shard_map/ppermute | solution.py:60
  137.6 16.6 %collective-permute-start.24 = (bf16[128,1024]{1,0:T(8,128)(2,1)S(1)}, bf16[128,1024]{1,0:T(8,128)(2,1)S(1)}, u32[]{:S(2)}, u32[]{:S(2)}) collective-permute-start(bf16[128,1024]{1,0:T(8,128)(2,1)S(1)} %add_convert_fusion.1), channel_id=1, source_target_pairs={{0,16},{2,18},{4,20},{6,22},{8,24},{10,26},{12,28},{14,30},{16,0},... | collective-permute-start | bytes 786440 | tf_op jit(solution)/shard_map/ppermute | solution.py:60
  153.6 13.0 %collective-permute-start.28 = (bf16[256,1024]{1,0:T(8,128)(2,1)S(1)}, bf16[256,1024]{1,0:T(8,128)(2,1)S(1)}, u32[]{:S(2)}, u32[]{:S(2)}) collective-permute-start(bf16[256,1024]{1,0:T(8,128)(2,1)S(1)} %constant_dynamic-update-slice_fusion.9), channel_id=1, source_target_pairs={{0,4},{2,6},{4,0},{6,2},{8,12},{10,14},{12,8},{14,10},{16,20},{18,... | collective-permute-start | bytes 1572872 | tf_op jit(solution)/shard_map/ppermute | solution.py:60
  154.2 12.5 %collective-permute-start.25 = (bf16[256,1024]{1,0:T(8,128)(2,1)S(1)}, bf16[256,1024]{1,0:T(8,128)(2,1)S(1)}, u32[]{:S(2)}, u32[]{:S(2)}) collective-permute-start(bf16[256,1024]{1,0:T(8,128)(2,1)S(1)} %constant_dynamic-update-slice_fusion.5), channel_id=1, source_target_pairs={{0,8},{2,10},{4,12},{6,14},{8,0},{10,2},{12,4},{14,6},{16,24},{18,... | collective-permute-start | bytes 1572872 | tf_op jit(solution)/shard_map/ppermute | solution.py:60
  166.7 2.9 %collective-permute-start.29 = (bf16[512,1024]{1,0:T(8,128)(2,1)S(1)}, bf16[512,1024]{1,0:T(8,128)(2,1)S(1)}, u32[]{:S(2)}, u32[]{:S(2)}) collective-permute-start(bf16[512,1024]{1,0:T(8,128)(2,1)S(1)} %constant_dynamic-update-slice_fusion.11.first_ref), channel_id=1, source_target_pairs={{0,2},{2,0},{4,6},{6,4},{8,10},{10,8},{12,14},{14,12},{16,18},{18,... | collective-permute-start | bytes 3145736 | tf_op jit(solution)/shard_map/ppermute | solution.py:60
  166.8 4.7 %collective-permute-start.26 = (bf16[512,1024]{1,0:T(8,128)(2,1)S(1)}, bf16[512,1024]{1,0:T(8,128)(2,1)}, u32[]{:S(2)}, u32[]{:S(2)}) collective-permute-start(bf16[512,1024]{1,0:T(8,128)(2,1)S(1)} %constant_dynamic-update-slice_fusion.7.first_ref), channel_id=1, source_target_pairs={{0,2},{2,0},{4,6},{6,4},{8,10},{10,8},{12,14},{14,12},{16,18},{18,... | collective-permute-start | bytes 3145736 | tf_op jit(solution)/shard_map/ppermute | solution.py:60
  (3 other events, 2.3 us)
